TPU v7x, 512 devices: a whole 4x4x16 slice. The times are simulated.
512 devices in a mesh: group: 4 (over x), seq: 32 (over y_hi, z), tp: 4 (over y_lo, core).
Axes of the slice: x: 4, y: 4 (y_hi: 2, y_lo: 2; y = y_hi * 2 + y_lo), z: 16, core: 2. Of those that a mesh axis runs over, the one named last changes fastest.
Arguments:
- hidden: bfloat16 [32768, 5120], P(('group', 'seq')), may hold values from -6 to 6
- norm_gain: bfloat16 [5120], replicated, may hold values from 0.5 to 1.5
- gen_value: bfloat16 [5120, 2560], P('seq', 'tp'), may hold values from -0.078125 to 0.078125
- gen_head: bfloat16 [2560, 64], P('tp'), may hold values from -0.125 to 0.125
- critic_embed: bfloat16 [2, 64, 5120], replicated, may hold values from -0.75 to 0.75
- critic_gain: bfloat16 [2, 5120], replicated, may hold values from 0.5 to 1.5
- critic_value: bfloat16 [5120, 5120], P('seq', ('group', 'tp')), may hold values from -0.078125 to 0.078125
- critic_head: bfloat16 [5120, 64], P(('group', 'tp')), may hold values from -0.125 to 0.125
- noise: bfloat16 [32768, 64], P('seq'), may hold values from -6 to 6
- owner: int32 [32768], P(('group', 'seq')), may hold values from 0 to 32767, as said below
- tsteps: int32 [16], replicated, may hold values from 0 to 999
- noise_mix: float32 [2, 1000], replicated, may hold values from 0.3 to 1
- gap_weight: float32 [1000], replicated, may hold values from 2 to 16
Outputs:
- gen_latent: bfloat16 [32768, 64], P(('group', 'seq'))
- grad_hidden: bfloat16 [32768, 5120], P(('group', 'seq'), 'tp')
Inputs may be any that keep to these rules, and one draw needn't show every extreme that they name: owner is a permutation of the token positions. The 256 tokens of one generator block (aligned blocks of 256) place at most 15 tokens in one critic position block (aligned blocks of 1024 positions), and exactly 15 in some; every critic position block receives tokens from every generator block.
All inputs are finite; a program needn't handle non-finite values.
Results may differ from a plain program's by a relative error of at most 0.035.
Values may be sent and summed in bfloat16 or wider, within the bound.
No kernel may reach another device: no remote copies, remote signals or barrier semaphores. Data moves between devices by JAX's collectives and lax.ppermute only.
A program may use at most 128 MiB of HBM per device.

v0:
```python
import jax
import jax.numpy as jnp
from jax import lax
from jax.sharding import PartitionSpec as P

FTOK = 2048


def gelu_tanh(v):
    return jax.nn.gelu(v, approximate=True)


def local(
    hidden,
    norm_gain,
    gen_value,
    gen_head,
    critic_embed,
    critic_gain,
    critic_value,
    critic_head,
    noise,
    owner,
    tsteps,
    noise_mix,
    gap_weight,
):
    rows = hidden.shape[0]
    width = hidden.shape[1]
    latent_width = gen_head.shape[1]
    seq_count = lax.axis_size("seq")
    group_count = lax.axis_size("group")
    crit_rows = noise.shape[0]
    capacity = 2 * (rows // seq_count) - 1
    group_id = lax.axis_index("group")
    shard_id = group_id * seq_count + lax.axis_index("seq")
    critic_id = group_id // 2
    sign = jnp.where(critic_id == 1, 1.0, -1.0).astype(jnp.float32)
    inputs = hidden.astype(jnp.float32)
    inverse = lax.rsqrt(jnp.mean(inputs * inputs, axis=-1, keepdims=True) + 1e-06)
    gain = norm_gain.astype(jnp.float32)
    normed = (inputs * inverse * gain).astype(jnp.bfloat16)
    gen_full, critic_full = (
        lax.all_gather(gen_value, "seq", axis=0, tiled=True),
        lax.all_gather(critic_value, "seq", axis=0, tiled=True),
    )
    values = jnp.dot(normed, gen_full, preferred_element_type=jnp.float32)
    activated, gelu_back = jax.vjp(gelu_tanh, values)
    latent_part = jnp.dot(
        activated.astype(jnp.bfloat16), gen_head, preferred_element_type=jnp.float32
    )
    gen_latent = lax.psum(latent_part.astype(jnp.bfloat16), "tp")
    target = owner // crit_rows
    order = jnp.argsort(target, stable=True)
    sorted_target = target[order]
    counts = jnp.sum(
        (target[:, None] == jnp.arange(seq_count, dtype=jnp.int32)[None, :]).astype(jnp.int32),
        axis=0,
    )
    starts = jnp.cumsum(counts) - counts
    ranks = jnp.arange(rows, dtype=jnp.int32) - starts[sorted_target]
    slots = jnp.full((seq_count, capacity), -1, jnp.int32).at[sorted_target, ranks].set(order)
    filled = slots >= 0
    safe = jnp.maximum(slots, 0)
    send_rows = jnp.where(filled[..., None], gen_latent[safe], jnp.zeros((), jnp.bfloat16))
    send_place = jnp.where(filled, owner[safe] % crit_rows, crit_rows)
    send_frame = (shard_id * rows + safe) // FTOK
    got_rows, got_place, got_frame = (
        lax.all_to_all(
            jnp.tile(send_rows, (group_count, 1, 1)),
            ("group", "seq"),
            split_axis=0,
            concat_axis=0,
            tiled=True,
        ),
        lax.all_to_all(
            jnp.tile(send_place, (group_count, 1)),
            ("group", "seq"),
            split_axis=0,
            concat_axis=0,
            tiled=True,
        ),
        lax.all_to_all(
            jnp.tile(send_frame, (group_count, 1)),
            ("group", "seq"),
            split_axis=0,
            concat_axis=0,
            tiled=True,
        ),
    )
    flat_place = got_place.reshape(-1)
    placed = (
        jnp.zeros((crit_rows, latent_width), jnp.float32)
        .at[flat_place]
        .set(got_rows.reshape(-1, latent_width).astype(jnp.float32), mode="drop")
    )
    frame_at = (
        jnp.zeros((crit_rows,), jnp.int32).at[flat_place].set(got_frame.reshape(-1), mode="drop")
    )
    level_pick = (
        tsteps[:, None] == jnp.arange(noise_mix.shape[1], dtype=jnp.int32)[None, :]
    ).astype(jnp.float32)
    table = jnp.stack([noise_mix[0], noise_mix[1], gap_weight], axis=1)
    per_frame = jnp.dot(level_pick, table, precision=lax.Precision.HIGHEST)
    frame_pick = (
        frame_at[:, None] == jnp.arange(tsteps.shape[0], dtype=jnp.int32)[None, :]
    ).astype(jnp.float32)
    per_row = jnp.dot(frame_pick, per_frame, precision=lax.Precision.HIGHEST)
    noisy = (per_row[:, 0:1] * placed + per_row[:, 1:2] * noise.astype(jnp.float32)).astype(
        jnp.bfloat16
    )
    embed = lax.dynamic_index_in_dim(critic_embed, critic_id, 0, keepdims=False)
    critic_scale = lax.dynamic_index_in_dim(critic_gain, critic_id, 0, keepdims=False).astype(
        jnp.float32
    )
    block = min(512, crit_rows)
    pieces = []
    for start in range(0, crit_rows, block):
        embedded = jnp.dot(noisy[start : start + block], embed, preferred_element_type=jnp.float32)
        scale_rows = lax.rsqrt(jnp.mean(embedded * embedded, axis=-1, keepdims=True) + 1e-06)
        pieces.append((embedded * scale_rows * critic_scale).astype(jnp.bfloat16))
    critic_normed = jnp.concatenate(pieces, axis=0)
    critic_values = jnp.dot(critic_normed, critic_full, preferred_element_type=jnp.float32)
    critic_act = gelu_tanh(critic_values).astype(jnp.bfloat16)
    term = jnp.dot(critic_act, critic_head, preferred_element_type=jnp.float32) * sign
    gap = lax.psum(term.astype(jnp.bfloat16), ("group", "tp")).astype(jnp.float32)
    pull = (per_row[:, 2:3] * gap).astype(jnp.bfloat16)
    mine = lax.dynamic_slice_in_dim(got_place, group_id * seq_count, seq_count, 0)
    back_rows = jnp.where(
        (mine < crit_rows)[..., None],
        pull[jnp.minimum(mine, crit_rows - 1)],
        jnp.zeros((), jnp.bfloat16),
    )
    returned = lax.all_to_all(back_rows, "seq", split_axis=0, concat_axis=0, tiled=True)
    landing = jnp.where(filled, slots, rows).reshape(-1)
    cotangent = (
        jnp.zeros((rows, latent_width), jnp.bfloat16)
        .at[landing]
        .set(returned.reshape(-1, latent_width), mode="drop")
    )
    grad_act = lax.dot_general(
        cotangent, gen_head, (((1,), (1,)), ((), ())), preferred_element_type=jnp.float32
    )
    grad_values = gelu_back(grad_act)[0].astype(jnp.bfloat16)
    grad_part = lax.dot_general(
        grad_values, gen_full, (((1,), (1,)), ((), ())), preferred_element_type=jnp.float32
    )
    columns_dev = width // lax.axis_size("tp")
    first_col = lax.axis_index("tp") * columns_dev
    grad_normed = lax.psum(grad_part.astype(jnp.bfloat16), "tp").astype(jnp.float32)
    scaled = grad_normed * gain
    mixed = jnp.mean(inputs * scaled, axis=-1, keepdims=True)
    grad_in = inverse * scaled - inputs * inverse * inverse * inverse * mixed
    grad_hidden = lax.dynamic_slice_in_dim(grad_in, first_col, columns_dev, 1).astype(jnp.bfloat16)
    return (gen_latent, grad_hidden)


def solution(mesh):
    return jax.shard_map(
        local,
        mesh=mesh,
        in_specs=(
            P(("group", "seq"), None),
            P(),
            P("seq", "tp"),
            P("tp", None),
            P(),
            P(),
            P("seq", ("group", "tp")),
            P(("group", "tp"), None),
            P("seq", None),
            P(("group", "seq")),
            P(),
            P(),
            P(),
        ),
        out_specs=(P(("group", "seq"), None), P(("group", "seq"), "tp")),
        check_vma=False,
    )
```

profile of v0, /device:TPU:1, one launch (start us, length us, event | category | flops | bytes accessed | tf_op | source)
XLA Modules:
  0.0 621.2 jit_solution(10950657447792440149)
XLA Ops:
  7.2 0.7 all-gather.3.cloned.1.call-update
  7.9 0.7 and_select_fusion
  8.6 0.1 convert_reduce_fusion
  8.9 0.1 reduce.1
  9.0 3.2 sort.17
  12.2 1.9 gather_fusion
  14.2 0.7 fusion.95
  14.8 0.7 fusion.94
  15.6 4.4 compare_select_fusion.5
  20.1 15.6 %select_select_fusion = s32[256]{0:T(256)S(1)} fusion(pred[256]{0:T(512)(128)(4,1)S(1)} %get-tuple-element.28, pred[256]{0:T(512)(128)(4,1)S(1)} %get-tuple-element.26, pred[256]{0:T(512)(128)(4,1)S(1)} %get-tuple-element.25, pred[256]{0:T(512)(128)(4,1)S(1)} %get-tuple-element.24, pred[256]{0:T(512)(128)(4,1)S(1)} %get-tuple-element.23, ...), kind=kLoop, calls=%fused_computation.170 | loop fusion | flops 6400 | bytes 8548 | tf_op jit(solution)/shard_map/gather | solution.py:61
  35.7 12.7 %scatter_fusion = s32[32,15]{0,1:T(8,128)S(1)} fusion(s32[32,15]{0,1:T(8,128)S(1)} %broadcast_in_dim.36, s32[256]{0:T(256)S(1)} %bitcast.73, s32[256]{0:T(256)S(1)} %get-tuple-element.3), kind=kCustom, calls=%fused_computation.4 | custom fusion | bytes 5120 | tf_op jit(solution)/shard_map/scatter | solution.py:62
  48.6 0.1 reshape.265
  48.8 3.5 gather_fusion.1
  52.6 0.6 tile.8
  53.2 23.0 %all-to-all-start = ((s32[128,1,15]{2,1,0:T(1,128)}), s32[128,1,15]{2,1,0:T(1,128)S(1)}, u32[]{:S(2)}, u32[]{:S(2)}) async-start(s32[128,1,15]{2,1,0:T(1,128)} %bitcast.38), calls=%async_computation | async-start | bytes 131072 | tf_op jit(solution)/shard_map/all_to_all | solution.py:76
  76.2 0.7 all-gather.5.cloned.1.call-update
  76.9 2.4 fusion.4
  79.6 110.4 %all-gather.3.cloned.1.call-done = bf16[5120,640]{1,0:T(8,128)(2,1)} async-done(((bf16[160,640]{1,0:T(8,128)(2,1)}), bf16[5120,640]{1,0:T(8,128)(2,1)}) %all-gather.3.cloned.1.call-update) | async-done | bytes 6553616 | tf_op jit(solution)/shard_map/all_gather | solution.py:44
  190.0 5.9 fusion.6
  196.0 0.3 convolution_convert_fusion.1
  196.3 18.2 %psum.21 = bf16[256,64]{0,1:T(8,128)(2,1)S(1)} all-reduce(bf16[256,64]{0,1:T(8,128)(2,1)S(1)} %convolution_convert_fusion.1), channel_id=1, replica_groups=mesh['group'=4,'seq'=32,'tp'=4] {'tp'}, use_global_device_ids=true, to_apply=%region_1.2 | all-reduce | flops 16384 | bytes 65536 | tf_op jit(solution)/shard_map/psum | solution.py:52
  214.4 0.1 copy.72
  214.6 1.5 gather_fusion.2
  216.1 0.6 tile.9
  216.8 12.5 %all-to-all-start.1 = ((s32[128,1,15]{2,1,0:T(1,128)}), s32[128,1,15]{2,1,0:T(1,128)S(1)}, u32[]{:S(2)}, u32[]{:S(2)}) async-start(s32[128,1,15]{2,1,0:T(1,128)} %bitcast.40), calls=%async_computation.1 | async-start | bytes 131072 | tf_op jit(solution)/shard_map/all_to_all | solution.py:83
  229.3 0.1 broadcast_select_fusion
  229.5 1.2 reshape.449
  230.7 15.2 %all-to-all-done.1 = s32[128,1,15]{2,1,0:T(1,128)S(1)} async-done(((s32[128,1,15]{2,1,0:T(1,128)}), s32[128,1,15]{2,1,0:T(1,128)S(1)}, u32[]{:S(2)}, u32[]{:S(2)}) %all-to-all-start.1) | async-done | bytes 7712 | tf_op jit(solution)/shard_map/all_to_all | solution.py:83
  245.9 6.3 %all-to-all-start.2 = ((bf16[128,2,480]{2,1,0:T(2,128)(2,1)}), bf16[128,2,480]{2,1,0:T(2,128)(2,1)S(1)}, u32[]{:S(2)}, u32[]{:S(2)}) async-start(bf16[128,2,480]{2,1,0:T(2,128)(2,1)} %reshape.449), calls=%async_computation.2 | async-start | bytes 524288 | tf_op jit(solution)/shard_map/all_to_all | solution.py:69
  252.3 0.2 fusion.57
  252.5 0.2 copy.73
  252.7 0.6 broadcast.526
  253.3 0.8 reduce.59
  254.2 0.2 reshape.211
  254.4 0.9 reduce.60
  255.3 0.2 reshape.297
  255.6 10.0 %scatter_custom_fusion.1 = s32[1024]{0:T(1024)S(1)} fusion(s32[1920]{0:T(1024)S(1)} %fusion.70, s32[1920]{0:T(1024)S(1)} %reshape.297, s32[]{:T(128)} %constant.72.clone.1), kind=kCustom, calls=%fused_computation.158 | custom fusion | bytes 4100 | tf_op jit(solution)/shard_map/scatter | solution.py:98
  265.6 0.4 fusion.44
  266.1 8.4 %all-to-all-done.2 = bf16[128,2,480]{2,1,0:T(2,128)(2,1)S(1)} async-done(((bf16[128,2,480]{2,1,0:T(2,128)(2,1)}), bf16[128,2,480]{2,1,0:T(2,128)(2,1)S(1)}, u32[]{:S(2)}, u32[]{:S(2)}) %all-to-all-start.2) | async-done | bytes 245792 | tf_op jit(solution)/shard_map/all_to_all | solution.py:69
  274.4 0.4 reshape.450
  274.9 0.1 reshape.305
  275.0 8.2 %scatter_custom_fusion.2 = f32[1024,64]{1,0:T(8,128)S(1)} fusion(s32[1920]{0:T(1024)S(1)} %fusion.70, f32[1920,64]{1,0:T(8,128)S(1)} %reshape.305, f32[]{:T(128)} %constant.52.clone.1), kind=kCustom, calls=%fused_computation.76 | custom fusion | bytes 262148 | tf_op jit(solution)/shard_map/scatter | solution.py:95
  283.2 0.3 add_convert_fusion
  283.5 1.6 multiply_reduce_fusion
  285.1 1.6 multiply_reduce_fusion.1
  286.8 5.9 multiply_convert_fusion.1
  292.7 60.5 %all-gather.5.cloned.1.call-done = bf16[5120,320]{1,0:T(8,128)(2,1)} async-done(((bf16[160,320]{1,0:T(8,128)(2,1)}), bf16[5120,320]{1,0:T(8,128)(2,1)}) %all-gather.5.cloned.1.call-update) | async-done | bytes 3276816 | tf_op jit(solution)/shard_map/all_gather | solution.py:45
  353.1 9.9 %fusion.20 = bf16[1024,64]{0,1:T(8,128)(2,1)} fusion(bf16[320,64]{0,1:T(8,128)(2,1)S(1)} %copy-done.9, bf16[5120,320]{1,0:T(8,128)(2,1)} %all-gather.5.cloned.1.call-done, bf16[512,5120]{1,0:T(8,128)(2,1)} %get-tuple-element.37, bf16[512,5120]{1,0:T(8,128)(2,1)} %get-tuple-element.36, f32[]{:T(128)S(6)} %select_n.124), kind=kOutput, calls=%fused_computation.42 | convolution fusion | flops 3421437952 | bytes 13934596 | tf_op jit(solution)/shard_map/dot_general | solution.py:125
  363.1 0.1 reshape.281
  363.3 133.3 %all-reduce.3.cloned.1.call-done = bf16[1024,64]{0,1:T(8,128)(2,1)} async-done(((bf16[1024,64]{0,1:T(8,128)(2,1)}), bf16[1024,64]{0,1:T(8,128)(2,1)}) %all-reduce.3.cloned.1.call-update) | async-done | bytes 131088 | tf_op jit(solution)/shard_map/psum | solution.py:126
  496.6 0.9 multiply_convert_fusion.6
  497.6 0.2 copy.75
  497.7 1.5 gather_fusion.3
  499.3 0.1 broadcast_select_fusion.1
  499.4 0.8 reshape.451
  500.2 14.4 %all-to-all-start.3 = ((bf16[32,2,480]{2,1,0:T(2,128)(2,1)}), bf16[32,2,480]{2,1,0:T(2,128)(2,1)S(1)}, u32[]{:S(2)}, u32[]{:S(2)}) async-start(bf16[32,2,480]{2,1,0:T(2,128)(2,1)} %reshape.451), calls=%async_computation.3 | async-start | bytes 131072 | tf_op jit(solution)/shard_map/all_to_all | solution.py:134
  514.8 0.1 reshape.210
  514.9 14.5 %all-to-all-done.3 = bf16[32,2,480]{2,1,0:T(2,128)(2,1)S(1)} async-done(((bf16[32,2,480]{2,1,0:T(2,128)(2,1)}), bf16[32,2,480]{2,1,0:T(2,128)(2,1)S(1)}, u32[]{:S(2)}, u32[]{:S(2)}) %all-to-all-start.3) | async-done | bytes 61472 | tf_op jit(solution)/shard_map/all_to_all | solution.py:134
  529.4 0.1 reshape.452
  529.6 1.9 scatter_custom_fusion.3
  531.5 7.0 %convolution_convert_fusion = bf16[256,5120]{1,0:T(8,128)(2,1)} fusion(bf16[5120,640]{1,0:T(8,128)(2,1)} %all-gather.3.cloned.1.call-done, f32[256,640]{1,0:T(8,128)S(1)} %copy-done.13, bf16[256,64]{1,0:T(8,128)(2,1)S(1)} %scatter_custom_fusion.3, bf16[640,64]{0,1:T(8,128)(2,1)S(1)} %copy-done.8), kind=kOutput, calls=%fused_computation.19 | convolution fusion | flops 1703280640 | bytes 9945088 | tf_op jit(solution)/shard_map/dot_general | solution.py:145
  538.6 70.6 %all-reduce.5.cloned.1.call-done = bf16[256,5120]{1,0:T(8,128)(2,1)} async-done(((bf16[256,5120]{1,0:T(8,128)(2,1)}), bf16[256,5120]{1,0:T(8,128)(2,1)}) %all-reduce.5.cloned.1.call-update) | async-done | bytes 2621456 | tf_op jit(solution)/shard_map/psum | solution.py:150
  609.2 4.3 fusion.5
  613.5 1.1 fusion.17
  (75 shorter events, 1.8 us)
Async XLA Ops:
  7.2 276.4 %copy-start = (bf16[2,64,5120]{2,1,0:T(8,128)(2,1)S(1)}, bf16[2,64,5120]{2,1,0:T(8,128)(2,1)}, u32[]{:S(2)}) copy-start(bf16[2,64,5120]{2,1,0:T(8,128)(2,1)} %param.17) | copy-start | bytes 3932164
  7.2 41.5 %copy-start.2 = (s32[256]{0:T(256)S(1)}, s32[256]{0:T(256)}, u32[]{:S(2)}) copy-start(s32[256]{0:T(256)} %param.22) | copy-start | bytes 3076
  7.2 182.8 %all-gather.3.cloned.1.call-start = ((), (), s32[]{:S(2)}) async-start(), calls=%async_computation.4 | async-start | bytes 6758400 | tf_op jit(solution)/shard_map/all_gather | solution.py:44
  48.7 30.5 %copy-start.7 = (f32[2,1000]{1,0:T(2,128)S(1)}, f32[2,1000]{1,0:T(2,128)}, u32[]{:S(2)}) copy-start(f32[2,1000]{1,0:T(2,128)} %param.24) | copy-start | bytes 24004
  48.7 30.6 %copy-start.6 = (bf16[5120]{0:T(1024)(128)(2,1)S(1)}, bf16[5120]{0:T(1024)(128)(2,1)}, u32[]{:S(2)}) copy-start(bf16[5120]{0:T(1024)(128)(2,1)} %param.14) | copy-start | bytes 30724
  48.8 30.8 %copy-start.5 = (bf16[2,5120]{1,0:T(2,128)(2,1)S(1)}, bf16[2,5120]{1,0:T(2,128)(2,1)}, u32[]{:S(2)}) copy-start(bf16[2,5120]{1,0:T(2,128)(2,1)} %param.18) | copy-start | bytes 61444
  53.2 162.9 %all-to-all-start = ((s32[128,1,15]{2,1,0:T(1,128)}), s32[128,1,15]{2,1,0:T(1,128)S(1)}, u32[]{:S(2)}, u32[]{:S(2)}) async-start(s32[128,1,15]{2,1,0:T(1,128)} %bitcast.38), calls=%async_computation | async-start | bytes 131072 | tf_op jit(solution)/shard_map/all_to_all | solution.py:76
  76.2 277.0 %all-gather.5.cloned.1.call-start = ((), (), s32[]{:S(2)}) async-start(), calls=%async_computation.5 | async-start | bytes 4055040 | tf_op jit(solution)/shard_map/all_gather | solution.py:45
  79.5 116.3 %copy-start.8 = (bf16[640,64]{0,1:T(8,128)(2,1)S(1)}, bf16[640,64]{0,1:T(8,128)(2,1)}, u32[]{:S(2)}) copy-start(bf16[640,64]{0,1:T(8,128)(2,1)} %param.16) | copy-start | bytes 245764
  195.9 78.5 %copy-start.12 = (f32[256,640]{1,0:T(8,128)}, f32[256,640]{1,0:T(8,128)S(1)}, u32[]{:S(2)}) copy-start(f32[256,640]{1,0:T(8,128)S(1)} %fusion.6) | copy-start | bytes 1966084
  195.9 56.4 %copy-start.10 = (f32[1000]{0:T(1024)S(1)}, f32[1000]{0:T(1024)}, u32[]{:S(2)}) copy-start(f32[1000]{0:T(1024)} %param.25) | copy-start | bytes 12004
  195.9 56.4 %copy-start.11 = (s32[16]{0:T(128)S(1)}, s32[16]{0:T(128)}, u32[]{:S(2)}) copy-start(s32[16]{0:T(128)} %param.23) | copy-start | bytes 196
  195.9 56.6 %copy-start.3 = (bf16[1024,64]{0,1:T(8,128)(2,1)S(1)}, bf16[1024,64]{0,1:T(8,128)(2,1)}, u32[]{:S(2)}) copy-start(bf16[1024,64]{0,1:T(8,128)(2,1)} %param.21) | copy-start | bytes 393220
  214.4 70.7 %copy-start.4 = (bf16[256,64]{0,1:T(8,128)(2,1)}, bf16[256,64]{0,1:T(8,128)(2,1)S(1)}, u32[]{:S(2)}) copy-start(bf16[256,64]{0,1:T(8,128)(2,1)S(1)} %psum.21) | copy-start | bytes 98308
  216.8 29.1 %all-to-all-start.1 = ((s32[128,1,15]{2,1,0:T(1,128)}), s32[128,1,15]{2,1,0:T(1,128)S(1)}, u32[]{:S(2)}, u32[]{:S(2)}) async-start(s32[128,1,15]{2,1,0:T(1,128)} %bitcast.40), calls=%async_computation.1 | async-start | bytes 131072 | tf_op jit(solution)/shard_map/all_to_all | solution.py:83
  245.9 28.5 %all-to-all-start.2 = ((bf16[128,2,480]{2,1,0:T(2,128)(2,1)}), bf16[128,2,480]{2,1,0:T(2,128)(2,1)S(1)}, u32[]{:S(2)}, u32[]{:S(2)}) async-start(bf16[128,2,480]{2,1,0:T(2,128)(2,1)} %reshape.449), calls=%async_computation.2 | async-start | bytes 524288 | tf_op jit(solution)/shard_map/all_to_all | solution.py:69
  252.3 244.4 %all-reduce.3.cloned.1.call-start = ((), (), s32[]{:S(2)}) async-start(), calls=%async_computation.6 | async-start | bytes 262144 | tf_op jit(solution)/shard_map/psum | solution.py:126
  286.7 66.4 %copy-start.9 = (bf16[320,64]{0,1:T(8,128)(2,1)S(1)}, bf16[320,64]{0,1:T(8,128)(2,1)}, u32[]{:S(2)}) copy-start(bf16[320,64]{0,1:T(8,128)(2,1)} %param.20) | copy-start | bytes 122884
  353.1 178.4 %copy-start.13 = (f32[256,640]{1,0:T(8,128)S(1)}, f32[256,640]{1,0:T(8,128)}, u32[]{:S(2)}) copy-start(f32[256,640]{1,0:T(8,128)} %copy-done.12) | copy-start | bytes 1966084
  500.2 29.2 %all-to-all-start.3 = ((bf16[32,2,480]{2,1,0:T(2,128)(2,1)}), bf16[32,2,480]{2,1,0:T(2,128)(2,1)S(1)}, u32[]{:S(2)}, u32[]{:S(2)}) async-start(bf16[32,2,480]{2,1,0:T(2,128)(2,1)} %reshape.451), calls=%async_computation.3 | async-start | bytes 131072 | tf_op jit(solution)/shard_map/all_to_all | solution.py:134
  514.7 94.5 %all-reduce.5.cloned.1.call-start = ((), (), s32[]{:S(2)}) async-start(), calls=%async_computation.7 | async-start | bytes 5242880 | tf_op jit(solution)/shard_map/psum | solution.py:150
  609.2 5.4 copy-start.1
Sparse Core Ops, SparseCore 0:
  11.1 178.7 all-gather.2
  193.1 160.0 all-gather.4
  363.1 133.4 all-reduce.2
  538.7 70.4 all-reduce.4
where the time goes:
time: 622 us; the launch traced here: 621 us
  waiting for transfers between devices  414 us (67%)
  starting transfers between devices  56.4 us (9%)
  local copies, waits for them, and re-layouts  49.7 us (8%)
  other arithmetic  41.3 us (7%)
  matrix products  26.9 us (4%)
  blocking collectives  18.2 us (3%)
  between operations  14.3 us (2%)
    psum x1, waiting for transfers between devices, local(): lax.psum(term.astype(jnp.bfloat16), ('group', 'tp')).astype(jnp.float32)  133 us
    all_gather x1, waiting for transfers between devices, local(): lax.all_gather(gen_value, 'seq', axis=0, tiled=True)  110 us
    psum x1, waiting for transfers between devices, local(): lax.psum(grad_part.astype(jnp.bfloat16), 'tp').astype(jnp.float32)  70.6 us
    all_gather x1, waiting for transfers between devices, local(): lax.all_gather(critic_value, 'seq', axis=0, tiled=True)  60.5 us
    all_to_all x1, starting transfers between devices, local(): lax.all_to_all(jnp.tile(send_place, (group_count, 1)), ('group', 'seq'),...  23 us
    gather x3, other arithmetic, local(): ranks = jnp.arange(rows, dtype=jnp.int32) - starts[sorted_target]  20.1 us
    psum x1, blocking collectives, local(): gen_latent = lax.psum(latent_part.astype(jnp.bfloat16), 'tp')  18.2 us
    all_to_all x1, waiting for transfers between devices, local(): lax.all_to_all(jnp.tile(send_frame, (group_count, 1)), ('group', 'seq'),...  15.2 us
  transfers between devices with their start and end apart: 8, of which 7 were waited for; matrix products, arithmetic and copies ran while one was open for 14% of the time, Pallas kernels for 0%

commit v1 on v0

v1 whole, which is shorter than its diff:
```python
import jax
import jax.numpy as jnp
from jax import lax
from jax.sharding import PartitionSpec as P

FTOK = 2048
SLOTS = 16
F32 = jnp.float32
BF16 = jnp.bfloat16


def gelu_tanh(v):
    return jax.nn.gelu(v, approximate=True)


class Axis:
    def __init__(self, name, count, stride):
        self.name, self.count, self.stride = name, count, stride

    def index(self):
        return (lax.axis_index(self.name) // self.stride) % self.count

    def pairs(self, shift):
        size = lax.axis_size(self.name)
        out = []
        for i in range(size):
            mine = (i // self.stride) % self.count
            out.append((i, i + ((mine + shift) % self.count - mine) * self.stride))
        return out

    def send(self, x, shift):
        return lax.ppermute(x, self.name, self.pairs(shift))


def pick(x, i, dim):
    return lax.dynamic_index_in_dim(x, i, dim, keepdims=False)


def put(x, piece, i, dim):
    return lax.dynamic_update_index_in_dim(x, piece, i, dim)


def reduce_scatter(x, axis):
    me, n = axis.index(), axis.count
    total = pick(x, me, 0)
    for j in range(1, n):
        total = total + axis.send(pick(x, (me + j) % n, 0), j)
    return total


def gather(x, axis):
    me, n = axis.index(), axis.count
    out = put(jnp.zeros((n,) + x.shape, x.dtype), x, me, 0)
    for j in range(1, n):
        out = put(out, axis.send(x, j), (me - j) % n, 0)
    return out


def exchange(x, axis, dim):
    me, n = axis.index(), axis.count
    out = x
    for j in range(1, n):
        out = put(out, axis.send(pick(x, (me + j) % n, dim), j), (me - j) % n, dim)
    return out


def ring_gather(x, y_hi, z):
    rows = x.shape[0]
    n = z.count
    me_y, me_z = y_hi.index(), z.index()
    out = jnp.zeros((2 * n * rows,) + x.shape[1:], x.dtype)
    far = y_hi.send(x, 1)
    for piece, at_y in ((x, me_y), (far, 1 - me_y)):

        def place(out, part, at_z, skip=0):
            start = (at_y * n + at_z % n) * rows + skip
            return lax.dynamic_update_slice(out, part, (start, jnp.zeros_like(start)))

        out = place(out, piece, me_z)
        up = down = piece
        for step in range(1, n // 2):
            up, down = z.send(up, 1), z.send(down, -1)
            out = place(out, up, me_z - step)
            out = place(out, down, me_z + step)
        half = rows // 2
        out = place(out, z.send(up[:half], 1), me_z + n // 2)
        out = place(out, z.send(down[half:], -1), me_z + n // 2, half)
    return out


def local(
    hidden,
    norm_gain,
    gen_value,
    gen_head,
    critic_embed,
    critic_gain,
    critic_value,
    critic_head,
    noise,
    owner,
    tsteps,
    noise_mix,
    gap_weight,
):
    rows, width = hidden.shape
    latent_width = gen_head.shape[1]
    seq_count = lax.axis_size("seq")
    group_id, seq_id, tp_id = (lax.axis_index(a) for a in ("group", "seq", "tp"))
    shard_id = group_id * seq_count + seq_id
    n_z = seq_count // 2
    y_hi, z = Axis("seq", 2, n_z), Axis("seq", n_z, 1)
    z_hi, z_lo = Axis("seq", n_z // 4, 4), Axis("seq", 4, 1)
    y_lo, core = Axis("tp", 2, 2), Axis("tp", 2, 1)
    tp, group = Axis("tp", 4, 1), Axis("group", 4, 1)

    with jax.named_scope("gather_value"):
        gen_full = ring_gather(gen_value, y_hi, z)

    with jax.named_scope("critic_matrix"):
        depth, cols = critic_value.shape
        critic_id = group_id // 2
        embed = lax.dynamic_slice(
            critic_embed, (critic_id, 0, seq_id * depth), (1, latent_width, depth)
        )[0].astype(F32)
        scale = lax.dynamic_slice(critic_gain, (critic_id, seq_id * depth), (1, depth))
        part = jnp.dot(
            embed * scale.astype(F32),
            critic_value.astype(F32),
            precision=lax.Precision.HIGHEST,
        )
        each = latent_width // seq_count
        part = part.reshape(4, n_z // 4, 2, each, cols)
        part = reduce_scatter(part, z_lo)
        part = reduce_scatter(part, z_hi)
        part = reduce_scatter(part, y_hi)
        part = gather(part, z_hi)
        part = gather(part, y_hi)
        part = gather(part, z_lo)
        part = part.transpose(0, 2, 1, 3, 4).reshape(latent_width, cols)
        part = gather(gather(part, tp), group)
        matrix = part.transpose(2, 0, 1, 3).reshape(latent_width, 16 * cols)
        matrix_hi = matrix.astype(BF16)
        matrix_lo = (matrix - matrix_hi.astype(F32)).astype(BF16)
        matrix_two = jnp.concatenate([matrix_hi, matrix_lo], axis=0)

    with jax.named_scope("critic_head"):
        head = gather(gather(critic_head, tp), group)
        head = jnp.concatenate([-head[:2], head[2:]], axis=0).reshape(16 * cols, latent_width)

    with jax.named_scope("fetch_noise"):
        crit_rows = noise.shape[0]
        target = owner // crit_rows
        at = (target[:, None] == jnp.arange(seq_count, dtype=jnp.int32)[None, :]).astype(BF16)
        ids = jnp.arange(rows, dtype=jnp.int32)
        before = (ids[None, :] < ids[:, None]).astype(BF16)
        prefix = jnp.dot(before, at, preferred_element_type=F32)
        rank = jnp.sum(prefix * at.astype(F32), axis=1).astype(jnp.int32)
        slot = target * SLOTS + rank
        total = seq_count * SLOTS
        holds = jnp.arange(total, dtype=jnp.int32)[:, None] == slot[None, :]
        wanted = jnp.sum(jnp.where(holds, (owner % crit_rows + 1)[None, :], 0), axis=1) - 1
        wanted = wanted.reshape(2, n_z // 4, 4, SLOTS)
        wanted = exchange(exchange(exchange(wanted, z_lo, 2), z_hi, 1), y_hi, 0)
        take = wanted.reshape(total)[:, None] == jnp.arange(crit_rows, dtype=jnp.int32)[None, :]
        found = jnp.dot(take.astype(BF16), noise, preferred_element_type=F32).astype(BF16)
        found = found.reshape(2, n_z // 4, 4, SLOTS, latent_width)
        found = exchange(exchange(exchange(found, y_hi, 0), z_hi, 1), z_lo, 2)
        own_noise = lax.dot_general(
            holds.astype(BF16),
            found.reshape(total, latent_width),
            (((0,), (0,)), ((), ())),
            preferred_element_type=F32,
        )

    with jax.named_scope("levels"):
        level = tsteps[shard_id * rows // FTOK]
        signal_mix, noise_part = noise_mix[0, level], noise_mix[1, level] * own_noise
        weight = gap_weight[level]

    with jax.named_scope("forward"):
        inputs = hidden.astype(F32)
        inverse = lax.rsqrt(jnp.mean(inputs * inputs, axis=-1, keepdims=True) + 1e-06)
        normed = (inputs * inverse * norm_gain.astype(F32)).astype(BF16)
        values = jnp.dot(normed, gen_full, preferred_element_type=F32)
        activated, gelu_back = jax.vjp(gelu_tanh, values)
        latent_part = jnp.dot(activated.astype(BF16), gen_head, preferred_element_type=F32)
        parts = lax.all_gather(latent_part.astype(BF16), "tp", axis=0)
        gen_latent = jnp.sum(parts.astype(F32), axis=0).astype(BF16)
        slope = gelu_back(jnp.ones_like(values))[0]

    with jax.named_scope("critics"):
        noisy = (signal_mix * gen_latent.astype(F32) + noise_part).astype(BF16)
        scales = []
        for which in range(2):
            embedded = jnp.dot(noisy, critic_embed[which], preferred_element_type=F32)
            scales.append(
                lax.rsqrt(jnp.mean(embedded * embedded, axis=-1, keepdims=True) + 1e-06)
            )
        raw = jnp.dot(
            jnp.concatenate([noisy, noisy], axis=1), matrix_two, preferred_element_type=F32
        )
        half = raw.shape[1] // 2
        acts = jnp.concatenate(
            [
                gelu_tanh(raw[:, :half] * scales[0]).astype(BF16),
                gelu_tanh(raw[:, half:] * scales[1]).astype(BF16),
            ],
            axis=1,
        )
        gap = jnp.dot(acts, head, preferred_element_type=F32)
        cotangent = (weight * gap).astype(BF16)

    with jax.named_scope("backward"):
        grad_act = lax.dot_general(
            cotangent, gen_head, (((1,), (1,)), ((), ())), preferred_element_type=F32
        )
        grad_values = (slope * grad_act).astype(BF16)
        mixed = jnp.sum(grad_values.astype(F32) * values, axis=1)
        for j in range(1, 4):
            mixed = mixed + tp.send(jnp.sum(grad_values.astype(F32) * values, axis=1), j)
        columns = width // 4
        yl, c = y_lo.index(), core.index()

        def grad_slice(at_y, at_c):
            start = (at_y * 2 + at_c) * columns
            weights = lax.dynamic_slice_in_dim(gen_full, start, columns, 0)
            return lax.dot_general(
                grad_values, weights, (((1,), (1,)), ((), ())), preferred_element_type=F32
            )

        far = core.send(grad_slice(1 - yl, 1 - c).astype(BF16), 1)
        far = (grad_slice(1 - yl, c) + far.astype(F32)).astype(BF16)
        far = y_lo.send(far, 1)
        near = core.send(grad_slice(yl, 1 - c).astype(BF16), 1)
        near = grad_slice(yl, c) + near.astype(F32)
        grad_normed = near + far.astype(F32)
        first = tp_id * columns
        gain = lax.dynamic_slice_in_dim(norm_gain, first, columns, 0).astype(F32)
        own = lax.dynamic_slice_in_dim(hidden, first, columns, 1).astype(F32)
        pulled = inverse * inverse * (mixed / width)[:, None]
        grad_hidden = (inverse * (grad_normed * gain) - own * pulled).astype(BF16)
    return (gen_latent, grad_hidden)


def solution(mesh):
    return jax.shard_map(
        local,
        mesh=mesh,
        in_specs=(
            P(("group", "seq"), None),
            P(),
            P("seq", "tp"),
            P("tp", None),
            P(),
            P(),
            P("seq", ("group", "tp")),
            P(("group", "tp"), None),
            P("seq", None),
            P(("group", "seq")),
            P(),
            P(),
            P(),
        ),
        out_specs=(P(("group", "seq"), None), P(("group", "seq"), "tp")),
        check_vma=False,
    )
```

time: 622 us -> 481 us (0.77)
  waiting for transfers between devices: 414 us -> 61.6 us
  starting transfers between devices: 56.4 us -> 290 us
  other arithmetic: 41.3 us -> 10.2 us
  local copies, waits for them, and re-layouts: 49.7 us -> 67.2 us
  between operations: 14.3 us -> 5.35 us
    ppermute x0 -> x79, starting transfers between devices: none -> 290 us  [send(): return lax.ppermute(x, self.name, self.pairs(shift))]
    psum x2 -> x0, waiting for transfers between devices: 204 us -> none  [the longest x1 133 us: local(): lax.psum(term.astype(jnp.bfloat16), ('group', 'tp')).astype(jnp.float32)]
    all_gather x2 -> x0, waiting for transfers between devices: 171 us -> none  [the longest x1 110 us: local(): lax.all_gather(gen_value, 'seq', axis=0, tiled=True)]
    ppermute x0 -> x79, waiting for transfers between devices: none -> 61.6 us  [send(): return lax.ppermute(x, self.name, self.pairs(shift))]
    all_to_all x4 -> x0, starting transfers between devices: 56.2 us -> none  [the longest x1 23 us: local(): lax.all_to_all(jnp.tile(send_place, (group_count, 1)), ('group', 'seq'),...]
    dynamic_update_slice x0 -> x70, local copies, waits for them, and re-layouts: none -> 53.8 us  [the longest x34 34.8 us: place(): return lax.dynamic_update_slice(out, part, (start, jnp.zeros_like(start)))]
    all_to_all x4 -> x0, waiting for transfers between devices: 38.1 us -> none  [the longest x1 15.2 us: local(): lax.all_to_all(jnp.tile(send_frame, (group_count, 1)), ('group', 'seq'),...]
    scatter x4 -> x0, local copies, waits for them, and re-layouts: 32.8 us -> none  [the longest x1 12.7 us: local(): jnp.full((seq_count, capacity), -1, jnp.int32).at[sorted_target, ranks]]
  transfers between devices with their start and end apart: 8 -> 79, of which waited for: 7 -> 16; matrix products, arithmetic and copies ran while one was open for 14% -> 17% of each run, Pallas kernels for 0% -> 0%
where the time goes in v1:
time: 481 us; the launch traced here: 477 us
  starting transfers between devices  290 us (60%)
  local copies, waits for them, and re-layouts  67.2 us (14%)
  waiting for transfers between devices  61.6 us (13%)
  matrix products  26.2 us (5%)
  blocking collectives  16.7 us (3%)
  other arithmetic  10.2 us (2%)
  between operations  5.35 us (1%)
    ppermute x79, starting transfers between devices, send(): return lax.ppermute(x, self.name, self.pairs(shift))  290 us
    ppermute x79, waiting for transfers between devices, send(): return lax.ppermute(x, self.name, self.pairs(shift))  61.6 us
    dynamic_update_slice x34, local copies, waits for them, and re-layouts, place(): return lax.dynamic_update_slice(out, part, (start, jnp.zeros_like(start)))  34.8 us
    dynamic_update_slice x36, local copies, waits for them, and re-layouts, put(): return lax.dynamic_update_index_in_dim(x, piece, i, dim)  19 us
    all_gather x1, blocking collectives, local(): parts = lax.all_gather(latent_part.astype(BF16), 'tp', axis=0)  16.7 us
    dot_general x4, matrix products, grad_slice(): lax.dot_general(grad_values, weights, (((1,), (1,)), ((), ())), preferred...  9.86 us
  transfers between devices with their start and end apart: 79, of which 16 were waited for; matrix products, arithmetic and copies ran while one was open for 17% of the time, Pallas kernels for 0%

profile of v1, /device:TPU:1, one launch (start us, length us, event | category | flops | bytes accessed | tf_op | source)
XLA Modules:
  0.0 477.3 jit_solution(14432067300919079240)
XLA Ops:
  0.6 4.5 collective-permute-start
  5.2 9.5 %collective-permute-start.1 = (bf16[160,640]{1,0:T(8,128)(2,1)}, bf16[160,640]{1,0:T(8,128)(2,1)}, u32[]{:S(2)}, u32[]{:S(2)}) collective-permute-start(bf16[160,640]{1,0:T(8,128)(2,1)} %param.15), channel_id=1, source_target_pairs={{0,60},{4,0},{8,4},{12,8},{16,12},{20,16},{24,20},{28,24},{32,28},... | collective-permute-start | bytes 614408 | tf_op jit(solution)/shard_map/gather_value/ppermute | solution.py:32
  19.8 5.2 %collective-permute-start.35 = (s32[2,4,16]{2,1,0:T(4,128)S(1)}, s32[2,4,16]{2,1,0:T(4,128)S(1)}, u32[]{:S(2)}, u32[]{:S(2)}) collective-permute-start(s32[2,4,16]{2,1,0:T(4,128)S(1)} %bitcast.212), channel_id=1, source_target_pairs={{0,12},{4,0},{8,4},{12,8},{16,28},{20,16},{24,20},{28,24},{32,44},... | collective-permute-start | bytes 1544 | tf_op jit(solution)/shard_map/fetch_noise/ppermute | solution.py:32
  35.9 3.2 broadcast_in_dim.183
  42.9 3.1 collective-permute-start.48
  46.1 3.8 collective-permute-start.36
  50.7 3.7 collective-permute-done.36
  54.4 8.9 %collective-permute-start.37 = (s32[2,4,16]{2,1,0:T(4,128)S(1)}, s32[2,4,16]{2,1,0:T(4,128)S(1)}, u32[]{:S(2)}, u32[]{:S(2)}) collective-permute-start(s32[2,4,16]{2,1,0:T(4,128)S(1)} %get-tuple-element.24), channel_id=1, source_target_pairs={{0,32},{4,36},{8,40},{12,44},{16,48},{20,52},{24,56},{28,60},{32,0... | collective-permute-start | bytes 1544 | tf_op jit(solution)/shard_map/fetch_noise/ppermute | solution.py:32
  67.7 5.7 %collective-permute-start.38 = (s32[2,4,16]{2,1,0:T(4,128)S(1)}, s32[2,4,16]{2,1,0:T(4,128)S(1)}, u32[]{:S(2)}, u32[]{:S(2)}) collective-permute-start(s32[2,4,16]{2,1,0:T(4,128)S(1)} %get-tuple-element.23), channel_id=1, source_target_pairs={{0,48},{4,52},{8,56},{12,60},{16,0},{20,4},{24,8},{28,12},{32,16},... | collective-permute-start | bytes 1544 | tf_op jit(solution)/shard_map/fetch_noise/ppermute | solution.py:32
  73.4 2.5 collective-permute-done.38
  75.9 4.2 collective-permute-start.49
  80.2 4.8 %collective-permute-start.39 = (s32[4,4,16]{2,1,0:T(4,128)S(1)}, s32[4,4,16]{2,1,0:T(4,128)S(1)}, u32[]{:S(2)}, u32[]{:S(2)}) collective-permute-start(s32[4,4,16]{2,1,0:T(4,128)S(1)} %fusion.84), channel_id=1, source_target_pairs={{0,64},{4,68},{8,72},{12,76},{16,80},{20,84},{24,88},{28,92},{32,9... | collective-permute-start | bytes 3080 | tf_op jit(solution)/shard_map/fetch_noise/ppermute | solution.py:32
  85.1 4.0 collective-permute-start.50
  89.2 8.7 %collective-permute-start.51 = (f32[2,2,320]{2,1,0:T(2,128)S(1)}, f32[2,2,320]{2,1,0:T(2,128)S(1)}, u32[]{:S(2)}, u32[]{:S(2)}) collective-permute-start(f32[2,2,320]{2,1,0:T(2,128)S(1)} %bitcast.209), channel_id=1, source_target_pairs={{0,32},{4,36},{8,40},{12,44},{16,48},{20,52},{24,56},{28,60},{32,0... | collective-permute-start | bytes 15368 | tf_op jit(solution)/shard_map/critic_matrix/ppermute | solution.py:32
  97.9 5.2 %collective-permute-start.52 = (f32[2,2,320]{2,1,0:T(2,128)S(1)}, f32[2,2,320]{2,1,0:T(2,128)S(1)}, u32[]{:S(2)}, u32[]{:S(2)}) collective-permute-start(f32[2,2,320]{2,1,0:T(2,128)S(1)} %bitcast.208), channel_id=1, source_target_pairs={{0,48},{4,52},{8,56},{12,60},{16,0},{20,4},{24,8},{28,12},{32,16},... | collective-permute-start | bytes 15368 | tf_op jit(solution)/shard_map/critic_matrix/ppermute | solution.py:32
  103.2 9.7 %collective-permute-start.67 = (bf16[320,64]{0,1:T(8,128)(2,1)S(1)}, bf16[320,64]{0,1:T(8,128)(2,1)S(1)}, u32[]{:S(2)}, u32[]{:S(2)}) collective-permute-start(bf16[320,64]{0,1:T(8,128)(2,1)S(1)} %copy-done.2), channel_id=1, source_target_pairs={{0,1},{1,2},{2,3},{3,0},{4,5},{5,6},{6,7},{7,4},{8,9},{9,10},{10,1... | collective-permute-start | bytes 122888 | tf_op jit(solution)/shard_map/critic_head/ppermute | solution.py:32
  112.9 3.0 collective-permute-start.68
  119.1 2.8 collective-permute-done.53
  121.9 4.0 collective-permute-start.54
  125.9 4.2 collective-permute-done.54
  130.1 4.8 %collective-permute-start.55 = (f32[2,320]{1,0:T(2,128)S(1)}, f32[2,320]{1,0:T(2,128)S(1)}, u32[]{:S(2)}, u32[]{:S(2)}) collective-permute-start(f32[2,320]{1,0:T(2,128)S(1)} %get-tuple-element.5), channel_id=1, source_target_pairs={{0,32},{4,36},{8,40},{12,44},{16,48},{20,52},{24,56},{28,60},{32,0... | collective-permute-start | bytes 7688 | tf_op jit(solution)/shard_map/critic_matrix/ppermute | solution.py:32
  134.9 8.2 %collective-permute-done.55 = f32[2,320]{1,0:T(2,128)S(1)} collective-permute-done((f32[2,320]{1,0:T(2,128)S(1)}, f32[2,320]{1,0:T(2,128)S(1)}, u32[]{:S(2)}, u32[]{:S(2)}) %collective-permute-start.55) | collective-permute-done | bytes 2592 | tf_op jit(solution)/shard_map/critic_matrix/ppermute | solution.py:32
  145.1 6.3 %collective-permute-done.56 = f32[2,320]{1,0:T(2,128)S(1)} collective-permute-done((f32[2,320]{1,0:T(2,128)S(1)}, f32[2,320]{1,0:T(2,128)S(1)}, u32[]{:S(2)}, u32[]{:S(2)}) %collective-permute-start.56) | collective-permute-done | bytes 2592 | tf_op jit(solution)/shard_map/critic_matrix/ppermute | solution.py:32
  153.8 4.1 collective-permute-done.40
  160.3 3.6 collective-permute-done.57
  163.8 8.0 %collective-permute-start.69 = (bf16[320,64]{0,1:T(8,128)(2,1)S(1)}, bf16[320,64]{0,1:T(8,128)(2,1)S(1)}, u32[]{:S(2)}, u32[]{:S(2)}) collective-permute-start(bf16[320,64]{0,1:T(8,128)(2,1)S(1)} %copy-done.2), channel_id=1, source_target_pairs={{0,3},{1,0},{2,1},{3,2},{4,7},{5,4},{6,5},{7,6},{8,11},{9,8},{10,9... | collective-permute-start | bytes 122888 | tf_op jit(solution)/shard_map/critic_head/ppermute | solution.py:32
  171.9 4.6 collective-permute-start.41
  178.6 3.4 collective-permute-start.59
  187.2 3.7 collective-permute-start.60
  190.9 6.9 %collective-permute-start.42 = (bf16[2,4,16,64]{3,2,1,0:T(8,128)(2,1)S(1)}, bf16[2,4,16,64]{3,2,1,0:T(8,128)(2,1)S(1)}, u32[]{:S(2)}, u32[]{:S(2)}) collective-permute-start(bf16[2,4,16,64]{3,2,1,0:T(8,128)(2,1)S(1)} %get-tuple-element.14), channel_id=1, source_target_pairs={{0,32},{4,36},{8,40},{12,44},{16,48},{20,52},{24,56},{28,60},{32,0... | collective-permute-start | bytes 49160 | tf_op jit(solution)/shard_map/fetch_noise/ppermute | solution.py:32
  197.9 6.4 %collective-permute-done.42 = bf16[2,4,16,64]{3,2,1,0:T(8,128)(2,1)S(1)} collective-permute-done((bf16[2,4,16,64]{3,2,1,0:T(8,128)(2,1)S(1)}, bf16[2,4,16,64]{3,2,1,0:T(8,128)(2,1)S(1)}, u32[]{:S(2)}, u32[]{:S(2)}) %collective-permute-start.42) | collective-permute-done | bytes 16416 | tf_op jit(solution)/shard_map/fetch_noise/ppermute | solution.py:32
  204.3 4.6 collective-permute-start.43
  208.9 4.6 collective-permute-done.43
  215.6 4.4 collective-permute-done.44
  222.2 6.7 %collective-permute-start.61 = (f32[64,320]{1,0:T(8,128)S(1)}, f32[64,320]{1,0:T(8,128)S(1)}, u32[]{:S(2)}, u32[]{:S(2)}) collective-permute-start(f32[64,320]{1,0:T(8,128)S(1)} %reshape.71), channel_id=1, source_target_pairs={{0,1},{1,2},{2,3},{3,0},{4,5},{5,6},{6,7},{7,4},{8,9},{9,10},{10,1... | collective-permute-start | bytes 245768 | tf_op jit(solution)/shard_map/critic_matrix/ppermute | solution.py:32
  228.9 2.8 collective-permute-start.62
  234.2 3.3 collective-permute-start.46
  241.9 3.2 collective-permute-start.16
  245.1 3.1 collective-permute-start.70
  248.4 4.3 collective-permute-start.71
  260.5 3.1 collective-permute-start.72
  267.4 3.2 collective-permute-start.65
  275.8 4.0 collective-permute-start.3
  283.1 3.1 collective-permute-start.66
  289.8 4.6 collective-permute-start.18
  299.0 4.6 collective-permute-start.5
  305.5 4.6 collective-permute-start.20
  313.6 4.6 collective-permute-start.7
  320.2 4.6 collective-permute-start.22
  329.9 4.6 collective-permute-start.9
  336.5 4.6 collective-permute-start.24
  344.5 4.6 collective-permute-start.11
  351.1 4.6 collective-permute-start.26
  359.0 4.6 collective-permute-start.13
  365.5 4.6 collective-permute-start.28
  373.4 4.6 collective-permute-start.15
  380.0 4.6 collective-permute-start.30
  403.0 4.6 collective-permute-start.32
  410.3 5.2 %fusion.23 = f32[256,640]{1,0:T(8,128)S(1)} fusion(bf16[5120,640]{1,0:T(8,128)(2,1)} %constant_dynamic-update-slice_fusion.10, bf16[256,5120]{1,0:T(8,128)(2,1)S(1)} %copy-done.1, f32[5120]{0:T(1024)S(1)} %copy-done.4, f32[256]{0:T(256)S(1)} %add_rsqrt_fusion.2), kind=kOutput, calls=%fused_computation.31 | convolution fusion | flops 1682964480 | bytes 9851904 | tf_op jit(solution)/shard_map/forward/dot_general | solution.py:185
  416.4 16.7 %all-gather = bf16[1024,64]{0,1:T(8,128)(2,1)S(1)} all-gather(bf16[256,64]{0,1:T(8,128)(2,1)S(1)} %convolution_convert_fusion.2), channel_id=2, replica_groups=mesh['group'=4,'seq'=32,'tp'=4] {'tp'}, dimensions={0}, use_global_device_ids=true | all-gather | bytes 163840 | tf_op jit(solution)/shard_map/forward/all_gather | solution.py:188
  440.7 3.5 multiply_reduce_fusion
  457.3 3.4 collective-permute-start.76
  465.7 5.5 %collective-permute-done.76 = f32[256]{0:T(256)S(1)} collective-permute-done((f32[256]{0:T(256)S(1)}, f32[256]{0:T(256)S(1)}, u32[]{:S(2)}, u32[]{:S(2)}) %collective-permute-start.76) | collective-permute-done | bytes 1056 | tf_op jit(solution)/shard_map/backward/ppermute | solution.py:32
  473.8 3.4 fusion.32
  (261 shorter events, 159.0 us)
Async XLA Ops:
  0.6 272.7 %collective-permute-start = (bf16[160,640]{1,0:T(8,128)(2,1)}, bf16[160,640]{1,0:T(8,128)(2,1)}, u32[]{:S(2)}, u32[]{:S(2)}) collective-permute-start(bf16[160,640]{1,0:T(8,128)(2,1)} %param.15), channel_id=1, source_target_pairs={{0,4},{4,8},{8,12},{12,16},{16,20},{20,24},{24,28},{28,32},{32,36}... | collective-permute-start | bytes 614408 | tf_op jit(solution)/shard_map/gather_value/ppermute | solution.py:32
  5.2 270.7 %collective-permute-start.1 = (bf16[160,640]{1,0:T(8,128)(2,1)}, bf16[160,640]{1,0:T(8,128)(2,1)}, u32[]{:S(2)}, u32[]{:S(2)}) collective-permute-start(bf16[160,640]{1,0:T(8,128)(2,1)} %param.15), channel_id=1, source_target_pairs={{0,60},{4,0},{8,4},{12,8},{16,12},{20,16},{24,20},{28,24},{32,28},... | collective-permute-start | bytes 614408 | tf_op jit(solution)/shard_map/gather_value/ppermute | solution.py:32
  15.9 24.8 %collective-permute-start.33 = (s32[2,4,16]{2,1,0:T(4,128)S(1)}, s32[2,4,16]{2,1,0:T(4,128)S(1)}, u32[]{:S(2)}, u32[]{:S(2)}) collective-permute-start(s32[2,4,16]{2,1,0:T(4,128)S(1)} %bitcast.214), channel_id=1, source_target_pairs={{0,4},{4,8},{8,12},{12,0},{16,20},{20,24},{24,28},{28,16},{32,36},... | collective-permute-start | bytes 1544 | tf_op jit(solution)/shard_map/fetch_noise/ppermute | solution.py:32
  17.8 25.1 %collective-permute-start.34 = (s32[2,4,16]{2,1,0:T(4,128)S(1)}, s32[2,4,16]{2,1,0:T(4,128)S(1)}, u32[]{:S(2)}, u32[]{:S(2)}) collective-permute-start(s32[2,4,16]{2,1,0:T(4,128)S(1)} %bitcast.213), channel_id=1, source_target_pairs={{0,8},{4,12},{8,0},{12,4},{16,24},{20,28},{24,16},{28,20},{32,40},... | collective-permute-start | bytes 1544 | tf_op jit(solution)/shard_map/fetch_noise/ppermute | solution.py:32
  19.8 26.3 %collective-permute-start.35 = (s32[2,4,16]{2,1,0:T(4,128)S(1)}, s32[2,4,16]{2,1,0:T(4,128)S(1)}, u32[]{:S(2)}, u32[]{:S(2)}) collective-permute-start(s32[2,4,16]{2,1,0:T(4,128)S(1)} %bitcast.212), channel_id=1, source_target_pairs={{0,12},{4,0},{8,4},{12,8},{16,28},{20,16},{24,20},{28,24},{32,44},... | collective-permute-start | bytes 1544 | tf_op jit(solution)/shard_map/fetch_noise/ppermute | solution.py:32
  40.7 39.5 %collective-permute-start.47 = (f32[4,2,2,320]{3,0,2,1:T(4,128)S(1)}, f32[4,2,2,320]{3,0,2,1:T(4,128)S(1)}, u32[]{:S(2)}, u32[]{:S(2)}) collective-permute-start(f32[4,2,2,320]{3,0,2,1:T(4,128)S(1)} %get-tuple-element.16), channel_id=1, source_target_pairs={{0,4},{4,8},{8,12},{12,0},{16,20},{20,24},{24,28},{28,16},{32,36},... | collective-permute-start | bytes 61448 | tf_op jit(solution)/shard_map/critic_matrix/ppermute | solution.py:32
  42.9 42.1 %collective-permute-start.48 = (f32[4,2,2,320]{3,0,2,1:T(4,128)S(1)}, f32[4,2,2,320]{3,0,2,1:T(4,128)S(1)}, u32[]{:S(2)}, u32[]{:S(2)}) collective-permute-start(f32[4,2,2,320]{3,0,2,1:T(4,128)S(1)} %get-tuple-element.18), channel_id=1, source_target_pairs={{0,8},{4,12},{8,0},{12,4},{16,24},{20,28},{24,16},{28,20},{32,40},... | collective-permute-start | bytes 61448 | tf_op jit(solution)/shard_map/critic_matrix/ppermute | solution.py:32
  54.4 13.3 %collective-permute-start.37 = (s32[2,4,16]{2,1,0:T(4,128)S(1)}, s32[2,4,16]{2,1,0:T(4,128)S(1)}, u32[]{:S(2)}, u32[]{:S(2)}) collective-permute-start(s32[2,4,16]{2,1,0:T(4,128)S(1)} %get-tuple-element.24), channel_id=1, source_target_pairs={{0,32},{4,36},{8,40},{12,44},{16,48},{20,52},{24,56},{28,60},{32,0... | collective-permute-start | bytes 1544 | tf_op jit(solution)/shard_map/fetch_noise/ppermute | solution.py:32
  80.2 17.7 %collective-permute-start.39 = (s32[4,4,16]{2,1,0:T(4,128)S(1)}, s32[4,4,16]{2,1,0:T(4,128)S(1)}, u32[]{:S(2)}, u32[]{:S(2)}) collective-permute-start(s32[4,4,16]{2,1,0:T(4,128)S(1)} %fusion.84), channel_id=1, source_target_pairs={{0,64},{4,68},{8,72},{12,76},{16,80},{20,84},{24,88},{28,92},{32,9... | collective-permute-start | bytes 3080 | tf_op jit(solution)/shard_map/fetch_noise/ppermute | solution.py:32
  85.1 18.1 %collective-permute-start.50 = (f32[2,2,320]{2,1,0:T(2,128)S(1)}, f32[2,2,320]{2,1,0:T(2,128)S(1)}, u32[]{:S(2)}, u32[]{:S(2)}) collective-permute-start(f32[2,2,320]{2,1,0:T(2,128)S(1)} %bitcast.210), channel_id=1, source_target_pairs={{0,16},{4,20},{8,24},{12,28},{16,32},{20,36},{24,40},{28,44},{32,4... | collective-permute-start | bytes 15368 | tf_op jit(solution)/shard_map/critic_matrix/ppermute | solution.py:32
  89.2 23.7 %collective-permute-start.51 = (f32[2,2,320]{2,1,0:T(2,128)S(1)}, f32[2,2,320]{2,1,0:T(2,128)S(1)}, u32[]{:S(2)}, u32[]{:S(2)}) collective-permute-start(f32[2,2,320]{2,1,0:T(2,128)S(1)} %bitcast.209), channel_id=1, source_target_pairs={{0,32},{4,36},{8,40},{12,44},{16,48},{20,52},{24,56},{28,60},{32,0... | collective-permute-start | bytes 15368 | tf_op jit(solution)/shard_map/critic_matrix/ppermute | solution.py:32
  97.9 18.0 %collective-permute-start.52 = (f32[2,2,320]{2,1,0:T(2,128)S(1)}, f32[2,2,320]{2,1,0:T(2,128)S(1)}, u32[]{:S(2)}, u32[]{:S(2)}) collective-permute-start(f32[2,2,320]{2,1,0:T(2,128)S(1)} %bitcast.208), channel_id=1, source_target_pairs={{0,48},{4,52},{8,56},{12,60},{16,0},{20,4},{24,8},{28,12},{32,16},... | collective-permute-start | bytes 15368 | tf_op jit(solution)/shard_map/critic_matrix/ppermute | solution.py:32
  103.2 68.7 %collective-permute-start.67 = (bf16[320,64]{0,1:T(8,128)(2,1)S(1)}, bf16[320,64]{0,1:T(8,128)(2,1)S(1)}, u32[]{:S(2)}, u32[]{:S(2)}) collective-permute-start(bf16[320,64]{0,1:T(8,128)(2,1)S(1)} %copy-done.2), channel_id=1, source_target_pairs={{0,1},{1,2},{2,3},{3,0},{4,5},{5,6},{6,7},{7,4},{8,9},{9,10},{10,1... | collective-permute-start | bytes 122888 | tf_op jit(solution)/shard_map/critic_head/ppermute | solution.py:32
  112.9 63.7 %collective-permute-start.68 = (bf16[320,64]{0,1:T(8,128)(2,1)S(1)}, bf16[320,64]{0,1:T(8,128)(2,1)S(1)}, u32[]{:S(2)}, u32[]{:S(2)}) collective-permute-start(bf16[320,64]{0,1:T(8,128)(2,1)S(1)} %copy-done.2), channel_id=1, source_target_pairs={{0,2},{1,3},{2,0},{3,1},{4,6},{5,7},{6,4},{7,5},{8,10},{9,11},{10,... | collective-permute-start | bytes 122888 | tf_op jit(solution)/shard_map/critic_head/ppermute | solution.py:32
  130.1 13.0 %collective-permute-start.55 = (f32[2,320]{1,0:T(2,128)S(1)}, f32[2,320]{1,0:T(2,128)S(1)}, u32[]{:S(2)}, u32[]{:S(2)}) collective-permute-start(f32[2,320]{1,0:T(2,128)S(1)} %get-tuple-element.5), channel_id=1, source_target_pairs={{0,32},{4,36},{8,40},{12,44},{16,48},{20,52},{24,56},{28,60},{32,0... | collective-permute-start | bytes 7688 | tf_op jit(solution)/shard_map/critic_matrix/ppermute | solution.py:32
  163.8 14.8 %collective-permute-start.69 = (bf16[320,64]{0,1:T(8,128)(2,1)S(1)}, bf16[320,64]{0,1:T(8,128)(2,1)S(1)}, u32[]{:S(2)}, u32[]{:S(2)}) collective-permute-start(bf16[320,64]{0,1:T(8,128)(2,1)S(1)} %copy-done.2), channel_id=1, source_target_pairs={{0,3},{1,0},{2,1},{3,2},{4,7},{5,4},{6,5},{7,6},{8,11},{9,8},{10,9... | collective-permute-start | bytes 122888 | tf_op jit(solution)/shard_map/critic_head/ppermute | solution.py:32
  171.9 15.2 %collective-permute-start.41 = (bf16[2,4,16,64]{3,2,1,0:T(8,128)(2,1)S(1)}, bf16[2,4,16,64]{3,2,1,0:T(8,128)(2,1)S(1)}, u32[]{:S(2)}, u32[]{:S(2)}) collective-permute-start(bf16[2,4,16,64]{3,2,1,0:T(8,128)(2,1)S(1)} %dynamic-slice_bitcast_fusion.6), channel_id=1, source_target_pairs={{0,16},{4,20},{8,24},{12,28},{16,32},{20,36},{24,40},{28,44},{32,4... | collective-permute-start | bytes 49160 | tf_op jit(solution)/shard_map/fetch_noise/ppermute | solution.py:32
  176.6 14.3 %collective-permute-start.58 = (f32[2,4,2,320]{3,2,0,1:T(2,128)S(1)}, f32[2,4,2,320]{3,2,0,1:T(2,128)S(1)}, u32[]{:S(2)}, u32[]{:S(2)}) collective-permute-start(f32[2,4,2,320]{3,2,0,1:T(2,128)S(1)} %constant_dynamic-update-slice_fusion), channel_id=1, source_target_pairs={{0,4},{4,8},{8,12},{12,0},{16,20},{20,24},{24,28},{28,16},{32,36},... | collective-permute-start | bytes 61448 | tf_op jit(solution)/shard_map/critic_matrix/ppermute | solution.py:32
  178.6 36.9 %collective-permute-start.59 = (f32[2,4,2,320]{3,2,0,1:T(2,128)S(1)}, f32[2,4,2,320]{3,2,0,1:T(2,128)S(1)}, u32[]{:S(2)}, u32[]{:S(2)}) collective-permute-start(f32[2,4,2,320]{3,2,0,1:T(2,128)S(1)} %constant_dynamic-update-slice_fusion), channel_id=1, source_target_pairs={{0,8},{4,12},{8,0},{12,4},{16,24},{20,28},{24,16},{28,20},{32,40},... | collective-permute-start | bytes 61448 | tf_op jit(solution)/shard_map/critic_matrix/ppermute | solution.py:32
  187.2 34.8 %collective-permute-start.60 = (f32[2,4,2,320]{3,2,0,1:T(2,128)S(1)}, f32[2,4,2,320]{3,2,0,1:T(2,128)S(1)}, u32[]{:S(2)}, u32[]{:S(2)}) collective-permute-start(f32[2,4,2,320]{3,2,0,1:T(2,128)S(1)} %constant_dynamic-update-slice_fusion), channel_id=1, source_target_pairs={{0,12},{4,0},{8,4},{12,8},{16,28},{20,16},{24,20},{28,24},{32,44},... | collective-permute-start | bytes 61448 | tf_op jit(solution)/shard_map/critic_matrix/ppermute | solution.py:32
  190.9 13.4 %collective-permute-start.42 = (bf16[2,4,16,64]{3,2,1,0:T(8,128)(2,1)S(1)}, bf16[2,4,16,64]{3,2,1,0:T(8,128)(2,1)S(1)}, u32[]{:S(2)}, u32[]{:S(2)}) collective-permute-start(bf16[2,4,16,64]{3,2,1,0:T(8,128)(2,1)S(1)} %get-tuple-element.14), channel_id=1, source_target_pairs={{0,32},{4,36},{8,40},{12,44},{16,48},{20,52},{24,56},{28,60},{32,0... | collective-permute-start | bytes 49160 | tf_op jit(solution)/shard_map/fetch_noise/ppermute | solution.py:32
  204.3 9.3 %collective-permute-start.43 = (bf16[2,4,16,64]{3,2,1,0:T(8,128)(2,1)S(1)}, bf16[2,4,16,64]{3,2,1,0:T(8,128)(2,1)S(1)}, u32[]{:S(2)}, u32[]{:S(2)}) collective-permute-start(bf16[2,4,16,64]{3,2,1,0:T(8,128)(2,1)S(1)} %get-tuple-element.13), channel_id=1, source_target_pairs={{0,48},{4,52},{8,56},{12,60},{16,0},{20,4},{24,8},{28,12},{32,16},... | collective-permute-start | bytes 49160 | tf_op jit(solution)/shard_map/fetch_noise/ppermute | solution.py:32
  220.0 14.2 %collective-permute-start.45 = (bf16[2,4,16,64]{3,2,1,0:T(8,128)(2,1)S(1)}, bf16[2,4,16,64]{3,2,1,0:T(8,128)(2,1)S(1)}, u32[]{:S(2)}, u32[]{:S(2)}) collective-permute-start(bf16[2,4,16,64]{3,2,1,0:T(8,128)(2,1)S(1)} %get-tuple-element.11), channel_id=1, source_target_pairs={{0,8},{4,12},{8,0},{12,4},{16,24},{20,28},{24,16},{28,20},{32,40},... | collective-permute-start | bytes 49160 | tf_op jit(solution)/shard_map/fetch_noise/ppermute | solution.py:32
  222.2 19.6 %collective-permute-start.61 = (f32[64,320]{1,0:T(8,128)S(1)}, f32[64,320]{1,0:T(8,128)S(1)}, u32[]{:S(2)}, u32[]{:S(2)}) collective-permute-start(f32[64,320]{1,0:T(8,128)S(1)} %reshape.71), channel_id=1, source_target_pairs={{0,1},{1,2},{2,3},{3,0},{4,5},{5,6},{6,7},{7,4},{8,9},{9,10},{10,1... | collective-permute-start | bytes 245768 | tf_op jit(solution)/shard_map/critic_matrix/ppermute | solution.py:32
  228.9 16.2 %collective-permute-start.62 = (f32[64,320]{1,0:T(8,128)S(1)}, f32[64,320]{1,0:T(8,128)S(1)}, u32[]{:S(2)}, u32[]{:S(2)}) collective-permute-start(f32[64,320]{1,0:T(8,128)S(1)} %reshape.71), channel_id=1, source_target_pairs={{0,2},{1,3},{2,0},{3,1},{4,6},{5,7},{6,4},{7,5},{8,10},{9,11},{10,... | collective-permute-start | bytes 245768 | tf_op jit(solution)/shard_map/critic_matrix/ppermute | solution.py:32
  241.9 41.2 %collective-permute-start.16 = (bf16[160,640]{1,0:T(8,128)(2,1)}, bf16[160,640]{1,0:T(8,128)(2,1)}, u32[]{:S(2)}, u32[]{:S(2)}) collective-permute-start(bf16[160,640]{1,0:T(8,128)(2,1)} %param.15), channel_id=1, source_target_pairs={{0,64},{4,68},{8,72},{12,76},{16,80},{20,84},{24,88},{28,92},{32,9... | collective-permute-start | bytes 614408 | tf_op jit(solution)/shard_map/gather_value/ppermute | solution.py:32
  245.1 15.4 %collective-permute-start.70 = (bf16[4,320,64]{1,0,2:T(4,128)(2,1)S(1)}, bf16[4,320,64]{1,0,2:T(4,128)(2,1)S(1)}, u32[]{:S(2)}, u32[]{:S(2)}) collective-permute-start(bf16[4,320,64]{1,0,2:T(4,128)(2,1)S(1)} %dynamic_update_slice.304), channel_id=1, source_target_pairs={{0,128},{128,256},{256,384},{384,0},{1,129},{129,257},{257,385},{3... | collective-permute-start | bytes 491528 | tf_op jit(solution)/shard_map/critic_head/ppermute | solution.py:32
  248.4 15.3 %collective-permute-start.71 = (bf16[4,320,64]{1,0,2:T(4,128)(2,1)S(1)}, bf16[4,320,64]{1,0,2:T(4,128)(2,1)}, u32[]{:S(2)}, u32[]{:S(2)}) collective-permute-start(bf16[4,320,64]{1,0,2:T(4,128)(2,1)S(1)} %dynamic_update_slice.304), channel_id=1, source_target_pairs={{0,256},{128,384},{256,0},{384,128},{1,257},{129,385},{257,1},{385... | collective-permute-start | bytes 491528 | tf_op jit(solution)/shard_map/critic_head/ppermute | solution.py:32
  263.7 32.3 %collective-permute-start.64 = (f32[4,64,320]{2,0,1:T(4,128)S(1)}, f32[4,64,320]{2,0,1:T(4,128)}, u32[]{:S(2)}, u32[]{:S(2)}) collective-permute-start(f32[4,64,320]{2,0,1:T(4,128)S(1)} %dynamic_update_slice.296), channel_id=1, source_target_pairs={{0,128},{128,256},{256,384},{384,0},{1,129},{129,257},{257,385},{3... | collective-permute-start | bytes 983048 | tf_op jit(solution)/shard_map/critic_matrix/ppermute | solution.py:32
  267.4 38.1 %collective-permute-start.65 = (f32[4,64,320]{2,0,1:T(4,128)S(1)}, f32[4,64,320]{2,0,1:T(4,128)S(1)}, u32[]{:S(2)}, u32[]{:S(2)}) collective-permute-start(f32[4,64,320]{2,0,1:T(4,128)S(1)} %dynamic_update_slice.296), channel_id=1, source_target_pairs={{0,256},{128,384},{256,0},{384,128},{1,257},{129,385},{257,1},{385... | collective-permute-start | bytes 983048 | tf_op jit(solution)/shard_map/critic_matrix/ppermute | solution.py:32
  273.3 12.9 %collective-permute-start.2 = (bf16[160,640]{1,0:T(8,128)(2,1)}, bf16[160,640]{1,0:T(8,128)(2,1)}, u32[]{:S(2)}, u32[]{:S(2)}) collective-permute-start(bf16[160,640]{1,0:T(8,128)(2,1)} %collective-permute-done), channel_id=1, source_target_pairs={{0,4},{4,8},{8,12},{12,16},{16,20},{20,24},{24,28},{28,32},{32,36}... | collective-permute-start | bytes 614408 | tf_op jit(solution)/shard_map/gather_value/ppermute | solution.py:32
  275.8 13.9 %collective-permute-start.3 = (bf16[160,640]{1,0:T(8,128)(2,1)}, bf16[160,640]{1,0:T(8,128)(2,1)}, u32[]{:S(2)}, u32[]{:S(2)}) collective-permute-start(bf16[160,640]{1,0:T(8,128)(2,1)} %collective-permute-done.1), channel_id=1, source_target_pairs={{0,60},{4,0},{8,4},{12,8},{16,12},{20,16},{24,20},{28,24},{32,28},... | collective-permute-start | bytes 614408 | tf_op jit(solution)/shard_map/gather_value/ppermute | solution.py:32
  283.1 27.1 %collective-permute-start.66 = (f32[4,64,320]{2,0,1:T(4,128)S(1)}, f32[4,64,320]{2,0,1:T(4,128)S(1)}, u32[]{:S(2)}, u32[]{:S(2)}) collective-permute-start(f32[4,64,320]{2,0,1:T(4,128)S(1)} %dynamic_update_slice.296), channel_id=1, source_target_pairs={{0,384},{128,0},{256,128},{384,256},{1,385},{129,1},{257,129},{385... | collective-permute-start | bytes 983048 | tf_op jit(solution)/shard_map/critic_matrix/ppermute | solution.py:32
  286.2 12.8 %collective-permute-start.17 = (bf16[160,640]{1,0:T(8,128)(2,1)}, bf16[160,640]{1,0:T(8,128)(2,1)}, u32[]{:S(2)}, u32[]{:S(2)}) collective-permute-start(bf16[160,640]{1,0:T(8,128)(2,1)} %collective-permute-done.16), channel_id=1, source_target_pairs={{0,4},{4,8},{8,12},{12,16},{16,20},{20,24},{24,28},{28,32},{32,36}... | collective-permute-start | bytes 614408 | tf_op jit(solution)/shard_map/gather_value/ppermute | solution.py:32
  289.8 13.8 %collective-permute-start.18 = (bf16[160,640]{1,0:T(8,128)(2,1)}, bf16[160,640]{1,0:T(8,128)(2,1)}, u32[]{:S(2)}, u32[]{:S(2)}) collective-permute-start(bf16[160,640]{1,0:T(8,128)(2,1)} %collective-permute-done.16), channel_id=1, source_target_pairs={{0,60},{4,0},{8,4},{12,8},{16,12},{20,16},{24,20},{28,24},{32,28},... | collective-permute-start | bytes 614408 | tf_op jit(solution)/shard_map/gather_value/ppermute | solution.py:32
  296.0 15.7 %collective-permute-start.4 = (bf16[160,640]{1,0:T(8,128)(2,1)}, bf16[160,640]{1,0:T(8,128)(2,1)}, u32[]{:S(2)}, u32[]{:S(2)}) collective-permute-start(bf16[160,640]{1,0:T(8,128)(2,1)} %collective-permute-done.2), channel_id=1, source_target_pairs={{0,4},{4,8},{8,12},{12,16},{16,20},{20,24},{24,28},{28,32},{32,36}... | collective-permute-start | bytes 614408 | tf_op jit(solution)/shard_map/gather_value/ppermute | solution.py:32
  299.0 14.6 %collective-permute-start.5 = (bf16[160,640]{1,0:T(8,128)(2,1)}, bf16[160,640]{1,0:T(8,128)(2,1)}, u32[]{:S(2)}, u32[]{:S(2)}) collective-permute-start(bf16[160,640]{1,0:T(8,128)(2,1)} %collective-permute-done.3), channel_id=1, source_target_pairs={{0,60},{4,0},{8,4},{12,8},{16,12},{20,16},{24,20},{28,24},{32,28},... | collective-permute-start | bytes 614408 | tf_op jit(solution)/shard_map/gather_value/ppermute | solution.py:32
  303.6 14.6 %collective-permute-start.19 = (bf16[160,640]{1,0:T(8,128)(2,1)}, bf16[160,640]{1,0:T(8,128)(2,1)}, u32[]{:S(2)}, u32[]{:S(2)}) collective-permute-start(bf16[160,640]{1,0:T(8,128)(2,1)} %collective-permute-done.17), channel_id=1, source_target_pairs={{0,4},{4,8},{8,12},{12,16},{16,20},{20,24},{24,28},{28,32},{32,36}... | collective-permute-start | bytes 614408 | tf_op jit(solution)/shard_map/gather_value/ppermute | solution.py:32
  305.5 14.6 %collective-permute-start.20 = (bf16[160,640]{1,0:T(8,128)(2,1)}, bf16[160,640]{1,0:T(8,128)(2,1)}, u32[]{:S(2)}, u32[]{:S(2)}) collective-permute-start(bf16[160,640]{1,0:T(8,128)(2,1)} %collective-permute-done.18), channel_id=1, source_target_pairs={{0,60},{4,0},{8,4},{12,8},{16,12},{20,16},{24,20},{28,24},{32,28},... | collective-permute-start | bytes 614408 | tf_op jit(solution)/shard_map/gather_value/ppermute | solution.py:32
  311.7 16.3 %collective-permute-start.6 = (bf16[160,640]{1,0:T(8,128)(2,1)}, bf16[160,640]{1,0:T(8,128)(2,1)S(1)}, u32[]{:S(2)}, u32[]{:S(2)}) collective-permute-start(bf16[160,640]{1,0:T(8,128)(2,1)} %collective-permute-done.4), channel_id=1, source_target_pairs={{0,4},{4,8},{8,12},{12,16},{16,20},{20,24},{24,28},{28,32},{32,36}... | collective-permute-start | bytes 614408 | tf_op jit(solution)/shard_map/gather_value/ppermute | solution.py:32
  313.6 16.3 %collective-permute-start.7 = (bf16[160,640]{1,0:T(8,128)(2,1)}, bf16[160,640]{1,0:T(8,128)(2,1)S(1)}, u32[]{:S(2)}, u32[]{:S(2)}) collective-permute-start(bf16[160,640]{1,0:T(8,128)(2,1)} %collective-permute-done.5), channel_id=1, source_target_pairs={{0,60},{4,0},{8,4},{12,8},{16,12},{20,16},{24,20},{28,24},{32,28},... | collective-permute-start | bytes 614408 | tf_op jit(solution)/shard_map/gather_value/ppermute | solution.py:32
  318.2 16.3 %collective-permute-start.21 = (bf16[160,640]{1,0:T(8,128)(2,1)}, bf16[160,640]{1,0:T(8,128)(2,1)S(1)}, u32[]{:S(2)}, u32[]{:S(2)}) collective-permute-start(bf16[160,640]{1,0:T(8,128)(2,1)} %collective-permute-done.19), channel_id=1, source_target_pairs={{0,4},{4,8},{8,12},{12,16},{16,20},{20,24},{24,28},{28,32},{32,36}... | collective-permute-start | bytes 614408 | tf_op jit(solution)/shard_map/gather_value/ppermute | solution.py:32
  320.2 16.3 %collective-permute-start.22 = (bf16[160,640]{1,0:T(8,128)(2,1)}, bf16[160,640]{1,0:T(8,128)(2,1)S(1)}, u32[]{:S(2)}, u32[]{:S(2)}) collective-permute-start(bf16[160,640]{1,0:T(8,128)(2,1)} %collective-permute-done.20), channel_id=1, source_target_pairs={{0,60},{4,0},{8,4},{12,8},{16,12},{20,16},{24,20},{28,24},{32,28},... | collective-permute-start | bytes 614408 | tf_op jit(solution)/shard_map/gather_value/ppermute | solution.py:32
  328.0 14.5 %collective-permute-start.8 = (bf16[160,640]{1,0:T(8,128)(2,1)S(1)}, bf16[160,640]{1,0:T(8,128)(2,1)S(1)}, u32[]{:S(2)}, u32[]{:S(2)}) collective-permute-start(bf16[160,640]{1,0:T(8,128)(2,1)S(1)} %collective-permute-done.6), channel_id=1, source_target_pairs={{0,4},{4,8},{8,12},{12,16},{16,20},{20,24},{24,28},{28,32},{32,36}... | collective-permute-start | bytes 614408 | tf_op jit(solution)/shard_map/gather_value/ppermute | solution.py:32
  329.9 14.6 %collective-permute-start.9 = (bf16[160,640]{1,0:T(8,128)(2,1)S(1)}, bf16[160,640]{1,0:T(8,128)(2,1)S(1)}, u32[]{:S(2)}, u32[]{:S(2)}) collective-permute-start(bf16[160,640]{1,0:T(8,128)(2,1)S(1)} %collective-permute-done.7), channel_id=1, source_target_pairs={{0,60},{4,0},{8,4},{12,8},{16,12},{20,16},{24,20},{28,24},{32,28},... | collective-permute-start | bytes 614408 | tf_op jit(solution)/shard_map/gather_value/ppermute | solution.py:32
  334.5 14.6 %collective-permute-start.23 = (bf16[160,640]{1,0:T(8,128)(2,1)S(1)}, bf16[160,640]{1,0:T(8,128)(2,1)S(1)}, u32[]{:S(2)}, u32[]{:S(2)}) collective-permute-start(bf16[160,640]{1,0:T(8,128)(2,1)S(1)} %collective-permute-done.21), channel_id=1, source_target_pairs={{0,4},{4,8},{8,12},{12,16},{16,20},{20,24},{24,28},{28,32},{32,36}... | collective-permute-start | bytes 614408 | tf_op jit(solution)/shard_map/gather_value/ppermute | solution.py:32
  336.5 14.6 %collective-permute-start.24 = (bf16[160,640]{1,0:T(8,128)(2,1)S(1)}, bf16[160,640]{1,0:T(8,128)(2,1)S(1)}, u32[]{:S(2)}, u32[]{:S(2)}) collective-permute-start(bf16[160,640]{1,0:T(8,128)(2,1)S(1)} %collective-permute-done.22), channel_id=1, source_target_pairs={{0,60},{4,0},{8,4},{12,8},{16,12},{20,16},{24,20},{28,24},{32,28},... | collective-permute-start | bytes 614408 | tf_op jit(solution)/shard_map/gather_value/ppermute | solution.py:32
  342.5 14.6 %collective-permute-start.10 = (bf16[160,640]{1,0:T(8,128)(2,1)S(1)}, bf16[160,640]{1,0:T(8,128)(2,1)S(1)}, u32[]{:S(2)}, u32[]{:S(2)}) collective-permute-start(bf16[160,640]{1,0:T(8,128)(2,1)S(1)} %collective-permute-done.8), channel_id=1, source_target_pairs={{0,4},{4,8},{8,12},{12,16},{16,20},{20,24},{24,28},{28,32},{32,36}... | collective-permute-start | bytes 614408 | tf_op jit(solution)/shard_map/gather_value/ppermute | solution.py:32
  344.5 14.4 %collective-permute-start.11 = (bf16[160,640]{1,0:T(8,128)(2,1)S(1)}, bf16[160,640]{1,0:T(8,128)(2,1)S(1)}, u32[]{:S(2)}, u32[]{:S(2)}) collective-permute-start(bf16[160,640]{1,0:T(8,128)(2,1)S(1)} %collective-permute-done.9), channel_id=1, source_target_pairs={{0,60},{4,0},{8,4},{12,8},{16,12},{20,16},{24,20},{28,24},{32,28},... | collective-permute-start | bytes 614408 | tf_op jit(solution)/shard_map/gather_value/ppermute | solution.py:32
  349.1 14.4 %collective-permute-start.25 = (bf16[160,640]{1,0:T(8,128)(2,1)S(1)}, bf16[160,640]{1,0:T(8,128)(2,1)S(1)}, u32[]{:S(2)}, u32[]{:S(2)}) collective-permute-start(bf16[160,640]{1,0:T(8,128)(2,1)S(1)} %collective-permute-done.23), channel_id=1, source_target_pairs={{0,4},{4,8},{8,12},{12,16},{16,20},{20,24},{24,28},{28,32},{32,36}... | collective-permute-start | bytes 614408 | tf_op jit(solution)/shard_map/gather_value/ppermute | solution.py:32
  351.1 14.4 %collective-permute-start.26 = (bf16[160,640]{1,0:T(8,128)(2,1)S(1)}, bf16[160,640]{1,0:T(8,128)(2,1)S(1)}, u32[]{:S(2)}, u32[]{:S(2)}) collective-permute-start(bf16[160,640]{1,0:T(8,128)(2,1)S(1)} %collective-permute-done.24), channel_id=1, source_target_pairs={{0,60},{4,0},{8,4},{12,8},{16,12},{20,16},{24,20},{28,24},{32,28},... | collective-permute-start | bytes 614408 | tf_op jit(solution)/shard_map/gather_value/ppermute | solution.py:32
  357.0 14.4 %collective-permute-start.12 = (bf16[160,640]{1,0:T(8,128)(2,1)S(1)}, bf16[160,640]{1,0:T(8,128)(2,1)S(1)}, u32[]{:S(2)}, u32[]{:S(2)}) collective-permute-start(bf16[160,640]{1,0:T(8,128)(2,1)S(1)} %collective-permute-done.10), channel_id=1, source_target_pairs={{0,4},{4,8},{8,12},{12,16},{16,20},{20,24},{24,28},{28,32},{32,36}... | collective-permute-start | bytes 614408 | tf_op jit(solution)/shard_map/gather_value/ppermute | solution.py:32
  359.0 14.5 %collective-permute-start.13 = (bf16[160,640]{1,0:T(8,128)(2,1)S(1)}, bf16[160,640]{1,0:T(8,128)(2,1)S(1)}, u32[]{:S(2)}, u32[]{:S(2)}) collective-permute-start(bf16[160,640]{1,0:T(8,128)(2,1)S(1)} %collective-permute-done.11), channel_id=1, source_target_pairs={{0,60},{4,0},{8,4},{12,8},{16,12},{20,16},{24,20},{28,24},{32,28},... | collective-permute-start | bytes 614408 | tf_op jit(solution)/shard_map/gather_value/ppermute | solution.py:32
  363.5 14.5 %collective-permute-start.27 = (bf16[160,640]{1,0:T(8,128)(2,1)S(1)}, bf16[160,640]{1,0:T(8,128)(2,1)S(1)}, u32[]{:S(2)}, u32[]{:S(2)}) collective-permute-start(bf16[160,640]{1,0:T(8,128)(2,1)S(1)} %collective-permute-done.25), channel_id=1, source_target_pairs={{0,4},{4,8},{8,12},{12,16},{16,20},{20,24},{24,28},{28,32},{32,36}... | collective-permute-start | bytes 614408 | tf_op jit(solution)/shard_map/gather_value/ppermute | solution.py:32
  365.5 14.5 %collective-permute-start.28 = (bf16[160,640]{1,0:T(8,128)(2,1)S(1)}, bf16[160,640]{1,0:T(8,128)(2,1)S(1)}, u32[]{:S(2)}, u32[]{:S(2)}) collective-permute-start(bf16[160,640]{1,0:T(8,128)(2,1)S(1)} %collective-permute-done.26), channel_id=1, source_target_pairs={{0,60},{4,0},{8,4},{12,8},{16,12},{20,16},{24,20},{28,24},{32,28},... | collective-permute-start | bytes 614408 | tf_op jit(solution)/shard_map/gather_value/ppermute | solution.py:32
  371.5 14.5 %collective-permute-start.14 = (bf16[80,640]{1,0:T(8,128)(2,1)S(1)}, bf16[80,640]{1,0:T(8,128)(2,1)S(1)}, u32[]{:S(2)}, u32[]{:S(2)}) collective-permute-start(bf16[80,640]{1,0:T(8,128)(2,1)S(1)} %slice.40), channel_id=1, source_target_pairs={{0,4},{4,8},{8,12},{12,16},{16,20},{20,24},{24,28},{28,32},{32,36}... | collective-permute-start | bytes 307208 | tf_op jit(solution)/shard_map/gather_value/ppermute | solution.py:32
  373.4 13.2 %collective-permute-start.15 = (bf16[80,640]{1,0:T(8,128)(2,1)S(1)}, bf16[80,640]{1,0:T(8,128)(2,1)S(1)}, u32[]{:S(2)}, u32[]{:S(2)}) collective-permute-start(bf16[80,640]{1,0:T(8,128)(2,1)S(1)} %slice.41), channel_id=1, source_target_pairs={{0,60},{4,0},{8,4},{12,8},{16,12},{20,16},{24,20},{28,24},{32,28},... | collective-permute-start | bytes 307208 | tf_op jit(solution)/shard_map/gather_value/ppermute | solution.py:32
  378.0 23.0 %collective-permute-start.29 = (bf16[160,640]{1,0:T(8,128)(2,1)S(1)}, bf16[160,640]{1,0:T(8,128)(2,1)S(1)}, u32[]{:S(2)}, u32[]{:S(2)}) collective-permute-start(bf16[160,640]{1,0:T(8,128)(2,1)S(1)} %collective-permute-done.27), channel_id=1, source_target_pairs={{0,4},{4,8},{8,12},{12,16},{16,20},{20,24},{24,28},{28,32},{32,36}... | collective-permute-start | bytes 614408 | tf_op jit(solution)/shard_map/gather_value/ppermute | solution.py:32
  380.0 23.0 %collective-permute-start.30 = (bf16[160,640]{1,0:T(8,128)(2,1)S(1)}, bf16[160,640]{1,0:T(8,128)(2,1)S(1)}, u32[]{:S(2)}, u32[]{:S(2)}) collective-permute-start(bf16[160,640]{1,0:T(8,128)(2,1)S(1)} %collective-permute-done.28), channel_id=1, source_target_pairs={{0,60},{4,0},{8,4},{12,8},{16,12},{20,16},{24,20},{28,24},{32,28},... | collective-permute-start | bytes 614408 | tf_op jit(solution)/shard_map/gather_value/ppermute | solution.py:32
  450.6 23.2 %collective-permute-start.73 = (bf16[256,1280]{1,0:T(8,128)(2,1)S(1)}, bf16[256,1280]{1,0:T(8,128)(2,1)S(1)}, u32[]{:S(2)}, u32[]{:S(2)}) collective-permute-start(bf16[256,1280]{1,0:T(8,128)(2,1)S(1)} %convolution_convert_fusion.1), channel_id=1, source_target_pairs={{0,1},{1,0},{2,3},{3,2},{4,5},{5,4},{6,7},{7,6},{8,9},{9,8},{10,11... | collective-permute-start | bytes 1966088 | tf_op jit(solution)/shard_map/backward/ppermute | solution.py:32
  455.0 18.8 %collective-permute-start.75 = (bf16[256,1280]{1,0:T(8,128)(2,1)S(1)}, bf16[256,1280]{1,0:T(8,128)(2,1)}, u32[]{:S(2)}, u32[]{:S(2)}) collective-permute-start(bf16[256,1280]{1,0:T(8,128)(2,1)S(1)} %fusion.31), channel_id=1, source_target_pairs={{0,2},{1,3},{2,0},{3,1},{4,6},{5,7},{6,4},{7,5},{8,10},{9,11},{10,... | collective-permute-start | bytes 1966088 | tf_op jit(solution)/shard_map/backward/ppermute | solution.py:32
  457.3 14.0 %collective-permute-start.76 = (f32[256]{0:T(256)S(1)}, f32[256]{0:T(256)S(1)}, u32[]{:S(2)}, u32[]{:S(2)}) collective-permute-start(f32[256]{0:T(256)S(1)} %get-tuple-element.33), channel_id=1, source_target_pairs={{0,1},{1,2},{2,3},{3,0},{4,5},{5,6},{6,7},{7,4},{8,9},{9,10},{10,1... | collective-permute-start | bytes 3080 | tf_op jit(solution)/shard_map/backward/ppermute | solution.py:32
  460.7 12.6 %collective-permute-start.77 = (f32[256]{0:T(256)S(1)}, f32[256]{0:T(256)S(1)}, u32[]{:S(2)}, u32[]{:S(2)}) collective-permute-start(f32[256]{0:T(256)S(1)} %get-tuple-element.33), channel_id=1, source_target_pairs={{0,2},{1,3},{2,0},{3,1},{4,6},{5,7},{6,4},{7,5},{8,10},{9,11},{10,... | collective-permute-start | bytes 3080 | tf_op jit(solution)/shard_map/backward/ppermute | solution.py:32
  462.9 10.9 %collective-permute-start.78 = (f32[256]{0:T(256)S(1)}, f32[256]{0:T(256)S(1)}, u32[]{:S(2)}, u32[]{:S(2)}) collective-permute-start(f32[256]{0:T(256)S(1)} %get-tuple-element.33), channel_id=1, source_target_pairs={{0,3},{1,0},{2,1},{3,2},{4,7},{5,4},{6,5},{7,6},{8,11},{9,8},{10,9... | collective-permute-start | bytes 3080 | tf_op jit(solution)/shard_map/backward/ppermute | solution.py:32
  (23 other events, 473.9 us)

commit v2 on v1

v2 whole, which is shorter than its diff:
```python
import jax
import jax.numpy as jnp
from jax import lax
from jax.sharding import Mesh
from jax.sharding import PartitionSpec as P

FTOK = 2048
SLOTS = 16
LANES = 128
F32 = jnp.float32
BF16 = jnp.bfloat16
SEQ = ("y_hi", "z")
TP = ("y_lo", "core")
BLOCK = ("group",) + SEQ
SWAP = ((0, 1), (1, 0))


def gelu_tanh(v):
    return jax.nn.gelu(v, approximate=True)


def to_tiles(x, tiles):
    flat = jnp.pad(x, ((0, 0), (0, tiles * 8 * LANES - x.shape[1])))
    return flat.reshape(x.shape[0], tiles * 8, LANES)


def swap_all(x):
    return lax.all_to_all(x, SEQ, split_axis=0, concat_axis=0, tiled=True)


def local(
    hidden,
    norm_gain,
    gen_value,
    gen_head,
    critic_embed,
    critic_gain,
    critic_value,
    critic_head,
    noise,
    owner,
    tsteps,
    noise_mix,
    gap_weight,
):
    rows, width = hidden.shape
    latent_width = gen_head.shape[1]
    depth, gen_cols = gen_value.shape
    seq_count = lax.axis_size(SEQ)
    group_id, seq_id = lax.axis_index("group"), lax.axis_index(SEQ)
    yl, c = lax.axis_index("y_lo"), lax.axis_index("core")
    shard_id = lax.axis_index(BLOCK)

    with jax.named_scope("gather_value"):
        gen_pair = lax.all_gather(gen_value, "y_hi", axis=1, tiled=True)
        gen_full = lax.all_gather(gen_pair, "z", axis=0, tiled=True)

    with jax.named_scope("critic_matrix_part"):
        cols = critic_value.shape[1]
        critic_id = group_id // 2
        embed = lax.dynamic_slice(
            critic_embed, (critic_id, 0, seq_id * depth), (1, latent_width, depth)
        )[0].astype(F32)
        scale = lax.dynamic_slice(critic_gain, (critic_id, seq_id * depth), (1, depth))
        part = jnp.dot(
            embed * scale.astype(F32),
            critic_value.astype(F32),
            precision=lax.Precision.HIGHEST,
        )
        each = latent_width // seq_count
        part = part.reshape(seq_count, each * cols)

    with jax.named_scope("noise_requests"):
        crit_rows = noise.shape[0]
        target = owner // crit_rows
        at = (target[:, None] == jnp.arange(seq_count, dtype=jnp.int32)[None, :]).astype(BF16)
        ids = jnp.arange(rows, dtype=jnp.int32)
        before = (ids[None, :] < ids[:, None]).astype(BF16)
        prefix = jnp.dot(before, at, preferred_element_type=F32)
        rank = jnp.sum(prefix * at.astype(F32), axis=1).astype(jnp.int32)
        slot = target * SLOTS + rank
        total = seq_count * SLOTS
        holds = jnp.arange(total, dtype=jnp.int32)[:, None] == slot[None, :]
        wanted = jnp.sum(jnp.where(holds, (owner % crit_rows + 1)[None, :], 0), axis=1) - 1
        wanted = wanted.astype(F32).reshape(seq_count, SLOTS)

    with jax.named_scope("first_exchange"):
        sent = to_tiles(jnp.concatenate([part, wanted], axis=1), 1)
        got = swap_all(sent).reshape(seq_count, -1)

    with jax.named_scope("noise_replies"):
        asked = got[:, each * cols : each * cols + SLOTS].reshape(total)
        take = asked[:, None] == jnp.arange(crit_rows, dtype=jnp.int32).astype(F32)[None, :]
        found = jnp.dot(take.astype(BF16), noise, preferred_element_type=F32).astype(BF16)
        found = found.reshape(seq_count, SLOTS * latent_width)
        mine = jnp.sum(got[:, : each * cols], axis=0).astype(BF16)

    with jax.named_scope("second_exchange"):
        mine = jnp.broadcast_to(mine[None, :], (seq_count, each * cols))
        sent = to_tiles(jnp.concatenate([found, mine], axis=1), 2)
        got = swap_all(sent).reshape(seq_count, -1)
        found = got[:, : SLOTS * latent_width].reshape(total, latent_width)
        matrix = got[:, SLOTS * latent_width : SLOTS * latent_width + each * cols]
        matrix = matrix.reshape(latent_width, cols)
        own_noise = lax.dot_general(
            holds.astype(BF16), found, (((0,), (0,)), ((), ())), preferred_element_type=F32
        )

    with jax.named_scope("critic_gather"):
        matrix = lax.all_gather(matrix, ("group",) + TP, axis=1, tiled=True)
        head = jnp.where(critic_id == 1, critic_head, -critic_head)
        head = lax.all_gather(head, ("group",) + TP, axis=0, tiled=True)

    with jax.named_scope("levels"):
        level = tsteps[shard_id * rows // FTOK]
        signal_mix, noise_part = noise_mix[0, level], noise_mix[1, level] * own_noise
        weight = gap_weight[level]

    with jax.named_scope("forward"):
        inputs = hidden.astype(F32)
        inverse = lax.rsqrt(jnp.mean(inputs * inputs, axis=-1, keepdims=True) + 1e-06)
        normed = (inputs * inverse * norm_gain.astype(F32)).astype(BF16)
        half = width // 2
        values = jnp.dot(
            normed[:, :half], gen_full[:, :gen_cols], preferred_element_type=F32
        ) + jnp.dot(normed[:, half:], gen_full[:, gen_cols:], preferred_element_type=F32)
        activated, gelu_back = jax.vjp(gelu_tanh, values)
        latent_part = jnp.dot(activated.astype(BF16), gen_head, preferred_element_type=F32)
        parts = lax.all_gather(latent_part.astype(BF16), TP, axis=0)
        gen_latent = jnp.sum(parts.astype(F32), axis=0).astype(BF16)
        slope = gelu_back(jnp.ones_like(values))[0]

    with jax.named_scope("critics"):
        noisy = (signal_mix * gen_latent.astype(F32) + noise_part).astype(BF16)
        raw = jnp.dot(noisy, matrix, preferred_element_type=F32)
        split = raw.shape[1] // 2
        acts = []
        for which in range(2):
            embedded = jnp.dot(noisy, critic_embed[which], preferred_element_type=F32)
            scale_rows = lax.rsqrt(jnp.mean(embedded * embedded, axis=-1, keepdims=True) + 1e-06)
            own = raw[:, which * split : (which + 1) * split] * scale_rows
            acts.append(gelu_tanh(own).astype(BF16))
        gap = jnp.dot(jnp.concatenate(acts, axis=1), head, preferred_element_type=F32)
        cotangent = (weight * gap).astype(BF16)

    with jax.named_scope("backward"):
        grad_act = lax.dot_general(
            cotangent, gen_head, (((1,), (1,)), ((), ())), preferred_element_type=F32
        )
        grad_values = (slope * grad_act).astype(BF16)
        mixed = jnp.sum(grad_values.astype(F32) * values, axis=1)
        mixed = mixed + lax.ppermute(mixed, "core", SWAP)
        mixed = mixed + lax.ppermute(mixed, "y_lo", SWAP)
        columns = width // 4

        def grad_slice(at_y, at_c):
            weights = lax.dynamic_slice(
                gen_full, (at_c * columns, at_y * gen_cols), (columns, gen_cols)
            )
            return lax.dot_general(
                grad_values, weights, (((1,), (1,)), ((), ())), preferred_element_type=F32
            )

        far = lax.ppermute(grad_slice(1 - yl, 1 - c).astype(BF16), "core", SWAP)
        far = (grad_slice(1 - yl, c) + far.astype(F32)).astype(BF16)
        far = lax.ppermute(far, "y_lo", SWAP)
        near = lax.ppermute(grad_slice(yl, 1 - c).astype(BF16), "core", SWAP)
        near = grad_slice(yl, c) + near.astype(F32)
        grad_normed = near + far.astype(F32)
        first = (yl * 2 + c) * columns
        gain = lax.dynamic_slice_in_dim(norm_gain, first, columns, 0).astype(F32)
        own = lax.dynamic_slice_in_dim(hidden, first, columns, 1).astype(F32)
        pulled = inverse * inverse * (mixed / width)[:, None]
        grad_hidden = (inverse * (grad_normed * gain) - own * pulled).astype(BF16)
    return (gen_latent, grad_hidden)


def solution(mesh):
    shape = mesh.devices.shape
    fine = Mesh(
        mesh.devices.reshape(shape[0], 2, shape[1] // 2, 2, shape[2] // 2),
        ("group", "y_hi", "z", "y_lo", "core"),
    )
    return jax.shard_map(
        local,
        mesh=fine,
        in_specs=(
            P(BLOCK, None),
            P(),
            P(SEQ, TP),
            P(TP, None),
            P(),
            P(),
            P(SEQ, ("group",) + TP),
            P(("group",) + TP, None),
            P(SEQ, None),
            P(BLOCK),
            P(),
            P(),
            P(),
        ),
        out_specs=(P(BLOCK, None), P(BLOCK, TP)),
        check_vma=False,
    )
```

time: 481 us -> 190 us (0.40)
  starting transfers between devices: 290 us -> 34.1 us
  local copies, waits for them, and re-layouts: 67.2 us -> 12 us
  blocking collectives: 16.7 us -> 59.9 us
  waiting for transfers between devices: 61.6 us -> 23.3 us
  between operations: 5.35 us -> 16.4 us
    ppermute x79 -> x5, starting transfers between devices: 290 us -> 11.9 us  [the longest x1 2.97 us: local(): mixed = mixed + lax.ppermute(mixed, 'y_lo', SWAP)]
    dynamic_update_slice x70 -> x0, local copies, waits for them, and re-layouts: 53.8 us -> none  [the longest x34 34.8 us: place(): return lax.dynamic_update_slice(out, part, (start, jnp.zeros_like(start)))]
    ppermute x79 -> x5, waiting for transfers between devices: 61.6 us -> 7.84 us  [the longest x1 7.81 us: local(): mixed = mixed + lax.ppermute(mixed, 'y_lo', SWAP)]
    all_gather x1 -> x4, blocking collectives: 16.7 us -> 59.9 us  [the longest x1 24.6 us: local(): head = lax.all_gather(head, ('group',) + TP, axis=0, tiled=True)]
    all_to_all x0 -> x2, starting transfers between devices: none -> 22.2 us  [swap_all(): return lax.all_to_all(x, SEQ, split_axis=0, concat_axis=0, tiled=True)]
    all_to_all x0 -> x2, waiting for transfers between devices: none -> 10.7 us  [swap_all(): return lax.all_to_all(x, SEQ, split_axis=0, concat_axis=0, tiled=True)]
    unnamed x19 -> x29, local copies, waits for them, and re-layouts: 0.53 us -> 6.41 us
    broadcast_in_dim x16 -> x0, local copies, waits for them, and re-layouts: 5.31 us -> none  [the longest x1 3.19 us: ring_gather(): out = jnp.zeros((2 * n * rows,) + x.shape[1:], x.dtype)]
  transfers between devices with their start and end apart: 79 -> 8, of which waited for: 16 -> 3; matrix products, arithmetic and copies ran while one was open for 17% -> 15% of each run, Pallas kernels for 0% -> 0%
where the time goes in v2:
time: 190 us; the launch traced here: 189 us
  blocking collectives  59.9 us (32%)
  starting transfers between devices  34.1 us (18%)
  matrix products  29.5 us (16%)
  waiting for transfers between devices  23.3 us (12%)
  between operations  16.4 us (9%)
  other arithmetic  13.7 us (7%)
  local copies, waits for them, and re-layouts  12 us (6%)
    all_gather x1, blocking collectives, local(): head = lax.all_gather(head, ('group',) + TP, axis=0, tiled=True)  24.6 us
    all_to_all x2, starting transfers between devices, swap_all(): return lax.all_to_all(x, SEQ, split_axis=0, concat_axis=0, tiled=True)  22.2 us
    all_gather x1, blocking collectives, local(): matrix = lax.all_gather(matrix, ('group',) + TP, axis=1, tiled=True)  18.4 us
    dot_general x4, matrix products, grad_slice(): lax.dot_general(grad_values, weights, (((1,), (1,)), ((), ())), preferred...  11.3 us
    all_to_all x2, waiting for transfers between devices, swap_all(): return lax.all_to_all(x, SEQ, split_axis=0, concat_axis=0, tiled=True)  10.7 us
    all_gather x1, blocking collectives, local(): gen_pair = lax.all_gather(gen_value, 'y_hi', axis=1, tiled=True)  9.64 us
    ppermute x1, waiting for transfers between devices, local(): mixed = mixed + lax.ppermute(mixed, 'y_lo', SWAP)  7.81 us
    all_gather x1, blocking collectives, local(): parts = lax.all_gather(latent_part.astype(BF16), TP, axis=0)  7.25 us
  transfers between devices with their start and end apart: 8, of which 3 were waited for; matrix products, arithmetic and copies ran while one was open for 15% of the time, Pallas kernels for 0%

profile of v2, /device:TPU:1, one launch (start us, length us, event | category | flops | bytes accessed | tf_op | source)
XLA Modules:
  0.0 188.9 jit_solution(11825526811695017285)
XLA Ops:
  7.2 0.0 copy-start
  7.2 0.0 all-gather.5.cloned.1.call-start
  7.2 9.6 %all_gather.18 = bf16[160,1280]{1,0:T(8,128)(2,1)} all-gather(bf16[160,640]{1,0:T(8,128)(2,1)} %param.15), channel_id=1, replica_groups=mesh['group'=4,'y_hi'=2,'z'=16,'y_lo'=2,'core'=2] {'y_hi'}, dimensions={1}, use_global_device_ids=true | all-gather | bytes 614400 | tf_op jit(solution)/shard_map/gather_value/all_gather | solution.py:55
  16.9 0.0 all-gather.5.cloned.1.call-update
  16.9 0.8 dynamic-slice_convert_fusion.1
  17.7 1.2 fusion.73
  18.9 0.1 reshape.76
  19.0 0.7 and_select_fusion.1
  19.7 0.2 fusion.58
  19.9 0.1 select_reduce_fusion
  20.1 0.1 convert_element_type.125
  20.2 0.7 copy.26
  20.8 17.6 %all-to-all-start = ((f32[32,8,128]{2,1,0:T(8,128)}), f32[32,8,128]{2,1,0:T(8,128)S(1)}, u32[]{:S(2)}, u32[]{:S(2)}) async-start(f32[32,8,128]{2,1,0:T(8,128)} %bitcast.15), calls=%async_computation | async-start | bytes 262144 | tf_op jit(solution)/shard_map/first_exchange/all_to_all | solution.py:28
  38.4 0.7 convert_element_type.114
  39.2 2.3 %fusion = f32[256]{0:T(256)S(1)} fusion(bf16[256,5120]{1,0:T(8,128)(2,1)} %param.13), kind=kLoop, calls=%fused_computation.4 | loop fusion | flops 3931904 | bytes 2622464 | tf_op jit(solution)/shard_map/forward/reduce_sum | solution.py:121
  41.5 2.3 %fusion.2 = bf16[256,5120]{1,0:T(8,128)(2,1)} fusion(bf16[256,5120]{1,0:T(8,128)(2,1)S(1)} %copy-done.1, f32[5120]{0:T(1024)S(1)} %convert_element_type.114, f32[256]{0:T(256)S(1)} %add_rsqrt_fusion.2), kind=kLoop, calls=%fused_computation.6 | loop fusion | flops 5242880 | bytes 5264384 | tf_op jit(solution)/shard_map/forward/convert_element_type | solution.py:122
  43.8 0.6 dynamic_slice.36
  45.7 10.6 %all-to-all-done = f32[32,8,128]{2,1,0:T(8,128)S(1)} async-done(((f32[32,8,128]{2,1,0:T(8,128)}), f32[32,8,128]{2,1,0:T(8,128)S(1)}, u32[]{:S(2)}, u32[]{:S(2)}) %all-to-all-start) | async-done | bytes 131104 | tf_op jit(solution)/shard_map/first_exchange/all_to_all | solution.py:28
  56.4 0.1 eq.52
  56.5 0.5 fusion.45
  57.1 0.1 copy.23
  57.2 0.1 reshape.79
  57.4 0.7 copy.28
  58.1 4.6 %all-to-all-start.1 = ((bf16[32,16,128]{2,1,0:T(8,128)(2,1)}), bf16[32,16,128]{2,1,0:T(8,128)(2,1)}, u32[]{:S(2)}, u32[]{:S(2)}) async-start(bf16[32,16,128]{2,1,0:T(8,128)(2,1)} %bitcast.19), calls=%async_computation.1 | async-start | bytes 262144 | tf_op jit(solution)/shard_map/second_exchange/all_to_all | solution.py:28
  62.7 24.6 %all-gather.2 = bf16[16,320,64]{1,2,0:T(8,128)(2,1)S(1)} all-gather(bf16[1,320,64]{1,2,0:T(8,128)(2,1)S(1)} %fusion.74), channel_id=1, replica_groups=mesh['group'=4,'y_hi'=2,'z'=16,'y_lo'=2,'core'=2] {'group','y_lo','core'}, dimensions={0}, use_global_device_ids=true | all-gather | bytes 696320 | tf_op jit(solution)/shard_map/critic_gather/all_gather | solution.py:112
  87.3 0.5 copy.25
  87.7 1.5 reshape.90
  89.9 1.3 dynamic_slice.37
  91.2 1.4 constant_dynamic-slice_fusion
  92.5 0.9 copy.32
  93.5 0.8 reshape.82
  94.3 0.1 reshape.83
  94.4 18.4 %all-gather.1 = bf16[16,320,64]{1,2,0:T(8,128)(2,1)S(1)} all-gather(bf16[1,320,64]{1,2,0:T(8,128)(2,1)S(1)} %bitcast.61), channel_id=1, replica_groups=mesh['group'=4,'y_hi'=2,'z'=16,'y_lo'=2,'core'=2] {'group','y_lo','core'}, dimensions={0}, use_global_device_ids=true | all-gather | bytes 696320 | tf_op jit(solution)/shard_map/critic_gather/all_gather | solution.py:110
  112.8 0.5 copy.24
  113.3 1.5 reshape.88
  114.7 4.8 %all-gather.5.cloned.1.call-done = bf16[2560,1280]{1,0:T(8,128)(2,1)} async-done(((bf16[160,1280]{1,0:T(8,128)(2,1)}), bf16[2560,1280]{1,0:T(8,128)(2,1)}) %all-gather.5.cloned.1.call-update) | async-done | bytes 6553616 | tf_op jit(solution)/shard_map/gather_value/all_gather | solution.py:56
  119.5 3.7 %fusion.3 = f32[256,640]{1,0:T(8,128)S(1)} fusion(bf16[2560,1280]{1,0:T(8,128)(2,1)} %all-gather.5.cloned.1.call-done, bf16[256,5120]{1,0:T(8,128)(2,1)} %fusion.2), kind=kOutput, calls=%fused_computation.9 | convolution fusion | flops 838860800 | bytes 5242880 | tf_op jit(solution)/shard_map/forward/dot_general | solution.py:126
  123.2 0.6 copy-done.2
  123.8 2.5 %fusion.39 = f32[256,640]{1,0:T(8,128)S(1)} fusion(f32[256,640]{1,0:T(8,128)S(1)} %fusion.3, bf16[2560,1280]{1,0:T(8,128)(2,1)S(1)} %copy-done.2, bf16[256,5120]{1,0:T(8,128)(2,1)} %fusion.2), kind=kOutput, calls=%fused_computation.52 | convolution fusion | flops 839024640 | bytes 5898240 | tf_op jit(solution)/shard_map/forward/dot_general | solution.py:124
  126.3 0.3 convolution_convert_fusion.2
  126.7 0.5 copy-done.10
  127.2 7.2 %all-gather = bf16[1024,64]{0,1:T(8,128)(2,1)S(1)} all-gather(bf16[256,64]{0,1:T(8,128)(2,1)S(1)} %convolution_convert_fusion.2), channel_id=2, replica_groups=mesh['group'=4,'y_hi'=2,'z'=16,'y_lo'=2,'core'=2] {'y_lo','core'}, dimensions={0}, use_global_device_ids=true | all-gather | bytes 163840 | tf_op jit(solution)/shard_map/forward/all_gather | solution.py:129
  134.4 0.1 reshape.86
  134.5 0.2 reduce_sum.76
  134.7 0.0 copy-start.6
  134.7 1.6 fusion.55
  136.3 2.1 %fusion.29 = f32[256]{0:T(256)S(1)} fusion(bf16[256,64]{0,1:T(8,128)(2,1)S(1)} %fusion.55, bf16[2,64,5120]{2,1,0:T(8,128)(2,1)} %param.17), kind=kOutput, calls=%fused_computation.39 | convolution fusion | flops 170393344 | bytes 689152 | tf_op jit(solution)/shard_map/critics/dot_general | solution.py:139
  138.4 1.0 fusion.30
  139.4 0.9 fusion.91
  140.2 3.1 %fusion.14 = (bf16[256,2560]{1,0:T(8,128)(2,1)}, bf16[256,2560]{1,0:T(8,128)(2,1)}) fusion(f32[256,5120]{1,0:T(8,128)S(1)} %fusion.91, f32[256]{0:T(256)S(1)} %get-tuple-element.11, f32[256]{0:T(256)S(1)} %get-tuple-element.10), kind=kLoop, calls=%fused_computation.20 | loop fusion | flops 13107200 | bytes 7866368 | tf_op jit(solution)/shard_map/critics/convert_element_type | solution.py:142
  143.3 4.2 %multiply_reduce_fusion = (f32[256]{0:T(256)S(1)}, bf16[256,640]{1,0:T(8,128)(2,1)S(1)}) fusion(f32[256,640]{1,0:T(8,128)} %copy-done.10, bf16[640,64]{0,1:T(8,128)(2,1)S(1)} %copy-done.8, bf16[5120,64]{0,1:T(8,128)(2,1)} %reshape.90, bf16[256,2560]{1,0:T(8,128)(2,1)} %get-tuple-element.3, bf16[256,2560]{1,0:T(8,128)(2,1)} %get-tuple-element.2, f32[]{:T(128)} %bitcast.1), kind=kOutput, calls=%fused_computation.75 | convolution fusion | flops 197623552 | bytes 4342788 | tf_op jit(solution)/shard_map/backward/dot_general | solution.py:147
  147.6 3.0 %convolution_convert_fusion = bf16[256,1280]{1,0:T(8,128)(2,1)} fusion(bf16[256,640]{1,0:T(8,128)(2,1)S(1)} %get-tuple-element.9, bf16[2560,1280]{1,0:T(8,128)(2,1)} %all-gather.5.cloned.1.call-done, s32[]{:T(128)S(6)} %select_n.80, s32[]{:T(128)S(6)} %select_n.81), kind=kOutput, calls=%fused_computation.35 | convolution fusion | flops 419758080 | bytes 2621448 | tf_op jit(solution)/shard_map/backward/dot_general | solution.py:160
  150.6 2.1 %collective-permute-start.1 = (bf16[256,1280]{1,0:T(8,128)(2,1)}, bf16[256,1280]{1,0:T(8,128)(2,1)}, u32[]{:S(2)}, u32[]{:S(2)}) collective-permute-start(bf16[256,1280]{1,0:T(8,128)(2,1)} %convolution_convert_fusion), channel_id=1, source_target_pairs={{0,1},{1,0},{2,3},{3,2},{4,5},{5,4},{6,7},{7,6},{8,9},{9,8},{10,11... | collective-permute-start | bytes 1966088 | tf_op jit(solution)/shard_map/backward/ppermute | solution.py:164
  152.6 3.0 %convolution_convert_fusion.1 = bf16[256,1280]{1,0:T(8,128)(2,1)} fusion(bf16[256,640]{1,0:T(8,128)(2,1)S(1)} %get-tuple-element.9, bf16[2560,1280]{1,0:T(8,128)(2,1)} %all-gather.5.cloned.1.call-done, s32[]{:T(128)S(6)} %select_n.80, s32[]{:T(128)S(6)} %select_n.79), kind=kOutput, calls=%fused_computation.36 | convolution fusion | flops 419758080 | bytes 2621448 | tf_op jit(solution)/shard_map/backward/dot_general | solution.py:160
  155.6 2.3 %collective-permute-start = (bf16[256,1280]{1,0:T(8,128)(2,1)}, bf16[256,1280]{1,0:T(8,128)(2,1)}, u32[]{:S(2)}, u32[]{:S(2)}) collective-permute-start(bf16[256,1280]{1,0:T(8,128)(2,1)} %convolution_convert_fusion.1), channel_id=1, source_target_pairs={{0,1},{1,0},{2,3},{3,2},{4,5},{5,4},{6,7},{7,6},{8,9},{9,8},{10,11... | collective-permute-start | bytes 1966088 | tf_op jit(solution)/shard_map/backward/ppermute | solution.py:167
  157.9 3.1 %add_convert_fusion = bf16[256,1280]{1,0:T(8,128)(2,1)} fusion(bf16[256,1280]{1,0:T(8,128)(2,1)} %collective-permute-done.1, bf16[256,640]{1,0:T(8,128)(2,1)S(1)} %get-tuple-element.9, bf16[2560,1280]{1,0:T(8,128)(2,1)} %all-gather.5.cloned.1.call-done, s32[]{:T(128)S(6)} %select_n.78, s32[]{:T(128)S(6)} %select_n.81), kind=kOutput, calls=%fused_computation.50 | convolution fusion | flops 420413440 | bytes 3276808 | tf_op jit(solution)/shard_map/backward/dot_general | solution.py:160
  161.1 2.3 %collective-permute-start.2 = (bf16[256,1280]{1,0:T(8,128)(2,1)}, bf16[256,1280]{1,0:T(8,128)(2,1)}, u32[]{:S(2)}, u32[]{:S(2)}) collective-permute-start(bf16[256,1280]{1,0:T(8,128)(2,1)} %add_convert_fusion), channel_id=1, source_target_pairs={{0,2},{2,0},{1,3},{3,1},{4,6},{6,4},{5,7},{7,5},{8,10},{10,8},{9,1... | collective-permute-start | bytes 1966088 | tf_op jit(solution)/shard_map/backward/ppermute | solution.py:166
  163.3 2.4 %collective-permute-start.3 = (f32[256]{0:T(256)S(1)}, f32[256]{0:T(256)S(1)}, u32[]{:S(2)}, u32[]{:S(2)}) collective-permute-start(f32[256]{0:T(256)S(1)} %get-tuple-element.8), channel_id=1, source_target_pairs={{0,1},{1,0},{2,3},{3,2},{4,5},{5,4},{6,7},{7,6},{8,9},{9,8},{10,11... | collective-permute-start | bytes 3080 | tf_op jit(solution)/shard_map/backward/ppermute | solution.py:152
  165.7 0.8 dynamic-slice_convert_fusion
  166.5 0.0 collective-permute-done.3
  166.5 3.0 %collective-permute-start.4 = (f32[256]{0:T(256)S(1)}, f32[256]{0:T(256)S(1)}, u32[]{:S(2)}, u32[]{:S(2)}) collective-permute-start(f32[256]{0:T(256)S(1)} %add.162), channel_id=1, source_target_pairs={{0,2},{2,0},{1,3},{3,1},{4,6},{6,4},{5,7},{7,5},{8,10},{10,8},{9,1... | collective-permute-start | bytes 3080 | tf_op jit(solution)/shard_map/backward/ppermute | solution.py:153
  169.5 2.1 %fusion.35 = f32[256,1280]{1,0:T(8,128)S(1)} fusion(bf16[256,640]{1,0:T(8,128)(2,1)S(1)} %get-tuple-element.9, bf16[2560,1280]{1,0:T(8,128)(2,1)} %all-gather.5.cloned.1.call-done, s32[]{:T(128)S(6)} %select_n.78, s32[]{:T(128)S(6)} %select_n.79), kind=kOutput, calls=%fused_computation.45 | convolution fusion | flops 419430400 | bytes 3276808 | tf_op jit(solution)/shard_map/backward/dot_general | solution.py:160
  171.6 7.8 %collective-permute-done.4 = f32[256]{0:T(256)S(1)} collective-permute-done((f32[256]{0:T(256)S(1)}, f32[256]{0:T(256)S(1)}, u32[]{:S(2)}, u32[]{:S(2)}) %collective-permute-start.4) | collective-permute-done | bytes 1056 | tf_op jit(solution)/shard_map/backward/ppermute | solution.py:153
  179.5 2.6 %subtract_convert_fusion = bf16[256,1280]{1,0:T(8,128)(2,1)} fusion(bf16[256,1280]{1,0:T(8,128)(2,1)} %collective-permute-done.2, f32[256,1280]{1,0:T(8,128)S(1)} %fusion.35, bf16[256,1280]{1,0:T(8,128)(2,1)} %collective-permute-done, f32[256]{0:T(256)S(1)} %multiply_multiply_fusion.4, bf16[256,5120]{1,0:T(8,128)(2,1)S(1)} %copy-done.1, s32[]{:T(128)S(6)} %select_n.82, ...), kind=kLoop, calls=%fused_computation.49 | loop fusion | flops 3276800 | bytes 3939332 | tf_op jit(solution)/shard_map/backward/convert_element_type | solution.py:174
  (39 shorter events, 0.2 us)
Async XLA Ops:
  7.2 49.3 %copy-start = (bf16[1024,64]{0,1:T(8,128)(2,1)S(1)}, bf16[1024,64]{0,1:T(8,128)(2,1)}, u32[]{:S(2)}) copy-start(bf16[1024,64]{0,1:T(8,128)(2,1)} %param.21) | copy-start | bytes 393220
  7.2 34.3 %copy-start.1 = (bf16[256,5120]{1,0:T(8,128)(2,1)S(1)}, bf16[256,5120]{1,0:T(8,128)(2,1)}, u32[]{:S(2)}) copy-start(bf16[256,5120]{1,0:T(8,128)(2,1)} %param.13) | copy-start | bytes 7864324
  7.2 112.3 %all-gather.5.cloned.1.call-start = ((), (), s32[]{:S(2)}) async-start(), calls=%async_computation.2 | async-start | bytes 6963200 | tf_op jit(solution)/shard_map/gather_value/all_gather | solution.py:56
  20.8 35.5 %all-to-all-start = ((f32[32,8,128]{2,1,0:T(8,128)}), f32[32,8,128]{2,1,0:T(8,128)S(1)}, u32[]{:S(2)}, u32[]{:S(2)}) async-start(f32[32,8,128]{2,1,0:T(8,128)} %bitcast.15), calls=%async_computation | async-start | bytes 262144 | tf_op jit(solution)/shard_map/first_exchange/all_to_all | solution.py:28
  41.5 2.3 %copy-start.9 = (s32[16]{0:T(128)S(1)}, s32[16]{0:T(128)}, u32[]{:S(2)}) copy-start(s32[16]{0:T(128)} %param.23) | copy-start | bytes 196
  43.8 18.8 %copy-start.5 = (bf16[320,64]{0,1:T(8,128)(2,1)S(1)}, bf16[320,64]{0,1:T(8,128)(2,1)}, u32[]{:S(2)}) copy-start(bf16[320,64]{0,1:T(8,128)(2,1)} %param.20) | copy-start | bytes 122884
  58.1 34.4 %all-to-all-start.1 = ((bf16[32,16,128]{2,1,0:T(8,128)(2,1)}), bf16[32,16,128]{2,1,0:T(8,128)(2,1)}, u32[]{:S(2)}, u32[]{:S(2)}) async-start(bf16[32,16,128]{2,1,0:T(8,128)(2,1)} %bitcast.19), calls=%async_computation.1 | async-start | bytes 262144 | tf_op jit(solution)/shard_map/second_exchange/all_to_all | solution.py:28
  119.5 4.2 %copy-start.2 = (bf16[2560,1280]{1,0:T(8,128)(2,1)S(1)}, bf16[2560,1280]{1,0:T(8,128)(2,1)}, u32[]{:S(2)}) copy-start(bf16[2560,1280]{1,0:T(8,128)(2,1)} %all-gather.5.cloned.1.call-done) | copy-start | bytes 19660804
  123.8 2.6 %copy-start.8 = (bf16[640,64]{0,1:T(8,128)(2,1)S(1)}, bf16[640,64]{0,1:T(8,128)(2,1)}, u32[]{:S(2)}) copy-start(bf16[640,64]{0,1:T(8,128)(2,1)} %param.16) | copy-start | bytes 245764
  123.8 10.9 %copy-start.4 = (bf16[512,64]{1,0:T(8,128)(2,1)S(1)}, bf16[512,64]{1,0:T(8,128)(2,1)}, u32[]{:S(2)}) copy-start(bf16[512,64]{1,0:T(8,128)(2,1)} %reshape.82) | copy-start | bytes 196612
  126.3 0.8 copy-start.10
  134.7 4.7 %copy-start.6 = (bf16[256,64]{0,1:T(8,128)(2,1)}, bf16[256,64]{0,1:T(8,128)(2,1)S(1)}, u32[]{:S(2)}) copy-start(bf16[256,64]{0,1:T(8,128)(2,1)S(1)} %reduce_sum.76) | copy-start | bytes 98308
  134.7 3.7 %copy-start.7 = (bf16[2,64,5120]{2,1,0:T(8,128)(2,1)S(1)}, bf16[2,64,5120]{2,1,0:T(8,128)(2,1)}, u32[]{:S(2)}) copy-start(bf16[2,64,5120]{2,1,0:T(8,128)(2,1)} %param.17) | copy-start | bytes 3932164
  136.3 3.1 %copy-start.3 = (bf16[5120,64]{0,1:T(8,128)(2,1)S(1)}, bf16[5120,64]{0,1:T(8,128)(2,1)}, u32[]{:S(2)}) copy-start(bf16[5120,64]{0,1:T(8,128)(2,1)} %reshape.88) | copy-start | bytes 1966084
  150.6 7.3 %collective-permute-start.1 = (bf16[256,1280]{1,0:T(8,128)(2,1)}, bf16[256,1280]{1,0:T(8,128)(2,1)}, u32[]{:S(2)}, u32[]{:S(2)}) collective-permute-start(bf16[256,1280]{1,0:T(8,128)(2,1)} %convolution_convert_fusion), channel_id=1, source_target_pairs={{0,1},{1,0},{2,3},{3,2},{4,5},{5,4},{6,7},{7,6},{8,9},{9,8},{10,11... | collective-permute-start | bytes 1966088 | tf_op jit(solution)/shard_map/backward/ppermute | solution.py:164
  155.6 23.8 %collective-permute-start = (bf16[256,1280]{1,0:T(8,128)(2,1)}, bf16[256,1280]{1,0:T(8,128)(2,1)}, u32[]{:S(2)}, u32[]{:S(2)}) collective-permute-start(bf16[256,1280]{1,0:T(8,128)(2,1)} %convolution_convert_fusion.1), channel_id=1, source_target_pairs={{0,1},{1,0},{2,3},{3,2},{4,5},{5,4},{6,7},{7,6},{8,9},{9,8},{10,11... | collective-permute-start | bytes 1966088 | tf_op jit(solution)/shard_map/backward/ppermute | solution.py:167
  161.1 18.4 %collective-permute-start.2 = (bf16[256,1280]{1,0:T(8,128)(2,1)}, bf16[256,1280]{1,0:T(8,128)(2,1)}, u32[]{:S(2)}, u32[]{:S(2)}) collective-permute-start(bf16[256,1280]{1,0:T(8,128)(2,1)} %add_convert_fusion), channel_id=1, source_target_pairs={{0,2},{2,0},{1,3},{3,1},{4,6},{6,4},{5,7},{7,5},{8,10},{10,8},{9,1... | collective-permute-start | bytes 1966088 | tf_op jit(solution)/shard_map/backward/ppermute | solution.py:166
  163.3 3.2 %collective-permute-start.3 = (f32[256]{0:T(256)S(1)}, f32[256]{0:T(256)S(1)}, u32[]{:S(2)}, u32[]{:S(2)}) collective-permute-start(f32[256]{0:T(256)S(1)} %get-tuple-element.8), channel_id=1, source_target_pairs={{0,1},{1,0},{2,3},{3,2},{4,5},{5,4},{6,7},{7,6},{8,9},{9,8},{10,11... | collective-permute-start | bytes 3080 | tf_op jit(solution)/shard_map/backward/ppermute | solution.py:152
  166.5 12.9 %collective-permute-start.4 = (f32[256]{0:T(256)S(1)}, f32[256]{0:T(256)S(1)}, u32[]{:S(2)}, u32[]{:S(2)}) collective-permute-start(f32[256]{0:T(256)S(1)} %add.162), channel_id=1, source_target_pairs={{0,2},{2,0},{1,3},{3,1},{4,6},{6,4},{5,7},{7,5},{8,10},{10,8},{9,1... | collective-permute-start | bytes 3080 | tf_op jit(solution)/shard_map/backward/ppermute | solution.py:153
Sparse Core Ops, SparseCore 0:
  17.0 102.4 all-gather.4

commit v3 on v2

--- a/solution.py
+++ b/solution.py
@@ -1,6 +1,10 @@
+import functools
+
 import jax
 import jax.numpy as jnp
 from jax import lax
+from jax.experimental import pallas as pl
+from jax.experimental.pallas import tpu as pltpu
 from jax.sharding import Mesh
 from jax.sharding import PartitionSpec as P
 
@@ -15,8 +19,250 @@
 SWAP = ((0, 1), (1, 0))
 
 
-def gelu_tanh(v):
-    return jax.nn.gelu(v, approximate=True)
+BUSY = 24 * 2**20
+GELU_IN = 0.7978845608028654
+GELU_CUBE = 0.044715
+NT = (((1,), (1,)), ((), ()))
+
+
+def twice_gelu(v):
+    return v * (1.0 + jnp.tanh(v * (GELU_IN + (GELU_IN * GELU_CUBE) * (v * v))))
+
+
+def whole(*shape):
+    return pl.BlockSpec(shape, lambda *_: (0,) * len(shape))
+
+
+def fetch(source, held, sems):
+    count = sems.shape[0]
+    deep = held.shape[0] // count
+    copies = []
+    for i in range(count):
+        at = pl.ds(i * deep, deep)
+        copies.append(pltpu.make_async_copy(source.at[at], held.at[at], sems.at[i]))
+        copies[i].start()
+    return copies
+
+
+def forward_kernel(normed_ref, weights_ref, head_ref, slope_ref, part_ref, held, total, sems):
+    copies = fetch(weights_ref, held, sems)
+    steps = 4
+    each = len(copies) // steps
+    half, cols = held.shape[0], total.shape[1]
+    deep = half // steps
+    for step in range(steps):
+        for copy in copies[step * each : (step + 1) * each]:
+            copy.wait()
+        first = slice(step * deep, (step + 1) * deep)
+        second = slice(half + step * deep, half + (step + 1) * deep)
+        term = jnp.dot(normed_ref[:, first], held[first, :cols], preferred_element_type=F32)
+        term += jnp.dot(normed_ref[:, second], held[first, cols:], preferred_element_type=F32)
+        if step == 0:
+            total[...] = term
+        else:
+            total[...] += term
+    v = total[...]
+    square = v * v
+    tanh = jnp.tanh(v * (GELU_IN + (GELU_IN * GELU_CUBE) * square))
+    cdf = 0.5 + 0.5 * tanh
+    bend = v * (1.0 - tanh * tanh) * (0.5 * GELU_IN + (1.5 * GELU_IN * GELU_CUBE) * square)
+    slope = cdf + bend
+    slope_ref[...] = slope
+    head = head_ref[...]
+    width = head.shape[1]
+    part_ref[:, :width] = jnp.dot(
+        (v * cdf).astype(BF16), head, preferred_element_type=F32
+    ).astype(BF16)
+    part_ref[:, width:] = jnp.dot(
+        (v * slope).astype(BF16), head, preferred_element_type=F32
+    ).astype(BF16)
+
+
+def forward(normed, gen_full, gen_head):
+    rows, width = normed.shape
+    cols, latent_width = gen_head.shape
+    vmem = pl.BlockSpec(memory_space=pltpu.VMEM)
+    return pl.pallas_call(
+        forward_kernel,
+        in_specs=[vmem, pl.BlockSpec(memory_space=pltpu.HBM), vmem],
+        out_specs=[vmem, vmem],
+        out_shape=[
+            jax.ShapeDtypeStruct((rows, cols), F32),
+            jax.ShapeDtypeStruct((rows, 2 * latent_width), BF16),
+        ],
+        scratch_shapes=[
+            pltpu.VMEM(gen_full.shape, BF16),
+            pltpu.VMEM((rows, cols), F32),
+            pltpu.SemaphoreType.DMA((8,)),
+        ],
+        compiler_params=pltpu.CompilerParams(vmem_limit_bytes=BUSY),
+        cost_estimate=pl.CostEstimate(
+            flops=2 * rows * width * cols, bytes_accessed=2 * width * cols, transcendentals=0
+        ),
+        name="forward",
+    )(normed, gen_full, gen_head)
+
+
+def block_at(ref, row, col, rows, cols):
+    row = pl.multiple_of(row * rows, rows)
+    col = pl.multiple_of(col * cols, cols)
+    return ref.at[pl.ds(row, rows), pl.ds(col, cols)]
+
+
+def store_slice(grad_values, held, copies, out_ref):
+    deep = held.shape[0] // len(copies)
+    for i, copy in enumerate(copies):
+        copy.wait()
+        at = slice(i * deep, (i + 1) * deep)
+        out_ref[:, at] = lax.dot_general(
+            grad_values, held[at, :], NT, preferred_element_type=F32
+        ).astype(BF16)
+
+
+def critic_kernel(
+    width,
+    place_ref,
+    tsteps_ref,
+    mix_ref,
+    weight_ref,
+    parts_ref,
+    noise_ref,
+    gram_ref,
+    matrix_ref,
+    head_ref,
+    gen_head_ref,
+    slope_ref,
+    weights_ref,
+    latent_ref,
+    values_ref,
+    mixed_ref,
+    far_ref,
+    held,
+    sems,
+):
+    columns, cols = held.shape[1:]
+    copies = []
+    for i in range(2):
+        source = block_at(weights_ref, place_ref[1 + 2 * i], place_ref[2 + 2 * i], columns, cols)
+        copies.append(fetch(source, held.at[i], sems.at[i]))
+    level = tsteps_ref[place_ref[0]]
+    parts = parts_ref[...].astype(F32)
+    parts = parts[0] + parts[1] + parts[2] + parts[3]
+    latent_width = latent_ref.shape[1]
+    latent = parts[:, :latent_width].astype(BF16)
+    latent_ref[...] = latent
+    noisy = mix_ref[0, level] * latent.astype(F32) + mix_ref[1, level] * noise_ref[...]
+    noisy = noisy.astype(BF16)
+    exact = noisy.astype(F32)
+    rows = noisy.shape[0]
+    scales = []
+    for which in range(2):
+        turned = jnp.dot(
+            exact, gram_ref[which], precision=lax.Precision.HIGHEST, preferred_element_type=F32
+        )
+        square = jnp.sum(turned * exact, axis=1, keepdims=True) / width
+        scales.append(lax.rsqrt(jnp.maximum(square, 0.0) + 1e-06))
+    blocks = matrix_ref.shape[0]
+    gap = jnp.zeros((rows, latent_width), F32)
+    for i in range(blocks):
+        own = jnp.dot(noisy, matrix_ref[i], preferred_element_type=F32)
+        act = twice_gelu(own * scales[i * 2 // blocks]).astype(BF16)
+        gap = gap + lax.dot_general(act, head_ref[i], NT, preferred_element_type=F32)
+    cotangent = (weight_ref[0, level] * (0.5 * gap)).astype(BF16)
+    cot = cotangent.astype(F32)
+    mixed_ref[...] = jnp.sum(cot * parts[:, latent_width:], axis=1, keepdims=True)
+    grad_act = lax.dot_general(cotangent, gen_head_ref[...], NT, preferred_element_type=F32)
+    grad_values = (slope_ref[...] * grad_act).astype(BF16)
+    values_ref[...] = grad_values
+    for i in range(2):
+        store_slice(grad_values, held.at[i], copies[i], far_ref.at[i])
+
+
+def critics(width, place, tables, parts, own_noise, gram, matrix, head, gen_head, slope, gen_full):
+    rows, cols = slope.shape
+    latent_width = gen_head.shape[1]
+    columns = gen_full.shape[0] // 2
+    smem = pl.BlockSpec(memory_space=pltpu.SMEM)
+    vmem = pl.BlockSpec(memory_space=pltpu.VMEM)
+    return pl.pallas_call(
+        functools.partial(critic_kernel, width),
+        in_specs=[smem] * 4 + [vmem] * 7 + [pl.BlockSpec(memory_space=pltpu.HBM)],
+        out_specs=[vmem] * 4,
+        out_shape=[
+            jax.ShapeDtypeStruct((rows, latent_width), BF16),
+            jax.ShapeDtypeStruct((rows, cols), BF16),
+            jax.ShapeDtypeStruct((rows, 1), F32),
+            jax.ShapeDtypeStruct((2, rows, columns), BF16),
+        ],
+        scratch_shapes=[
+            pltpu.VMEM((2, columns, cols), BF16),
+            pltpu.SemaphoreType.DMA((2, 2)),
+        ],
+        compiler_params=pltpu.CompilerParams(vmem_limit_bytes=BUSY),
+        name="critics",
+    )(place, *tables, parts, own_noise, gram, matrix, head, gen_head, slope, gen_full)
+
+
+def slices_kernel(place_ref, values_ref, weights_ref, out_ref, held, sems):
+    columns, cols = held.shape[1:]
+    copies = []
+    for i in range(2):
+        source = block_at(weights_ref, place_ref[2 * i], place_ref[2 * i + 1], columns, cols)
+        copies.append(fetch(source, held.at[i], sems.at[i]))
+    for i in range(2):
+        store_slice(values_ref[...], held.at[i], copies[i], out_ref.at[i])
+
+
+def grad_slices(place, grad_values, gen_full):
+    rows, cols = grad_values.shape
+    columns = gen_full.shape[0] // 2
+    vmem = pl.BlockSpec(memory_space=pltpu.VMEM)
+    return pl.pallas_call(
+        slices_kernel,
+        in_specs=[
+            pl.BlockSpec(memory_space=pltpu.SMEM),
+            vmem,
+            pl.BlockSpec(memory_space=pltpu.HBM),
+        ],
+        out_specs=vmem,
+        out_shape=jax.ShapeDtypeStruct((2, rows, columns), BF16),
+        scratch_shapes=[
+            pltpu.VMEM((2, columns, cols), BF16),
+            pltpu.SemaphoreType.DMA((2, 2)),
+        ],
+        compiler_params=pltpu.CompilerParams(vmem_limit_bytes=BUSY),
+        cost_estimate=pl.CostEstimate(
+            flops=4 * rows * cols * columns,
+            bytes_accessed=4 * cols * columns,
+            transcendentals=0,
+        ),
+        name="grad_slices",
+    )(place, grad_values, gen_full)
+
+
+def finish_kernel(near_ref, far_ref, inverse_ref, gain_ref, out_ref):
+    far = far_ref[...].astype(F32) * (inverse_ref[...] * gain_ref[...])
+    out_ref[...] = (near_ref[...] + far).astype(BF16)
+
+
+def finish(near, far, inverse, gain):
+    rows, columns = near.shape
+    steps = 2
+    part = pl.BlockSpec((rows // steps, columns), lambda i: (i, 0))
+    return pl.pallas_call(
+        finish_kernel,
+        grid=(steps,),
+        in_specs=[
+            part,
+            part,
+            pl.BlockSpec((rows // steps, 1), lambda i: (i, 0)),
+            whole(1, columns),
+        ],
+        out_specs=part,
+        out_shape=jax.ShapeDtypeStruct((rows, columns), BF16),
+        compiler_params=pltpu.CompilerParams(vmem_limit_bytes=16 * 2**20),
+        name="finish",
+    )(near, far, inverse, gain)
 
 
 def to_tiles(x, tiles):
@@ -45,7 +291,7 @@
 ):
     rows, width = hidden.shape
     latent_width = gen_head.shape[1]
-    depth, gen_cols = gen_value.shape
+    depth = gen_value.shape[0]
     seq_count = lax.axis_size(SEQ)
     group_id, seq_id = lax.axis_index("group"), lax.axis_index(SEQ)
     yl, c = lax.axis_index("y_lo"), lax.axis_index("core")
@@ -54,6 +300,7 @@
     with jax.named_scope("gather_value"):
         gen_pair = lax.all_gather(gen_value, "y_hi", axis=1, tiled=True)
         gen_full = lax.all_gather(gen_pair, "z", axis=0, tiled=True)
+        gen_full = pltpu.with_memory_space_constraint(gen_full, pltpu.HBM)
 
     with jax.named_scope("critic_matrix_part"):
         cols = critic_value.shape[1]
@@ -107,71 +354,54 @@
         )
 
     with jax.named_scope("critic_gather"):
-        matrix = lax.all_gather(matrix, ("group",) + TP, axis=1, tiled=True)
-        head = jnp.where(critic_id == 1, critic_head, -critic_head)
-        head = lax.all_gather(head, ("group",) + TP, axis=0, tiled=True)
-
-    with jax.named_scope("levels"):
-        level = tsteps[shard_id * rows // FTOK]
-        signal_mix, noise_part = noise_mix[0, level], noise_mix[1, level] * own_noise
-        weight = gap_weight[level]
+        matrix = lax.all_gather(matrix, ("group",) + TP, axis=0)
+        head = jnp.where(critic_id == 1, critic_head, -critic_head).T
+        head = lax.all_gather(head, ("group",) + TP, axis=0)
+        gram = lax.dot_general(
+            critic_embed, critic_embed, (((2,), (2,)), ((0,), (0,))), preferred_element_type=F32
+        )
 
     with jax.named_scope("forward"):
         inputs = hidden.astype(F32)
         inverse = lax.rsqrt(jnp.mean(inputs * inputs, axis=-1, keepdims=True) + 1e-06)
         normed = (inputs * inverse * norm_gain.astype(F32)).astype(BF16)
-        half = width // 2
-        values = jnp.dot(
-            normed[:, :half], gen_full[:, :gen_cols], preferred_element_type=F32
-        ) + jnp.dot(normed[:, half:], gen_full[:, gen_cols:], preferred_element_type=F32)
-        activated, gelu_back = jax.vjp(gelu_tanh, values)
-        latent_part = jnp.dot(activated.astype(BF16), gen_head, preferred_element_type=F32)
-        parts = lax.all_gather(latent_part.astype(BF16), TP, axis=0)
-        gen_latent = jnp.sum(parts.astype(F32), axis=0).astype(BF16)
-        slope = gelu_back(jnp.ones_like(values))[0]
+        slope, part = forward(normed, gen_full, gen_head)
+        parts = lax.all_gather(part, TP, axis=0)
 
     with jax.named_scope("critics"):
-        noisy = (signal_mix * gen_latent.astype(F32) + noise_part).astype(BF16)
-        raw = jnp.dot(noisy, matrix, preferred_element_type=F32)
-        split = raw.shape[1] // 2
-        acts = []
-        for which in range(2):
-            embedded = jnp.dot(noisy, critic_embed[which], preferred_element_type=F32)
-            scale_rows = lax.rsqrt(jnp.mean(embedded * embedded, axis=-1, keepdims=True) + 1e-06)
-            own = raw[:, which * split : (which + 1) * split] * scale_rows
-            acts.append(gelu_tanh(own).astype(BF16))
-        gap = jnp.dot(jnp.concatenate(acts, axis=1), head, preferred_element_type=F32)
-        cotangent = (weight * gap).astype(BF16)
+        frame = shard_id * rows // FTOK
+        place = jnp.stack([frame, 1 - c, 1 - yl, 1 - c, yl]).astype(jnp.int32)
+        tables = (tsteps, noise_mix, gap_weight[None, :])
+        gen_latent, grad_values, mixed, far = critics(
+            width,
+            place,
+            tables,
+            parts,
+            own_noise,
+            gram,
+            matrix,
+            head,
+            gen_head,
+            slope,
+            gen_full,
+        )
 
     with jax.named_scope("backward"):
-        grad_act = lax.dot_general(
-            cotangent, gen_head, (((1,), (1,)), ((), ())), preferred_element_type=F32
-        )
-        grad_values = (slope * grad_act).astype(BF16)
-        mixed = jnp.sum(grad_values.astype(F32) * values, axis=1)
-        mixed = mixed + lax.ppermute(mixed, "core", SWAP)
-        mixed = mixed + lax.ppermute(mixed, "y_lo", SWAP)
         columns = width // 4
-
-        def grad_slice(at_y, at_c):
-            weights = lax.dynamic_slice(
-                gen_full, (at_c * columns, at_y * gen_cols), (columns, gen_cols)
-            )
-            return lax.dot_general(
-                grad_values, weights, (((1,), (1,)), ((), ())), preferred_element_type=F32
-            )
-
-        far = lax.ppermute(grad_slice(1 - yl, 1 - c).astype(BF16), "core", SWAP)
-        far = (grad_slice(1 - yl, c) + far.astype(F32)).astype(BF16)
-        far = lax.ppermute(far, "y_lo", SWAP)
-        near = lax.ppermute(grad_slice(yl, 1 - c).astype(BF16), "core", SWAP)
-        near = grad_slice(yl, c) + near.astype(F32)
-        grad_normed = near + far.astype(F32)
         first = (yl * 2 + c) * columns
         gain = lax.dynamic_slice_in_dim(norm_gain, first, columns, 0).astype(F32)
         own = lax.dynamic_slice_in_dim(hidden, first, columns, 1).astype(F32)
-        pulled = inverse * inverse * (mixed / width)[:, None]
-        grad_hidden = (inverse * (grad_normed * gain) - own * pulled).astype(BF16)
+        slope_out = inverse * gain[None, :]
+        pulled = inverse * inverse * (mixed / width)
+        got = lax.ppermute(far, "core", SWAP)
+        places = jnp.stack([c, 1 - yl, c, yl])
+        slices = grad_slices(places.astype(jnp.int32), grad_values, gen_full)
+        far = (slices[0].astype(F32) + got[0].astype(F32)).astype(BF16)
+        far, slices, got, pulled = lax.optimization_barrier((far, slices, got, pulled))
+        far = lax.ppermute(far, "y_lo", SWAP)
+        near = slices[1].astype(F32) + got[1].astype(F32)
+        near = slope_out * near - own * pulled
+        grad_hidden = finish(near, far, inverse, gain[None, :])
     return (gen_latent, grad_hidden)
 
 

time: 190 us -> 178 us (0.937)
  matrix products: 29.5 us -> 6.7 us
  Pallas kernels: 0 us -> 19 us
  starting transfers between devices: 34.1 us -> 26.5 us
  other arithmetic: 13.7 us -> 7.9 us
  waiting for transfers between devices: 23.3 us -> 28.5 us
  blocking collectives: 59.9 us -> 62.3 us
  between operations: 16.4 us -> 14.4 us
    dot_general x11 -> x1, matrix products: 26 us -> 3 us  [local(): lax.dot_general(critic_embed, critic_embed, (((2,), (2,)), ((0,), (0,))),...]
    pallas_call x0 -> x4, Pallas kernels: none -> 19 us  [the longest x1 8.99 us: critics(): pl.pallas_call(functools.partial(critic_kernel, width), in_specs=[smem] *...]
    ppermute x1, waiting for transfers between devices: 0.01 us -> 13.2 us  [local(): far = lax.ppermute(far, 'y_lo', SWAP)]
    ppermute x4 -> x1, waiting for transfers between devices: 7.84 us -> 0.01 us  [local(): got = lax.ppermute(far, 'core', SWAP)]
    ppermute x4 -> x1, starting transfers between devices: 9.64 us -> 2.07 us  [local(): got = lax.ppermute(far, 'core', SWAP)]
    convert_element_type x2 -> x1, other arithmetic: 5.67 us -> 0.99 us  [local(): far = (slices[0].astype(F32) + got[0].astype(F32)).astype(BF16)]
    dynamic_slice x3 -> x0, local copies, waits for them, and re-layouts: 3.23 us -> none  [the longest x1 1.37 us: local(): noise_mix[0, level]]
    all_gather x3, blocking collectives: 50.2 us -> 52.7 us  [the longest x1 24.6 us: local(): head = lax.all_gather(head, ('group',) + TP, axis=0)]
  transfers between devices with their start and end apart: 8 -> 5, of which waited for: 3 -> 3; matrix products, arithmetic and copies ran while one was open for 15% -> 13% of each run, Pallas kernels for 0% -> 2%
where the time goes in v3:
time: 178 us; the launch traced here: 177 us
  blocking collectives  62.3 us (35%)
  waiting for transfers between devices  28.5 us (16%)
  starting transfers between devices  26.5 us (15%)
  Pallas kernels  19 us (11%)
  between operations  14.4 us (8%)
  local copies, waits for them, and re-layouts  11.8 us (7%)
  other arithmetic  7.9 us (4%)
  matrix products  6.7 us (4%)
    all_gather x1, blocking collectives, local(): head = lax.all_gather(head, ('group',) + TP, axis=0)  24.6 us
    all_to_all x2, starting transfers between devices, swap_all(): return lax.all_to_all(x, SEQ, split_axis=0, concat_axis=0, tiled=True)  22.2 us
    all_gather x1, blocking collectives, local(): matrix = lax.all_gather(matrix, ('group',) + TP, axis=0)  20 us
    ppermute x1, waiting for transfers between devices, local(): far = lax.ppermute(far, 'y_lo', SWAP)  13.2 us
    all_to_all x2, waiting for transfers between devices, swap_all(): return lax.all_to_all(x, SEQ, split_axis=0, concat_axis=0, tiled=True)  10.4 us
    all_gather x1, blocking collectives, local(): gen_pair = lax.all_gather(gen_value, 'y_hi', axis=1, tiled=True)  9.61 us
    pallas_call x1, Pallas kernels, critics(): pl.pallas_call(functools.partial(critic_kernel, width), in_specs=[smem] *...  8.99 us
    all_gather x1, blocking collectives, local(): parts = lax.all_gather(part, TP, axis=0)  8.04 us
  transfers between devices with their start and end apart: 5, of which 3 were waited for; matrix products, arithmetic and copies ran while one was open for 13% of the time, Pallas kernels for 2%

profile of v3, /device:TPU:1, one launch (start us, length us, event | category | flops | bytes accessed | tf_op | source)
XLA Modules:
  0.0 177.2 jit_solution(10386284842009116394)
XLA Ops:
  7.2 0.0 copy-start
  7.2 0.0 copy-start.10
  7.2 0.0 copy-start.13
  7.2 0.0 all-gather.4.cloned.1.call-start
  7.2 9.6 %all_gather.21 = bf16[160,1280]{1,0:T(8,128)(2,1)} all-gather(bf16[160,640]{1,0:T(8,128)(2,1)} %param.15), channel_id=1, replica_groups=mesh['group'=4,'y_hi'=2,'z'=16,'y_lo'=2,'core'=2] {'y_hi'}, dimensions={1}, use_global_device_ids=true | all-gather | bytes 614400 | tf_op jit(solution)/shard_map/gather_value/all_gather | solution.py:301
  16.9 0.0 all-gather.4.cloned.1.call-update
  16.9 0.7 and_select_fusion.1
  17.6 0.2 fusion.9
  17.8 0.0 copy-start.16
  17.8 0.1 select_reduce_fusion
  18.0 0.1 convert_element_type.94
  18.1 0.8 dynamic-slice_convert_fusion.1
  18.8 1.1 fusion.16
  19.9 0.1 reshape.85
  20.0 0.7 copy.44
  20.7 17.6 %all-to-all-start = ((f32[32,8,128]{2,1,0:T(8,128)}), f32[32,8,128]{2,1,0:T(8,128)S(1)}, u32[]{:S(2)}, u32[]{:S(2)}) async-start(f32[32,8,128]{2,1,0:T(8,128)} %bitcast.16), calls=%async_computation | async-start | bytes 262144 | tf_op jit(solution)/shard_map/first_exchange/all_to_all | solution.py:274
  38.3 0.0 copy-start.8
  38.4 2.5 %fusion = f32[256]{0:T(256)S(1)} fusion(bf16[256,5120]{1,0:T(8,128)(2,1)} %param.13), kind=kLoop, calls=%fused_computation.2 | loop fusion | flops 3931904 | bytes 2622464 | tf_op jit(solution)/shard_map/forward/reduce_sum | solution.py:366
  40.9 0.1 copy-done.8
  40.9 0.8 fusion.2.normed_ref
  41.7 0.1 copy-done.11
  41.8 0.8 copy.35.head_ref.gen_head_ref
  42.6 0.1 stack.29.place_ref
  42.7 3.0 %fusion.25.gram_ref = f32[2,64,64]{2,1,0:T(8,128)} fusion(bf16[2,64,5120]{2,1,0:T(8,128)(2,1)} %param.17), kind=kOutput, calls=%fused_computation.56 | convolution fusion | flops 83886080 | bytes 1343488 | tf_op jit(solution)/shard_map/critic_gather/dot_general | solution.py:360
  45.7 10.4 %all-to-all-done = f32[32,8,128]{2,1,0:T(8,128)S(1)} async-done(((f32[32,8,128]{2,1,0:T(8,128)}), f32[32,8,128]{2,1,0:T(8,128)S(1)}, u32[]{:S(2)}, u32[]{:S(2)}) %all-to-all-start) | async-done | bytes 131104 | tf_op jit(solution)/shard_map/first_exchange/all_to_all | solution.py:274
  56.1 0.1 eq.52
  56.2 0.5 fusion.6
  56.8 0.1 copy.36
  56.9 0.1 reshape.88
  57.1 0.7 copy.46
  57.8 4.6 %all-to-all-start.1 = ((bf16[32,16,128]{2,1,0:T(8,128)(2,1)}), bf16[32,16,128]{2,1,0:T(8,128)(2,1)}, u32[]{:S(2)}, u32[]{:S(2)}) async-start(bf16[32,16,128]{2,1,0:T(8,128)(2,1)} %bitcast.20), calls=%async_computation.1 | async-start | bytes 262144 | tf_op jit(solution)/shard_map/second_exchange/all_to_all | solution.py:274
  62.4 24.6 %all-gather.1 = bf16[1024,320]{1,0:T(8,128)(2,1)S(1)} all-gather(bf16[64,320]{1,0:T(8,128)(2,1)S(1)} %fusion.17), channel_id=3, replica_groups=mesh['group'=4,'y_hi'=2,'z'=16,'y_lo'=2,'core'=2] {'group','y_lo','core'}, dimensions={0}, use_global_device_ids=true | all-gather | bytes 696320 | tf_op jit(solution)/shard_map/critic_gather/all_gather | solution.py:359
  87.0 0.0 all-to-all-done.1
  87.0 0.9 copy.50
  88.0 0.6 slice.34
  88.6 0.6 slice.35
  89.2 1.7 reshape.91
  90.9 1.5 reshape.92
  92.4 1.9 %fusion.13.noise_ref = f32[256,64]{1,0:T(8,128)} fusion(bf16[512,64]{1,0:T(8,128)(2,1)} %reshape.91, s32[256]{0:T(256)} %copy-done.16), kind=kOutput, calls=%fused_computation.18 | convolution fusion | flops 16908288 | bytes 132096 | tf_op jit(solution)/shard_map/second_exchange/dot_general | solution.py:352
  94.3 20.0 %all_gather.25.matrix_ref = bf16[16,64,320]{2,1,0:T(8,128)(2,1)} all-gather(bf16[1,64,320]{2,1,0:T(8,128)(2,1)} %reshape.92), channel_id=1, replica_groups=mesh['group'=4,'y_hi'=2,'z'=16,'y_lo'=2,'core'=2] {'group','y_lo','core'}, dimensions={0}, use_global_device_ids=true | all-gather | bytes 696320 | tf_op jit(solution)/shard_map/critic_gather/all_gather | solution.py:357
  114.3 4.9 %all-gather.4.cloned.1.call-done.weights_ref = bf16[2560,1280]{1,0:T(8,128)(2,1)} async-done(((bf16[160,1280]{1,0:T(8,128)(2,1)}), bf16[2560,1280]{1,0:T(8,128)(2,1)}) %all-gather.4.cloned.1.call-update) | async-done | bytes 6553616 | tf_op jit(solution)/shard_map/gather_value/all_gather | solution.py:302
  119.2 0.9 copy-done.2
  120.1 0.0 copy-start.6
  120.2 0.0 copy-start.7
  120.2 5.0 %forward.1 = (f32[256,640]{1,0:T(8,128)S(1)}, bf16[256,128]{1,0:T(8,128)(2,1)S(1)}) custom-call(bf16[256,5120]{1,0:T(8,128)(2,1)S(1)} %fusion.2.normed_ref, bf16[2560,1280]{1,0:T(8,128)(2,1)} %all-gather.4.cloned.1.call-done.weights_ref, bf16[640,64]{1,0:T(8,128)(2,1)S(1)} %copy-done.2), custom_call_target="tpu_custom_call" | custom-call | flops 1677721600 | bytes 6553600 | tf_op jit(solution)/shard_map/forward/forward/pallas_call | solution.py:85
  125.2 8.0 %all-gather = bf16[1024,128]{1,0:T(8,128)(2,1)S(1)} all-gather(bf16[256,128]{1,0:T(8,128)(2,1)S(1)} %get-tuple-element.12), channel_id=2, replica_groups=mesh['group'=4,'y_hi'=2,'z'=16,'y_lo'=2,'core'=2] {'y_lo','core'}, dimensions={0}, use_global_device_ids=true | all-gather | bytes 327680 | tf_op jit(solution)/shard_map/forward/all_gather | solution.py:369
  133.3 0.0 copy-done.1
  133.3 9.0 %critics.1 = (bf16[256,64]{1,0:T(8,128)(2,1)S(1)}, bf16[256,640]{1,0:T(8,128)(2,1)S(1)}, f32[256,1]{1,0:T(8,128)S(1)}, bf16[2,256,1280]{2,1,0:T(8,128)(2,1)}) custom-call(s32[5]{0:T(128)S(1)} %stack.29.place_ref, s32[16]{0:T(128)S(1)} %copy-done.7, f32[2,1000]{1,0:T(2,128)S(1)} %copy-done.5, f32[1,1000]{1,0:T(1,128)S(1)} %bitcast.45, ...), custom_call_target="tpu_custom_call" | custom-call | tf_op jit(solution)/shard_map/critics/critics/pallas_call | solution.py:187
  142.3 2.1 %collective-permute-start = (bf16[2,256,1280]{2,1,0:T(8,128)(2,1)}, bf16[2,256,1280]{2,1,0:T(8,128)(2,1)S(1)}, u32[]{:S(2)}, u32[]{:S(2)}) collective-permute-start(bf16[2,256,1280]{2,1,0:T(8,128)(2,1)} %get-tuple-element.16), channel_id=1, source_target_pairs={{0,1},{1,0},{2,3},{3,2},{4,5},{5,4},{6,7},{7,6},{8,9},{9,8},{10,11... | collective-permute-start | bytes 3932168 | tf_op jit(solution)/shard_map/backward/ppermute | solution.py:396
  144.4 0.7 copy.39.inverse_ref
  145.1 0.1 pad_add_fusion.place_ref
  145.2 3.9 %grad_slices.1 = bf16[2,256,1280]{2,1,0:T(8,128)(2,1)S(1)} custom-call(s32[4]{0:T(128)S(1)} %pad_add_fusion.place_ref, bf16[256,640]{1,0:T(8,128)(2,1)S(1)} %get-tuple-element.15.values_ref, bf16[2560,1280]{1,0:T(8,128)(2,1)} %all-gather.4.cloned.1.call-done.weights_ref), custom_call_target="tpu_custom_call" | custom-call | flops 838860800 | bytes 3276800 | tf_op jit(solution)/shard_map/backward/grad_slices/pallas_call | solution.py:220
  149.1 0.0 copy-start.15
  149.2 0.0 collective-permute-done
  149.2 0.0 copy-start.9
  149.2 1.1 copy-done.9
  150.2 1.0 fusion.12
  151.2 2.2 %collective-permute-start.1 = (bf16[256,1280]{1,0:T(8,128)(2,1)}, bf16[256,1280]{1,0:T(8,128)(2,1)S(1)}, u32[]{:S(2)}, u32[]{:S(2)}) collective-permute-start(bf16[256,1280]{1,0:T(8,128)(2,1)} %fusion.12), channel_id=1, source_target_pairs={{0,2},{2,0},{1,3},{3,1},{4,6},{6,4},{5,7},{7,5},{8,10},{10,8},{9,1... | collective-permute-start | bytes 1966088 | tf_op jit(solution)/shard_map/backward/ppermute | solution.py:401
  153.5 0.1 dynamic-slice_convert_fusion
  153.6 0.7 copy.42
  154.3 0.1 reduce
  154.4 1.7 fusion.5.near_ref
  156.1 13.2 %collective-permute-done.1.far_ref = bf16[256,1280]{1,0:T(8,128)(2,1)S(1)} collective-permute-done((bf16[256,1280]{1,0:T(8,128)(2,1)}, bf16[256,1280]{1,0:T(8,128)(2,1)S(1)}, u32[]{:S(2)}, u32[]{:S(2)}) %collective-permute-start.1) | collective-permute-done | bytes 655392 | tf_op jit(solution)/shard_map/backward/ppermute | solution.py:401
  169.3 1.1 finish.1
  (35 shorter events, 0.2 us)
Async XLA Ops:
  7.2 49.0 %copy-start = (bf16[1024,64]{0,1:T(8,128)(2,1)S(1)}, bf16[1024,64]{0,1:T(8,128)(2,1)}, u32[]{:S(2)}) copy-start(bf16[1024,64]{0,1:T(8,128)(2,1)} %param.21) | copy-start | bytes 393220
  7.2 11.6 %copy-start.10 = (bf16[160,320]{1,0:T(8,128)(2,1)S(1)}, bf16[160,320]{1,0:T(8,128)(2,1)}, u32[]{:S(2)}) copy-start(bf16[160,320]{1,0:T(8,128)(2,1)} %param.19) | copy-start | bytes 307204
  7.2 31.1 %copy-start.13 = (bf16[5120]{0:T(1024)(128)(2,1)S(1)}, bf16[5120]{0:T(1024)(128)(2,1)}, u32[]{:S(2)}) copy-start(bf16[5120]{0:T(1024)(128)(2,1)} %param.14) | copy-start | bytes 30724
  7.2 112.0 %all-gather.4.cloned.1.call-start = ((), (), s32[]{:S(2)}) async-start(), calls=%async_computation.2 | async-start | bytes 6963200 | tf_op jit(solution)/shard_map/gather_value/all_gather | solution.py:302
  17.8 1.0 copy-start.16
  20.7 35.4 %all-to-all-start = ((f32[32,8,128]{2,1,0:T(8,128)}), f32[32,8,128]{2,1,0:T(8,128)S(1)}, u32[]{:S(2)}, u32[]{:S(2)}) async-start(f32[32,8,128]{2,1,0:T(8,128)} %bitcast.16), calls=%async_computation | async-start | bytes 262144 | tf_op jit(solution)/shard_map/first_exchange/all_to_all | solution.py:274
  38.3 2.6 %copy-start.8 = (bf16[256,5120]{1,0:T(8,128)(2,1)S(1)}, bf16[256,5120]{1,0:T(8,128)(2,1)}, u32[]{:S(2)}) copy-start(bf16[256,5120]{1,0:T(8,128)(2,1)} %param.13) | copy-start | bytes 7864324
  40.9 0.8 copy-start.14
  40.9 0.9 copy-start.11
  45.7 16.7 %copy-start.12 = (bf16[320,64]{0,1:T(8,128)(2,1)S(1)}, bf16[320,64]{0,1:T(8,128)(2,1)}, u32[]{:S(2)}) copy-start(bf16[320,64]{0,1:T(8,128)(2,1)} %param.20) | copy-start | bytes 122884
  57.8 29.2 %all-to-all-start.1 = ((bf16[32,16,128]{2,1,0:T(8,128)(2,1)}), bf16[32,16,128]{2,1,0:T(8,128)(2,1)}, u32[]{:S(2)}, u32[]{:S(2)}) async-start(bf16[32,16,128]{2,1,0:T(8,128)(2,1)} %bitcast.20), calls=%async_computation.1 | async-start | bytes 262144 | tf_op jit(solution)/shard_map/second_exchange/all_to_all | solution.py:274
  119.2 0.9 copy-start.2
  120.1 13.1 %copy-start.1 = (bf16[16,64,320]{2,1,0:T(8,128)(2,1)S(1)}, bf16[16,64,320]{2,1,0:T(8,128)(2,1)}, u32[]{:S(2)}) copy-start(bf16[16,64,320]{2,1,0:T(8,128)(2,1)} %all_gather.25.matrix_ref) | copy-start | bytes 1966084
  120.1 13.1 %copy-start.3 = (f32[2,64,64]{2,1,0:T(8,128)S(1)}, f32[2,64,64]{2,1,0:T(8,128)}, u32[]{:S(2)}) copy-start(f32[2,64,64]{2,1,0:T(8,128)} %fusion.25.gram_ref) | copy-start | bytes 98308
  120.1 13.1 %copy-start.4 = (f32[256,64]{1,0:T(8,128)S(1)}, f32[256,64]{1,0:T(8,128)}, u32[]{:S(2)}) copy-start(f32[256,64]{1,0:T(8,128)} %fusion.13.noise_ref) | copy-start | bytes 196612
  120.1 13.1 %copy-start.5 = (f32[2,1000]{1,0:T(2,128)S(1)}, f32[2,1000]{1,0:T(2,128)}, u32[]{:S(2)}) copy-start(f32[2,1000]{1,0:T(2,128)} %mix_ref.1) | copy-start | bytes 24004
  120.1 13.1 %copy-start.6 = (f32[1000]{0:T(1024)S(1)}, f32[1000]{0:T(1024)}, u32[]{:S(2)}) copy-start(f32[1000]{0:T(1024)} %param.25) | copy-start | bytes 12004
  120.2 13.1 %copy-start.7 = (s32[16]{0:T(128)S(1)}, s32[16]{0:T(128)}, u32[]{:S(2)}) copy-start(s32[16]{0:T(128)} %tsteps_ref.1) | copy-start | bytes 196
  142.3 6.9 %collective-permute-start = (bf16[2,256,1280]{2,1,0:T(8,128)(2,1)}, bf16[2,256,1280]{2,1,0:T(8,128)(2,1)S(1)}, u32[]{:S(2)}, u32[]{:S(2)}) collective-permute-start(bf16[2,256,1280]{2,1,0:T(8,128)(2,1)} %get-tuple-element.16), channel_id=1, source_target_pairs={{0,1},{1,0},{2,3},{3,2},{4,5},{5,4},{6,7},{7,6},{8,9},{9,8},{10,11... | collective-permute-start | bytes 3932168 | tf_op jit(solution)/shard_map/backward/ppermute | solution.py:396
  149.1 5.3 %copy-start.15 = (f32[256]{0:T(256)S(1)}, f32[256]{0:T(256)}, u32[]{:S(2)}) copy-start(f32[256]{0:T(256)} %copy-done.14) | copy-start | bytes 3076
  149.2 1.1 copy-start.9
  151.2 18.1 %collective-permute-start.1 = (bf16[256,1280]{1,0:T(8,128)(2,1)}, bf16[256,1280]{1,0:T(8,128)(2,1)S(1)}, u32[]{:S(2)}, u32[]{:S(2)}) collective-permute-start(bf16[256,1280]{1,0:T(8,128)(2,1)} %fusion.12), channel_id=1, source_target_pairs={{0,2},{2,0},{1,3},{3,1},{4,6},{6,4},{5,7},{7,5},{8,10},{10,8},{9,1... | collective-permute-start | bytes 1966088 | tf_op jit(solution)/shard_map/backward/ppermute | solution.py:401
Sparse Core Ops, SparseCore 0:
  17.0 102.1 all-gather.3

commit v4 on v3

--- a/solution.py
+++ b/solution.py
@@ -44,8 +44,12 @@
     return copies
 
 
-def forward_kernel(normed_ref, weights_ref, head_ref, slope_ref, part_ref, held, total, sems):
+def forward_kernel(
+    normed_ref, weights_ref, head_ref, slope_ref, part_ref, held, head_held, total, sems, head_sem
+):
     copies = fetch(weights_ref, held, sems)
+    head_copy = pltpu.make_async_copy(head_ref, head_held, head_sem)
+    head_copy.start()
     steps = 4
     each = len(copies) // steps
     half, cols = held.shape[0], total.shape[1]
@@ -68,32 +72,36 @@
     bend = v * (1.0 - tanh * tanh) * (0.5 * GELU_IN + (1.5 * GELU_IN * GELU_CUBE) * square)
     slope = cdf + bend
     slope_ref[...] = slope
-    head = head_ref[...]
-    width = head.shape[1]
-    part_ref[:, :width] = jnp.dot(
-        (v * cdf).astype(BF16), head, preferred_element_type=F32
+    head_copy.wait()
+    head = head_held[...]
+    width = head.shape[0]
+    part_ref[:, :width] = lax.dot_general(
+        (v * cdf).astype(BF16), head, NT, preferred_element_type=F32
     ).astype(BF16)
-    part_ref[:, width:] = jnp.dot(
-        (v * slope).astype(BF16), head, preferred_element_type=F32
+    part_ref[:, width:] = lax.dot_general(
+        (v * slope).astype(BF16), head, NT, preferred_element_type=F32
     ).astype(BF16)
 
 
 def forward(normed, gen_full, gen_head):
     rows, width = normed.shape
-    cols, latent_width = gen_head.shape
+    latent_width, cols = gen_head.shape
     vmem = pl.BlockSpec(memory_space=pltpu.VMEM)
+    hbm = pl.BlockSpec(memory_space=pltpu.HBM)
     return pl.pallas_call(
         forward_kernel,
-        in_specs=[vmem, pl.BlockSpec(memory_space=pltpu.HBM), vmem],
-        out_specs=[vmem, vmem],
+        in_specs=[vmem, hbm, hbm],
+        out_specs=[vmem, vmem, vmem],
         out_shape=[
             jax.ShapeDtypeStruct((rows, cols), F32),
             jax.ShapeDtypeStruct((rows, 2 * latent_width), BF16),
+            jax.ShapeDtypeStruct(gen_full.shape, BF16),
         ],
         scratch_shapes=[
-            pltpu.VMEM(gen_full.shape, BF16),
+            pltpu.VMEM(gen_head.shape, BF16),
             pltpu.VMEM((rows, cols), F32),
             pltpu.SemaphoreType.DMA((8,)),
+            pltpu.SemaphoreType.DMA,
         ],
         compiler_params=pltpu.CompilerParams(vmem_limit_bytes=BUSY),
         cost_estimate=pl.CostEstimate(
@@ -103,19 +111,15 @@
     )(normed, gen_full, gen_head)
 
 
-def block_at(ref, row, col, rows, cols):
-    row = pl.multiple_of(row * rows, rows)
-    col = pl.multiple_of(col * cols, cols)
-    return ref.at[pl.ds(row, rows), pl.ds(col, cols)]
-
-
-def store_slice(grad_values, held, copies, out_ref):
-    deep = held.shape[0] // len(copies)
-    for i, copy in enumerate(copies):
-        copy.wait()
-        at = slice(i * deep, (i + 1) * deep)
-        out_ref[:, at] = lax.dot_general(
-            grad_values, held[at, :], NT, preferred_element_type=F32
+def store_slice(grad_values, weights_ref, row, col, out_ref):
+    rows, cols = out_ref.shape[1], grad_values.shape[1]
+    col = pl.ds(pl.multiple_of(col * cols, cols), cols)
+    parts = 2
+    deep = rows // parts
+    for i in range(parts):
+        at = pl.ds(pl.multiple_of(row * rows + i * deep, deep), deep)
+        out_ref[:, i * deep : (i + 1) * deep] = lax.dot_general(
+            grad_values, weights_ref[at, col], NT, preferred_element_type=F32
         ).astype(BF16)
 
 
@@ -134,17 +138,10 @@
     slope_ref,
     weights_ref,
     latent_ref,
-    values_ref,
     mixed_ref,
-    far_ref,
-    held,
-    sems,
+    sent_ref,
+    kept_ref,
 ):
-    columns, cols = held.shape[1:]
-    copies = []
-    for i in range(2):
-        source = block_at(weights_ref, place_ref[1 + 2 * i], place_ref[2 + 2 * i], columns, cols)
-        copies.append(fetch(source, held.at[i], sems.at[i]))
     level = tsteps_ref[place_ref[0]]
     parts = parts_ref[...].astype(F32)
     parts = parts[0] + parts[1] + parts[2] + parts[3]
@@ -171,73 +168,35 @@
     cotangent = (weight_ref[0, level] * (0.5 * gap)).astype(BF16)
     cot = cotangent.astype(F32)
     mixed_ref[...] = jnp.sum(cot * parts[:, latent_width:], axis=1, keepdims=True)
-    grad_act = lax.dot_general(cotangent, gen_head_ref[...], NT, preferred_element_type=F32)
+    grad_act = jnp.dot(cotangent, gen_head_ref[...], preferred_element_type=F32)
     grad_values = (slope_ref[...] * grad_act).astype(BF16)
-    values_ref[...] = grad_values
     for i in range(2):
-        store_slice(grad_values, held.at[i], copies[i], far_ref.at[i])
+        row, col = place_ref[1 + 2 * i], place_ref[2 + 2 * i]
+        store_slice(grad_values, weights_ref, row, col, sent_ref.at[i])
+    for i in range(2):
+        row, col = place_ref[5 + 2 * i], place_ref[6 + 2 * i]
+        store_slice(grad_values, weights_ref, row, col, kept_ref.at[i])
 
 
 def critics(width, place, tables, parts, own_noise, gram, matrix, head, gen_head, slope, gen_full):
     rows, cols = slope.shape
-    latent_width = gen_head.shape[1]
+    latent_width = gen_head.shape[0]
     columns = gen_full.shape[0] // 2
     smem = pl.BlockSpec(memory_space=pltpu.SMEM)
     vmem = pl.BlockSpec(memory_space=pltpu.VMEM)
     return pl.pallas_call(
         functools.partial(critic_kernel, width),
-        in_specs=[smem] * 4 + [vmem] * 7 + [pl.BlockSpec(memory_space=pltpu.HBM)],
+        in_specs=[smem] * 4 + [vmem] * 8,
         out_specs=[vmem] * 4,
         out_shape=[
             jax.ShapeDtypeStruct((rows, latent_width), BF16),
-            jax.ShapeDtypeStruct((rows, cols), BF16),
             jax.ShapeDtypeStruct((rows, 1), F32),
             jax.ShapeDtypeStruct((2, rows, columns), BF16),
-        ],
-        scratch_shapes=[
-            pltpu.VMEM((2, columns, cols), BF16),
-            pltpu.SemaphoreType.DMA((2, 2)),
+            jax.ShapeDtypeStruct((2, rows, columns), BF16),
         ],
         compiler_params=pltpu.CompilerParams(vmem_limit_bytes=BUSY),
         name="critics",
     )(place, *tables, parts, own_noise, gram, matrix, head, gen_head, slope, gen_full)
-
-
-def slices_kernel(place_ref, values_ref, weights_ref, out_ref, held, sems):
-    columns, cols = held.shape[1:]
-    copies = []
-    for i in range(2):
-        source = block_at(weights_ref, place_ref[2 * i], place_ref[2 * i + 1], columns, cols)
-        copies.append(fetch(source, held.at[i], sems.at[i]))
-    for i in range(2):
-        store_slice(values_ref[...], held.at[i], copies[i], out_ref.at[i])
-
-
-def grad_slices(place, grad_values, gen_full):
-    rows, cols = grad_values.shape
-    columns = gen_full.shape[0] // 2
-    vmem = pl.BlockSpec(memory_space=pltpu.VMEM)
-    return pl.pallas_call(
-        slices_kernel,
-        in_specs=[
-            pl.BlockSpec(memory_space=pltpu.SMEM),
-            vmem,
-            pl.BlockSpec(memory_space=pltpu.HBM),
-        ],
-        out_specs=vmem,
-        out_shape=jax.ShapeDtypeStruct((2, rows, columns), BF16),
-        scratch_shapes=[
-            pltpu.VMEM((2, columns, cols), BF16),
-            pltpu.SemaphoreType.DMA((2, 2)),
-        ],
-        compiler_params=pltpu.CompilerParams(vmem_limit_bytes=BUSY),
-        cost_estimate=pl.CostEstimate(
-            flops=4 * rows * cols * columns,
-            bytes_accessed=4 * cols * columns,
-            transcendentals=0,
-        ),
-        name="grad_slices",
-    )(place, grad_values, gen_full)
 
 
 def finish_kernel(near_ref, far_ref, inverse_ref, gain_ref, out_ref):
@@ -365,14 +324,16 @@
         inputs = hidden.astype(F32)
         inverse = lax.rsqrt(jnp.mean(inputs * inputs, axis=-1, keepdims=True) + 1e-06)
         normed = (inputs * inverse * norm_gain.astype(F32)).astype(BF16)
-        slope, part = forward(normed, gen_full, gen_head)
+        head_turned = gen_head.T
+        head_kept = pltpu.with_memory_space_constraint(head_turned, pltpu.HBM)
+        slope, part, gen_full = forward(normed, gen_full, head_kept)
         parts = lax.all_gather(part, TP, axis=0)
 
     with jax.named_scope("critics"):
         frame = shard_id * rows // FTOK
-        place = jnp.stack([frame, 1 - c, 1 - yl, 1 - c, yl]).astype(jnp.int32)
+        place = jnp.stack([frame, 1 - c, 1 - yl, 1 - c, yl, c, 1 - yl, c, yl]).astype(jnp.int32)
         tables = (tsteps, noise_mix, gap_weight[None, :])
-        gen_latent, grad_values, mixed, far = critics(
+        gen_latent, mixed, sent, kept = critics(
             width,
             place,
             tables,
@@ -381,7 +342,7 @@
             gram,
             matrix,
             head,
-            gen_head,
+            head_turned,
             slope,
             gen_full,
         )
@@ -393,13 +354,11 @@
         own = lax.dynamic_slice_in_dim(hidden, first, columns, 1).astype(F32)
         slope_out = inverse * gain[None, :]
         pulled = inverse * inverse * (mixed / width)
-        got = lax.ppermute(far, "core", SWAP)
-        places = jnp.stack([c, 1 - yl, c, yl])
-        slices = grad_slices(places.astype(jnp.int32), grad_values, gen_full)
-        far = (slices[0].astype(F32) + got[0].astype(F32)).astype(BF16)
-        far, slices, got, pulled = lax.optimization_barrier((far, slices, got, pulled))
+        got = lax.ppermute(sent, "core", SWAP)
+        far = (kept[0].astype(F32) + got[0].astype(F32)).astype(BF16)
+        far, kept, got = lax.optimization_barrier((far, kept, got))
         far = lax.ppermute(far, "y_lo", SWAP)
-        near = slices[1].astype(F32) + got[1].astype(F32)
+        near = kept[1].astype(F32) + got[1].astype(F32)
         near = slope_out * near - own * pulled
         grad_hidden = finish(near, far, inverse, gain[None, :])
     return (gen_latent, grad_hidden)

time: 178 us -> 172 us (0.966)
  Pallas kernels: 19 us -> 13.5 us
  waiting for transfers between devices: 28.5 us -> 31.5 us
  local copies, waits for them, and re-layouts: 11.8 us -> 8.97 us
    pallas_call x2 -> x1, Pallas kernels: 8.95 us -> 5.15 us  [forward(): pl.pallas_call(forward_kernel, in_specs=[vmem, hbm, hbm], out_specs=[vmem...]
    unnamed x41 -> x36, local copies, waits for them, and re-layouts: 6.04 us -> 3.17 us
  transfers between devices with their start and end apart: 5 -> 5, of which waited for: 3 -> 4; matrix products, arithmetic and copies ran while one was open for 13% -> 13% of each run, Pallas kernels for 2% -> 0%
where the time goes in v4:
time: 172 us; the launch traced here: 171 us
  blocking collectives  62.1 us (36%)
  waiting for transfers between devices  31.5 us (18%)
  starting transfers between devices  26.9 us (16%)
  between operations  14.4 us (8%)
  Pallas kernels  13.5 us (8%)
  local copies, waits for them, and re-layouts  8.97 us (5%)
  other arithmetic  6.81 us (4%)
  matrix products  6.7 us (4%)
    all_gather x1, blocking collectives, local(): head = lax.all_gather(head, ('group',) + TP, axis=0)  24.6 us
    all_to_all x2, starting transfers between devices, swap_all(): return lax.all_to_all(x, SEQ, split_axis=0, concat_axis=0, tiled=True)  22.2 us
    all_gather x1, blocking collectives, local(): matrix = lax.all_gather(matrix, ('group',) + TP, axis=0)  20 us
    ppermute x1, waiting for transfers between devices, local(): far = lax.ppermute(far, 'y_lo', SWAP)  13.9 us
    all_to_all x2, waiting for transfers between devices, swap_all(): return lax.all_to_all(x, SEQ, split_axis=0, concat_axis=0, tiled=True)  11.3 us
    all_gather x1, blocking collectives, local(): gen_pair = lax.all_gather(gen_value, 'y_hi', axis=1, tiled=True)  9.61 us
    all_gather x1, blocking collectives, local(): parts = lax.all_gather(part, TP, axis=0)  7.93 us
    pallas_call x1, Pallas kernels, critics(): pl.pallas_call(functools.partial(critic_kernel, width), in_specs=[smem] *...  7.23 us
  transfers between devices with their start and end apart: 5, of which 4 were waited for; matrix products, arithmetic and copies ran while one was open for 13% of the time, Pallas kernels for 0%

profile of v4, /device:TPU:1, one launch (start us, length us, event | category | flops | bytes accessed | tf_op | source)
XLA Modules:
  0.0 170.9 jit_solution(896319780671906208)
XLA Ops:
  7.2 0.0 copy-start
  7.2 0.0 copy-start.9
  7.2 0.0 copy-start.11
  7.2 0.0 all-gather.4.cloned.1.call-start
  7.2 9.6 %all_gather.21 = bf16[160,1280]{1,0:T(8,128)(2,1)} all-gather(bf16[160,640]{1,0:T(8,128)(2,1)} %param.15), channel_id=1, replica_groups=mesh['group'=4,'y_hi'=2,'z'=16,'y_lo'=2,'core'=2] {'y_hi'}, dimensions={1}, use_global_device_ids=true | all-gather | bytes 614400 | tf_op jit(solution)/shard_map/gather_value/all_gather | solution.py:260
  16.9 0.0 all-gather.4.cloned.1.call-update
  16.9 0.7 and_select_fusion.1
  17.6 0.2 fusion.9
  17.8 0.0 copy-start.14
  17.8 0.1 select_reduce_fusion
  18.0 0.1 convert_element_type.94
  18.0 0.8 dynamic-slice_convert_fusion.1
  18.8 0.0 copy-done.14
  18.8 0.0 copy-done.9
  18.8 1.1 fusion.16
  19.9 0.1 reshape.85
  20.0 0.7 copy.36
  20.7 17.6 %all-to-all-start = ((f32[32,8,128]{2,1,0:T(8,128)}), f32[32,8,128]{2,1,0:T(8,128)S(1)}, u32[]{:S(2)}, u32[]{:S(2)}) async-start(f32[32,8,128]{2,1,0:T(8,128)} %bitcast.17), calls=%async_computation | async-start | bytes 262144 | tf_op jit(solution)/shard_map/first_exchange/all_to_all | solution.py:233
  38.3 0.0 copy-done.11
  38.3 0.0 copy-start.8
  38.4 2.5 %fusion = f32[256]{0:T(256)S(1)} fusion(bf16[256,5120]{1,0:T(8,128)(2,1)} %param.13), kind=kLoop, calls=%fused_computation.2 | loop fusion | flops 3931904 | bytes 2622464 | tf_op jit(solution)/shard_map/forward/reduce_sum | solution.py:325
  40.9 0.1 copy-done.8
  40.9 0.8 fusion.2.normed_ref
  41.7 0.0 copy-done.12
  41.7 0.1 stack.27.place_ref
  41.8 3.0 %fusion.25.gram_ref = f32[2,64,64]{2,1,0:T(8,128)} fusion(bf16[2,64,5120]{2,1,0:T(8,128)(2,1)} %param.17), kind=kOutput, calls=%fused_computation.55 | convolution fusion | flops 83886080 | bytes 1343488 | tf_op jit(solution)/shard_map/critic_gather/dot_general | solution.py:319
  44.8 11.3 %all-to-all-done = f32[32,8,128]{2,1,0:T(8,128)S(1)} async-done(((f32[32,8,128]{2,1,0:T(8,128)}), f32[32,8,128]{2,1,0:T(8,128)S(1)}, u32[]{:S(2)}, u32[]{:S(2)}) %all-to-all-start) | async-done | bytes 131104 | tf_op jit(solution)/shard_map/first_exchange/all_to_all | solution.py:233
  56.2 0.1 eq.52
  56.2 0.0 copy-done
  56.2 0.5 fusion.6
  56.8 0.1 copy.29
  56.9 0.1 reshape.88
  57.2 0.7 copy.38
  57.8 4.6 %all-to-all-start.1 = ((bf16[32,16,128]{2,1,0:T(8,128)(2,1)}), bf16[32,16,128]{2,1,0:T(8,128)(2,1)}, u32[]{:S(2)}, u32[]{:S(2)}) async-start(bf16[32,16,128]{2,1,0:T(8,128)(2,1)} %bitcast.21), calls=%async_computation.1 | async-start | bytes 262144 | tf_op jit(solution)/shard_map/second_exchange/all_to_all | solution.py:233
  62.4 0.0 copy-done.10
  62.4 24.6 %all-gather.1 = bf16[1024,320]{1,0:T(8,128)(2,1)S(1)} all-gather(bf16[64,320]{1,0:T(8,128)(2,1)S(1)} %fusion.17), channel_id=3, replica_groups=mesh['group'=4,'y_hi'=2,'z'=16,'y_lo'=2,'core'=2] {'group','y_lo','core'}, dimensions={0}, use_global_device_ids=true | all-gather | bytes 696320 | tf_op jit(solution)/shard_map/critic_gather/all_gather | solution.py:318
  87.0 0.0 all-to-all-done.1
  87.0 0.9 copy.42
  88.0 0.6 slice.34
  88.6 0.6 slice.35
  89.2 1.7 reshape.91
  90.9 1.5 reshape.92
  92.3 1.9 %fusion.13.noise_ref = f32[256,64]{1,0:T(8,128)} fusion(bf16[512,64]{1,0:T(8,128)(2,1)} %reshape.91, s32[256]{0:T(256)} %copy-done.14), kind=kOutput, calls=%fused_computation.18 | convolution fusion | flops 16908288 | bytes 132096 | tf_op jit(solution)/shard_map/second_exchange/dot_general | solution.py:311
  94.2 20.0 %all_gather.25.matrix_ref = bf16[16,64,320]{2,1,0:T(8,128)(2,1)} all-gather(bf16[1,64,320]{2,1,0:T(8,128)(2,1)} %reshape.92), channel_id=1, replica_groups=mesh['group'=4,'y_hi'=2,'z'=16,'y_lo'=2,'core'=2] {'group','y_lo','core'}, dimensions={0}, use_global_device_ids=true | all-gather | bytes 696320 | tf_op jit(solution)/shard_map/critic_gather/all_gather | solution.py:316
  114.3 4.9 %all-gather.4.cloned.1.call-done.weights_ref = bf16[2560,1280]{1,0:T(8,128)(2,1)} async-done(((bf16[160,1280]{1,0:T(8,128)(2,1)}), bf16[2560,1280]{1,0:T(8,128)(2,1)}) %all-gather.4.cloned.1.call-update) | async-done | bytes 6553616 | tf_op jit(solution)/shard_map/gather_value/all_gather | solution.py:261
  119.2 0.0 copy-start.6
  119.2 0.0 copy-start.7
  119.2 5.2 %forward.1 = (f32[256,640]{1,0:T(8,128)S(1)}, bf16[256,128]{1,0:T(8,128)(2,1)S(1)}, bf16[2560,1280]{1,0:T(8,128)(2,1)S(1)}) custom-call(bf16[256,5120]{1,0:T(8,128)(2,1)S(1)} %fusion.2.normed_ref, bf16[2560,1280]{1,0:T(8,128)(2,1)} %all-gather.4.cloned.1.call-done.weights_ref, bf16[64,640]{1,0:T(8,128)(2,1)} %bitcast.46), custom_call_target="tpu_custom_call" | custom-call | flops 1677721600 | bytes 6553600 | tf_op jit(solution)/shard_map/forward/forward/pallas_call | solution.py:91
  124.4 7.9 %all-gather = bf16[1024,128]{1,0:T(8,128)(2,1)S(1)} all-gather(bf16[256,128]{1,0:T(8,128)(2,1)S(1)} %get-tuple-element.12), channel_id=2, replica_groups=mesh['group'=4,'y_hi'=2,'z'=16,'y_lo'=2,'core'=2] {'y_lo','core'}, dimensions={0}, use_global_device_ids=true | all-gather | bytes 327680 | tf_op jit(solution)/shard_map/forward/all_gather | solution.py:330
  132.3 0.0 copy-done.1
  132.3 0.0 copy-done.2
  132.3 0.0 copy-done.3
  132.4 7.2 %critics.1 = (bf16[256,64]{1,0:T(8,128)(2,1)S(1)}, f32[256,1]{1,0:T(8,128)S(1)}, bf16[2,256,1280]{2,1,0:T(8,128)(2,1)}, bf16[2,256,1280]{2,1,0:T(8,128)(2,1)S(1)}) custom-call(s32[9]{0:T(128)S(1)} %stack.27.place_ref, s32[16]{0:T(128)S(1)} %copy-done.7, f32[2,1000]{1,0:T(2,128)S(1)} %copy-done.5, f32[1,1000]{1,0:T(1,128)S(1)} %bitcast.48, ...), custom_call_target="tpu_custom_call" | custom-call | tf_op jit(solution)/shard_map/critics/critics/pallas_call | solution.py:187
  139.6 2.1 %collective-permute-start = (bf16[2,256,1280]{2,1,0:T(8,128)(2,1)}, bf16[2,256,1280]{2,1,0:T(8,128)(2,1)S(1)}, u32[]{:S(2)}, u32[]{:S(2)}) collective-permute-start(bf16[2,256,1280]{2,1,0:T(8,128)(2,1)} %get-tuple-element.17), channel_id=1, source_target_pairs={{0,1},{1,0},{2,3},{3,2},{4,5},{5,4},{6,7},{7,6},{8,9},{9,8},{10,11... | collective-permute-start | bytes 3932168 | tf_op jit(solution)/shard_map/backward/ppermute | solution.py:357
  141.7 0.8 copy.31.inverse_ref
  142.5 0.1 dynamic-slice_convert_fusion
  142.6 0.7 copy.34
  143.3 1.4 collective-permute-done
  144.8 0.2 fusion.12
  144.9 2.6 %collective-permute-start.1 = (bf16[256,1280]{1,0:T(8,128)(2,1)S(1)}, bf16[256,1280]{1,0:T(8,128)(2,1)S(1)}, u32[]{:S(2)}, u32[]{:S(2)}) collective-permute-start(bf16[256,1280]{1,0:T(8,128)(2,1)S(1)} %fusion.12), channel_id=1, source_target_pairs={{0,2},{2,0},{1,3},{3,1},{4,6},{6,4},{5,7},{7,5},{8,10},{10,8},{9,1... | collective-permute-start | bytes 1966088 | tf_op jit(solution)/shard_map/backward/ppermute | solution.py:360
  147.5 0.1 multiply_reduce_fusion
  147.7 1.5 fusion.5.near_ref
  149.1 13.9 %collective-permute-done.1.far_ref = bf16[256,1280]{1,0:T(8,128)(2,1)S(1)} collective-permute-done((bf16[256,1280]{1,0:T(8,128)(2,1)S(1)}, bf16[256,1280]{1,0:T(8,128)(2,1)S(1)}, u32[]{:S(2)}, u32[]{:S(2)}) %collective-permute-start.1) | collective-permute-done | bytes 655392 | tf_op jit(solution)/shard_map/backward/ppermute | solution.py:360
  163.0 1.1 finish.1
  (27 shorter events, 0.2 us)
Async XLA Ops:
  7.2 49.1 %copy-start = (bf16[1024,64]{0,1:T(8,128)(2,1)S(1)}, bf16[1024,64]{0,1:T(8,128)(2,1)}, u32[]{:S(2)}) copy-start(bf16[1024,64]{0,1:T(8,128)(2,1)} %param.21) | copy-start | bytes 393220
  7.2 11.6 %copy-start.9 = (bf16[160,320]{1,0:T(8,128)(2,1)S(1)}, bf16[160,320]{1,0:T(8,128)(2,1)}, u32[]{:S(2)}) copy-start(bf16[160,320]{1,0:T(8,128)(2,1)} %param.19) | copy-start | bytes 307204
  7.2 31.1 %copy-start.11 = (bf16[5120]{0:T(1024)(128)(2,1)S(1)}, bf16[5120]{0:T(1024)(128)(2,1)}, u32[]{:S(2)}) copy-start(bf16[5120]{0:T(1024)(128)(2,1)} %param.14) | copy-start | bytes 30724
  7.2 112.0 %all-gather.4.cloned.1.call-start = ((), (), s32[]{:S(2)}) async-start(), calls=%async_computation.2 | async-start | bytes 6963200 | tf_op jit(solution)/shard_map/gather_value/all_gather | solution.py:261
  17.8 1.0 copy-start.14
  20.7 35.4 %all-to-all-start = ((f32[32,8,128]{2,1,0:T(8,128)}), f32[32,8,128]{2,1,0:T(8,128)S(1)}, u32[]{:S(2)}, u32[]{:S(2)}) async-start(f32[32,8,128]{2,1,0:T(8,128)} %bitcast.17), calls=%async_computation | async-start | bytes 262144 | tf_op jit(solution)/shard_map/first_exchange/all_to_all | solution.py:233
  38.3 2.6 %copy-start.8 = (bf16[256,5120]{1,0:T(8,128)(2,1)S(1)}, bf16[256,5120]{1,0:T(8,128)(2,1)}, u32[]{:S(2)}) copy-start(bf16[256,5120]{1,0:T(8,128)(2,1)} %param.13) | copy-start | bytes 7864324
  40.9 0.8 copy-start.12
  44.8 17.6 %copy-start.10 = (bf16[320,64]{0,1:T(8,128)(2,1)S(1)}, bf16[320,64]{0,1:T(8,128)(2,1)}, u32[]{:S(2)}) copy-start(bf16[320,64]{0,1:T(8,128)(2,1)} %param.20) | copy-start | bytes 122884
  57.8 29.2 %all-to-all-start.1 = ((bf16[32,16,128]{2,1,0:T(8,128)(2,1)}), bf16[32,16,128]{2,1,0:T(8,128)(2,1)}, u32[]{:S(2)}, u32[]{:S(2)}) async-start(bf16[32,16,128]{2,1,0:T(8,128)(2,1)} %bitcast.21), calls=%async_computation.1 | async-start | bytes 262144 | tf_op jit(solution)/shard_map/second_exchange/all_to_all | solution.py:233
  119.2 13.1 %copy-start.1 = (bf16[16,64,320]{2,1,0:T(8,128)(2,1)S(1)}, bf16[16,64,320]{2,1,0:T(8,128)(2,1)}, u32[]{:S(2)}) copy-start(bf16[16,64,320]{2,1,0:T(8,128)(2,1)} %all_gather.25.matrix_ref) | copy-start | bytes 1966084
  119.2 13.1 %copy-start.2 = (bf16[640,64]{0,1:T(8,128)(2,1)S(1)}, bf16[640,64]{0,1:T(8,128)(2,1)}, u32[]{:S(2)}) copy-start(bf16[640,64]{0,1:T(8,128)(2,1)} %param.16) | copy-start | bytes 245764
  119.2 13.1 %copy-start.3 = (f32[2,64,64]{2,1,0:T(8,128)S(1)}, f32[2,64,64]{2,1,0:T(8,128)}, u32[]{:S(2)}) copy-start(f32[2,64,64]{2,1,0:T(8,128)} %fusion.25.gram_ref) | copy-start | bytes 98308
  119.2 13.1 %copy-start.4 = (f32[256,64]{1,0:T(8,128)S(1)}, f32[256,64]{1,0:T(8,128)}, u32[]{:S(2)}) copy-start(f32[256,64]{1,0:T(8,128)} %fusion.13.noise_ref) | copy-start | bytes 196612
  119.2 13.1 %copy-start.5 = (f32[2,1000]{1,0:T(2,128)S(1)}, f32[2,1000]{1,0:T(2,128)}, u32[]{:S(2)}) copy-start(f32[2,1000]{1,0:T(2,128)} %mix_ref.1) | copy-start | bytes 24004
  119.2 13.1 %copy-start.6 = (f32[1000]{0:T(1024)S(1)}, f32[1000]{0:T(1024)}, u32[]{:S(2)}) copy-start(f32[1000]{0:T(1024)} %param.25) | copy-start | bytes 12004
  119.2 13.1 %copy-start.7 = (s32[16]{0:T(128)S(1)}, s32[16]{0:T(128)}, u32[]{:S(2)}) copy-start(s32[16]{0:T(128)} %tsteps_ref.1) | copy-start | bytes 196
  139.6 8.0 %copy-start.13 = (f32[256]{0:T(256)S(1)}, f32[256]{0:T(256)}, u32[]{:S(2)}) copy-start(f32[256]{0:T(256)} %copy-done.12) | copy-start | bytes 3076
  139.6 5.1 %collective-permute-start = (bf16[2,256,1280]{2,1,0:T(8,128)(2,1)}, bf16[2,256,1280]{2,1,0:T(8,128)(2,1)S(1)}, u32[]{:S(2)}, u32[]{:S(2)}) collective-permute-start(bf16[2,256,1280]{2,1,0:T(8,128)(2,1)} %get-tuple-element.17), channel_id=1, source_target_pairs={{0,1},{1,0},{2,3},{3,2},{4,5},{5,4},{6,7},{7,6},{8,9},{9,8},{10,11... | collective-permute-start | bytes 3932168 | tf_op jit(solution)/shard_map/backward/ppermute | solution.py:357
  144.9 18.1 %collective-permute-start.1 = (bf16[256,1280]{1,0:T(8,128)(2,1)S(1)}, bf16[256,1280]{1,0:T(8,128)(2,1)S(1)}, u32[]{:S(2)}, u32[]{:S(2)}) collective-permute-start(bf16[256,1280]{1,0:T(8,128)(2,1)S(1)} %fusion.12), channel_id=1, source_target_pairs={{0,2},{2,0},{1,3},{3,1},{4,6},{6,4},{5,7},{7,5},{8,10},{10,8},{9,1... | collective-permute-start | bytes 1966088 | tf_op jit(solution)/shard_map/backward/ppermute | solution.py:360
Sparse Core Ops, SparseCore 0:
  17.0 102.1 all-gather.3

commit v5 on v4

--- a/solution.py
+++ b/solution.py
@@ -19,7 +19,7 @@
 SWAP = ((0, 1), (1, 0))
 
 
-BUSY = 24 * 2**20
+BUSY = 16 * 2**20
 GELU_IN = 0.7978845608028654
 GELU_CUBE = 0.044715
 NT = (((1,), (1,)), ((), ()))
@@ -159,12 +159,14 @@
         )
         square = jnp.sum(turned * exact, axis=1, keepdims=True) / width
         scales.append(lax.rsqrt(jnp.maximum(square, 0.0) + 1e-06))
-    blocks = matrix_ref.shape[0]
+    wide = 256
+    count = matrix_ref.shape[1] // wide
     gap = jnp.zeros((rows, latent_width), F32)
-    for i in range(blocks):
-        own = jnp.dot(noisy, matrix_ref[i], preferred_element_type=F32)
-        act = twice_gelu(own * scales[i * 2 // blocks]).astype(BF16)
-        gap = gap + lax.dot_general(act, head_ref[i], NT, preferred_element_type=F32)
+    for i in range(count):
+        at = slice(i * wide, (i + 1) * wide)
+        own = jnp.dot(noisy, matrix_ref[:, at], preferred_element_type=F32)
+        act = twice_gelu(own * scales[i * 2 // count]).astype(BF16)
+        gap = gap + lax.dot_general(act, head_ref[:, at], NT, preferred_element_type=F32)
     cotangent = (weight_ref[0, level] * (0.5 * gap)).astype(BF16)
     cot = cotangent.astype(F32)
     mixed_ref[...] = jnp.sum(cot * parts[:, latent_width:], axis=1, keepdims=True)
@@ -224,9 +226,47 @@
     )(near, far, inverse, gain)
 
 
-def to_tiles(x, tiles):
-    flat = jnp.pad(x, ((0, 0), (0, tiles * 8 * LANES - x.shape[1])))
-    return flat.reshape(x.shape[0], tiles * 8, LANES)
+def unpack_kernel(got_ref, slot_ref, noise_ref, matrix_ref):
+    got = got_ref[...]
+    total, lanes = got.shape
+    half = lanes // 2
+    rows = slot_ref.shape[0]
+    at = lax.broadcasted_iota(jnp.int32, (rows, total), 1)
+    holds = jnp.where(at == slot_ref[...], 1.0, 0.0).astype(BF16)
+    noise_ref[...] = jnp.dot(holds, got, preferred_element_type=F32)[:, :half]
+    senders = total // SLOTS
+    count = 2 * (matrix_ref.shape[1] // half)
+    row = lax.broadcasted_iota(jnp.int32, (count * senders, total), 0)
+    at = lax.broadcasted_iota(jnp.int32, (count * senders, total), 1)
+    chosen = jnp.where(at == (row % senders) * SLOTS + row // senders, 1.0, 0.0).astype(BF16)
+    parts = jnp.dot(chosen, got, preferred_element_type=F32).astype(BF16)
+    for k in range(count):
+        channel = k // (count // 2) * senders
+        col = k % (count // 2) * half
+        matrix_ref[channel : channel + senders, col : col + half] = parts[
+            k * senders : (k + 1) * senders, half:
+        ]
+
+
+def unpack(got, slot, cols):
+    rows = slot.shape[0]
+    half = got.shape[1] // 2
+    vmem = pl.BlockSpec(memory_space=pltpu.VMEM)
+    return pl.pallas_call(
+        unpack_kernel,
+        in_specs=[vmem, vmem],
+        out_specs=[vmem, vmem],
+        out_shape=[
+            jax.ShapeDtypeStruct((rows, half), F32),
+            jax.ShapeDtypeStruct((half, cols), BF16),
+        ],
+        compiler_params=pltpu.CompilerParams(vmem_limit_bytes=16 * 2**20),
+        name="unpack",
+    )(got, slot)
+
+
+def side_by_side(x):
+    return x.transpose(1, 0, 2).reshape(x.shape[1], -1)
 
 
 def swap_all(x):
@@ -273,8 +313,10 @@
             critic_value.astype(F32),
             precision=lax.Precision.HIGHEST,
         )
-        each = latent_width // seq_count
-        part = part.reshape(seq_count, each * cols)
+        quarter = LANES // 2
+        wide = cols // quarter
+        part = part.reshape(2, seq_count, wide, quarter).transpose(1, 2, 0, 3)
+        part = part.reshape(seq_count, wide, LANES).astype(BF16)
 
     with jax.named_scope("noise_requests"):
         crit_rows = noise.shape[0]
@@ -283,39 +325,39 @@
         ids = jnp.arange(rows, dtype=jnp.int32)
         before = (ids[None, :] < ids[:, None]).astype(BF16)
         prefix = jnp.dot(before, at, preferred_element_type=F32)
-        rank = jnp.sum(prefix * at.astype(F32), axis=1).astype(jnp.int32)
-        slot = target * SLOTS + rank
+        rank = jnp.sum(prefix * at.astype(F32), axis=1, keepdims=True).astype(jnp.int32)
+        slot = target[:, None] * SLOTS + rank
         total = seq_count * SLOTS
-        holds = jnp.arange(total, dtype=jnp.int32)[:, None] == slot[None, :]
-        wanted = jnp.sum(jnp.where(holds, (owner % crit_rows + 1)[None, :], 0), axis=1) - 1
-        wanted = wanted.astype(F32).reshape(seq_count, SLOTS)
+        holds = jnp.arange(total, dtype=jnp.int32)[:, None] == slot[:, 0][None, :]
+        wanted = jnp.sum(jnp.where(holds, (owner % crit_rows + 1)[None, :], 0), axis=1)
+        wanted = wanted.reshape(seq_count, SLOTS)
+        digits = [jnp.pad(d, ((0, 0), (0, quarter - SLOTS))) for d in (wanted // 32, wanted % 32)]
+        digits = jnp.concatenate(digits, axis=1).astype(BF16)[:, None, :]
 
     with jax.named_scope("first_exchange"):
-        sent = to_tiles(jnp.concatenate([part, wanted], axis=1), 1)
-        got = swap_all(sent).reshape(seq_count, -1)
+        sent = jnp.concatenate([part, digits], axis=1)
+        sent = jnp.pad(sent, ((0, 0), (0, 8 - sent.shape[1]), (0, 0)))
+        got = swap_all(sent)
 
     with jax.named_scope("noise_replies"):
-        asked = got[:, each * cols : each * cols + SLOTS].reshape(total)
-        take = asked[:, None] == jnp.arange(crit_rows, dtype=jnp.int32).astype(F32)[None, :]
+        digits = got[:, wide].astype(F32)
+        asked = (digits[:, :SLOTS] * 32 + digits[:, quarter : quarter + SLOTS]).reshape(total)
+        take = asked[:, None] == jnp.arange(1, crit_rows + 1, dtype=jnp.int32).astype(F32)[None, :]
         found = jnp.dot(take.astype(BF16), noise, preferred_element_type=F32).astype(BF16)
-        found = found.reshape(seq_count, SLOTS * latent_width)
-        mine = jnp.sum(got[:, : each * cols], axis=0).astype(BF16)
+        found = found.reshape(seq_count, SLOTS, latent_width)
+        mine = jnp.sum(got[:, :wide].astype(F32), axis=0).astype(BF16)
+        mine = jnp.concatenate([mine[:, :quarter], mine[:, quarter:]], axis=0)
+        mine = jnp.pad(mine, ((0, SLOTS - mine.shape[0]), (0, 0)))
 
     with jax.named_scope("second_exchange"):
-        mine = jnp.broadcast_to(mine[None, :], (seq_count, each * cols))
-        sent = to_tiles(jnp.concatenate([found, mine], axis=1), 2)
-        got = swap_all(sent).reshape(seq_count, -1)
-        found = got[:, : SLOTS * latent_width].reshape(total, latent_width)
-        matrix = got[:, SLOTS * latent_width : SLOTS * latent_width + each * cols]
-        matrix = matrix.reshape(latent_width, cols)
-        own_noise = lax.dot_general(
-            holds.astype(BF16), found, (((0,), (0,)), ((), ())), preferred_element_type=F32
-        )
+        mine = jnp.broadcast_to(mine[None], (seq_count, SLOTS, quarter))
+        got = swap_all(jnp.concatenate([found, mine], axis=2))
+        own_noise, matrix = unpack(got.reshape(total, LANES), slot, cols)
 
     with jax.named_scope("critic_gather"):
-        matrix = lax.all_gather(matrix, ("group",) + TP, axis=0)
+        matrix = side_by_side(lax.all_gather(matrix, ("group",) + TP, axis=0))
         head = jnp.where(critic_id == 1, critic_head, -critic_head).T
-        head = lax.all_gather(head, ("group",) + TP, axis=0)
+        head = side_by_side(lax.all_gather(head, ("group",) + TP, axis=0))
         gram = lax.dot_general(
             critic_embed, critic_embed, (((2,), (2,)), ((0,), (0,))), preferred_element_type=F32
         )

time: 172 us -> 168 us (0.977)
  local copies, waits for them, and re-layouts: 8.97 us -> 12.7 us
  matrix products: 6.7 us -> 4.08 us
  waiting for transfers between devices: 31.5 us -> 29.1 us
  blocking collectives: 62.1 us -> 60.1 us
    all_gather x1, waiting for transfers between devices: 4.9 us -> 1.59 us  [local(): gen_full = lax.all_gather(gen_pair, 'z', axis=0, tiled=True)]
    all_gather x0 -> x2, local copies, waits for them, and re-layouts: none -> 2.71 us  [the longest x1 1.35 us: local(): head = side_by_side(lax.all_gather(head, ('group',) + TP, axis=0))]
    reduce_sum x1, other arithmetic: 2.5 us -> 0.6 us  [local(): jnp.mean(inputs * inputs, axis=-1, keepdims=True) + 1e-06]
    dot_general x1 -> x0, matrix products: 1.89 us -> none  [local(): lax.dot_general(holds.astype(BF16), found, (((0,), (0,)), ((), ())), pref...]
    all_gather x2, blocking collectives: 44.6 us -> 42.8 us  [the longest x1 24.3 us: local(): head = side_by_side(lax.all_gather(head, ('group',) + TP, axis=0))]
    reshape x4 -> x3, local copies, waits for them, and re-layouts: 3.38 us -> 4.28 us  [the longest x2 4.2 us: side_by_side(): return x.transpose(1, 0, 2).reshape(x.shape[1], -1)]
    unnamed x36 -> x33, local copies, waits for them, and re-layouts: 3.17 us -> 3.6 us
  transfers between devices with their start and end apart: 5 -> 5, of which waited for: 4 -> 4; matrix products, arithmetic and copies ran while one was open for 13% -> 13% of each run, Pallas kernels for 0% -> 1%
where the time goes in v5:
time: 168 us
  blocking collectives  60.1 us (36%)
  waiting for transfers between devices  29.1 us (17%)
  starting transfers between devices  27.1 us (16%)
  between operations  14.4 us (9%)
  Pallas kernels  13.4 us (8%)
  local copies, waits for them, and re-layouts  12.7 us (8%)
  other arithmetic  6.74 us (4%)
  matrix products  4.08 us (2%)
    all_gather x1, blocking collectives, local(): head = side_by_side(lax.all_gather(head, ('group',) + TP, axis=0))  24.3 us
    all_to_all x2, starting transfers between devices, swap_all(): return lax.all_to_all(x, SEQ, split_axis=0, concat_axis=0, tiled=True)  22.2 us
    all_gather x1, blocking collectives, local(): matrix = side_by_side(lax.all_gather(matrix, ('group',) + TP, axis=0))  18.5 us
    ppermute x1, waiting for transfers between devices, local(): far = lax.ppermute(far, 'y_lo', SWAP)  13.8 us
    all_to_all x2, waiting for transfers between devices, swap_all(): return lax.all_to_all(x, SEQ, split_axis=0, concat_axis=0, tiled=True)  12.2 us
    all_gather x1, blocking collectives, local(): gen_pair = lax.all_gather(gen_value, 'y_hi', axis=1, tiled=True)  9.64 us
    all_gather x1, blocking collectives, local(): parts = lax.all_gather(part, TP, axis=0)  7.61 us
    pallas_call x1, Pallas kernels, critics(): pl.pallas_call(functools.partial(critic_kernel, width), in_specs=[smem] *...  5.84 us
  transfers between devices with their start and end apart: 5, of which 4 were waited for; matrix products, arithmetic and copies ran while one was open for 13% of the time, Pallas kernels for 1%

profile of v5, /device:TPU:1, one launch (start us, length us, event | category | flops | bytes accessed | tf_op | source)
XLA Modules:
  0.0 167.6 jit_solution(17864293713745584860)
XLA Ops:
  7.2 0.0 copy-start
  7.2 0.0 copy-start.12
  7.2 0.0 copy-start.9
  7.2 0.0 all-gather.5.cloned.1.call-start
  7.2 9.6 %all_gather.24 = bf16[160,1280]{1,0:T(8,128)(2,1)} all-gather(bf16[160,640]{1,0:T(8,128)(2,1)} %param.15), channel_id=1, replica_groups=mesh['group'=4,'y_hi'=2,'z'=16,'y_lo'=2,'core'=2] {'y_hi'}, dimensions={1}, use_global_device_ids=true | all-gather | bytes 614400 | tf_op jit(solution)/shard_map/gather_value/all_gather | solution.py:300
  16.9 0.0 all-gather.5.cloned.1.call-update
  16.9 0.7 and_select_fusion.1
  17.6 0.2 fusion.10
  17.8 0.1 select_reduce_fusion
  18.0 0.1 reshape.120
  18.1 1.0 copy.42
  19.1 0.8 dynamic-slice_convert_fusion.1
  19.9 0.9 convert_multiply_fusion.2
  20.7 0.3 fusion.9
  21.1 0.1 copy.43
  21.2 0.1 convert_element_type.101
  21.3 0.1 maximum_maximum_fusion
  21.4 0.6 pad.19.clone
  22.1 17.6 %all-to-all-start = ((bf16[32,8,128]{2,1,0:T(8,128)(2,1)}), bf16[32,8,128]{2,1,0:T(8,128)(2,1)S(1)}, u32[]{:S(2)}, u32[]{:S(2)}) async-start(bf16[32,8,128]{2,1,0:T(8,128)(2,1)} %pad.19.clone), calls=%async_computation | async-start | bytes 131072 | tf_op jit(solution)/shard_map/first_exchange/all_to_all | solution.py:273
  39.7 0.0 copy-done.12
  39.7 0.0 copy-start.10
  39.7 0.6 fusion
  40.3 1.1 copy-done.10
  41.5 0.8 fusion.2.normed_ref
  42.2 0.0 copy-done.13
  42.3 0.1 copy.46.slot_ref
  42.4 0.0 copy-done.11
  42.4 12.2 %all-to-all-done = bf16[32,8,128]{2,1,0:T(8,128)(2,1)S(1)} async-done(((bf16[32,8,128]{2,1,0:T(8,128)(2,1)}), bf16[32,8,128]{2,1,0:T(8,128)(2,1)S(1)}, u32[]{:S(2)}, u32[]{:S(2)}) %all-to-all-start) | async-done | bytes 65568 | tf_op jit(solution)/shard_map/first_exchange/all_to_all | solution.py:273
  54.6 0.1 slice_add_fusion
  54.7 0.1 eq.54
  54.8 0.5 fusion.6
  55.3 0.1 copy.45
  55.5 0.1 fusion.25
  55.6 0.8 pad_maximum_fusion
  56.4 4.6 %all-to-all-start.1 = ((bf16[32,16,128]{2,1,0:T(8,128)(2,1)}), bf16[32,16,128]{2,1,0:T(8,128)(2,1)}, u32[]{:S(2)}, u32[]{:S(2)}) async-start(bf16[32,16,128]{2,1,0:T(8,128)(2,1)} %pad_maximum_fusion), calls=%async_computation.1 | async-start | bytes 262144 | tf_op jit(solution)/shard_map/second_exchange/all_to_all | solution.py:273
  61.0 24.3 %all-gather.2 = bf16[1024,320]{1,0:T(8,128)(2,1)S(1)} all-gather(bf16[64,320]{1,0:T(8,128)(2,1)S(1)} %fusion.14), channel_id=4, replica_groups=mesh['group'=4,'y_hi'=2,'z'=16,'y_lo'=2,'core'=2] {'group','y_lo','core'}, dimensions={0}, use_global_device_ids=true | all-gather | bytes 696320 | tf_op jit(solution)/shard_map/critic_gather/all_gather | solution.py:360
  85.3 1.4 copy.57
  86.6 1.8 %reshape.124.head_ref = bf16[64,5120]{1,0:T(8,128)(2,1)S(1)} reshape(bf16[64,16,320]{2,1,0:T(8,128)(2,1)} %bitcast.59) | data formatting | bytes 1310720 | tf_op jit(solution)/shard_map/critic_gather/reshape | solution.py:269
  88.4 0.1 stack.27.place_ref
  88.5 3.0 %fusion.26.gram_ref = f32[2,64,64]{2,1,0:T(8,128)} fusion(bf16[2,64,5120]{2,1,0:T(8,128)(2,1)} %param.17), kind=kOutput, calls=%fused_computation.66 | convolution fusion | flops 83886080 | bytes 1343488 | tf_op jit(solution)/shard_map/critic_gather/dot_general | solution.py:361
  91.5 0.0 all-to-all-done.1
  91.5 1.3 unpack.1
  92.8 0.7 copy-done.4
  93.5 18.5 %all-gather.1 = bf16[1024,320]{1,0:T(8,128)(2,1)S(1)} all-gather(bf16[64,320]{1,0:T(8,128)(2,1)S(1)} %get-tuple-element.16), channel_id=3, replica_groups=mesh['group'=4,'y_hi'=2,'z'=16,'y_lo'=2,'core'=2] {'group','y_lo','core'}, dimensions={0}, use_global_device_ids=true | all-gather | bytes 696320 | tf_op jit(solution)/shard_map/critic_gather/all_gather | solution.py:358
  112.0 1.4 copy.58
  113.4 2.4 %reshape.123.matrix_ref = bf16[64,5120]{1,0:T(8,128)(2,1)} reshape(bf16[64,16,320]{2,1,0:T(8,128)(2,1)} %bitcast.60) | data formatting | bytes 1310720 | tf_op jit(solution)/shard_map/critic_gather/reshape | solution.py:269
  115.8 1.6 all-gather.5.cloned.1.call-done.weights_ref
  117.4 0.0 copy-start.7
  117.4 0.0 copy-start.8
  117.5 5.1 %forward.1 = (f32[256,640]{1,0:T(8,128)S(1)}, bf16[256,128]{1,0:T(8,128)(2,1)S(1)}, bf16[2560,1280]{1,0:T(8,128)(2,1)S(1)}) custom-call(bf16[256,5120]{1,0:T(8,128)(2,1)S(1)} %fusion.2.normed_ref, bf16[2560,1280]{1,0:T(8,128)(2,1)} %all-gather.5.cloned.1.call-done.weights_ref, bf16[64,640]{1,0:T(8,128)(2,1)} %bitcast.54), custom_call_target="tpu_custom_call" | custom-call | flops 1677721600 | bytes 6553600 | tf_op jit(solution)/shard_map/forward/forward/pallas_call | solution.py:91
  122.6 7.6 %all-gather = bf16[1024,128]{1,0:T(8,128)(2,1)S(1)} all-gather(bf16[256,128]{1,0:T(8,128)(2,1)S(1)} %get-tuple-element.14), channel_id=2, replica_groups=mesh['group'=4,'y_hi'=2,'z'=16,'y_lo'=2,'core'=2] {'y_lo','core'}, dimensions={0}, use_global_device_ids=true | all-gather | bytes 327680 | tf_op jit(solution)/shard_map/forward/all_gather | solution.py:372
  130.2 0.0 copy-done.2
  130.3 5.8 %critics.1 = (bf16[256,64]{1,0:T(8,128)(2,1)S(1)}, f32[256,1]{1,0:T(8,128)S(1)}, bf16[2,256,1280]{2,1,0:T(8,128)(2,1)}, bf16[2,256,1280]{2,1,0:T(8,128)(2,1)S(1)}) custom-call(s32[9]{0:T(128)S(1)} %stack.27.place_ref, s32[16]{0:T(128)S(1)} %copy-done.8, f32[2,1000]{1,0:T(2,128)S(1)} %copy-done.6, f32[1,1000]{1,0:T(1,128)S(1)} %bitcast.56, ...), custom_call_target="tpu_custom_call" | custom-call | tf_op jit(solution)/shard_map/critics/critics/pallas_call | solution.py:189
  136.1 2.2 %collective-permute-start = (bf16[2,256,1280]{2,1,0:T(8,128)(2,1)}, bf16[2,256,1280]{2,1,0:T(8,128)(2,1)S(1)}, u32[]{:S(2)}, u32[]{:S(2)}) collective-permute-start(bf16[2,256,1280]{2,1,0:T(8,128)(2,1)} %get-tuple-element.21), channel_id=1, source_target_pairs={{0,1},{1,0},{2,3},{3,2},{4,5},{5,4},{6,7},{7,6},{8,9},{9,8},{10,11... | collective-permute-start | bytes 3932168 | tf_op jit(solution)/shard_map/backward/ppermute | solution.py:399
  138.3 0.7 copy.49.inverse_ref
  139.1 0.1 dynamic-slice_convert_fusion
  139.2 0.7 copy.52
  139.9 1.5 collective-permute-done
  141.4 0.2 fusion.13
  141.6 2.7 %collective-permute-start.1 = (bf16[256,1280]{1,0:T(8,128)(2,1)S(1)}, bf16[256,1280]{1,0:T(8,128)(2,1)S(1)}, u32[]{:S(2)}, u32[]{:S(2)}) collective-permute-start(bf16[256,1280]{1,0:T(8,128)(2,1)S(1)} %fusion.13), channel_id=1, source_target_pairs={{0,2},{2,0},{1,3},{3,1},{4,6},{6,4},{5,7},{7,5},{8,10},{10,8},{9,1... | collective-permute-start | bytes 1966088 | tf_op jit(solution)/shard_map/backward/ppermute | solution.py:402
  144.2 0.1 multiply_reduce_fusion
  144.3 1.5 fusion.5.near_ref
  145.8 13.8 %collective-permute-done.1.far_ref = bf16[256,1280]{1,0:T(8,128)(2,1)S(1)} collective-permute-done((bf16[256,1280]{1,0:T(8,128)(2,1)S(1)}, bf16[256,1280]{1,0:T(8,128)(2,1)S(1)}, u32[]{:S(2)}, u32[]{:S(2)}) %collective-permute-start.1) | collective-permute-done | bytes 655392 | tf_op jit(solution)/shard_map/backward/ppermute | solution.py:402
  159.6 1.1 finish.1
  (31 shorter events, 0.2 us)
Async XLA Ops:
  7.2 47.6 %copy-start = (bf16[1024,64]{0,1:T(8,128)(2,1)S(1)}, bf16[1024,64]{0,1:T(8,128)(2,1)}, u32[]{:S(2)}) copy-start(bf16[1024,64]{0,1:T(8,128)(2,1)} %param.21) | copy-start | bytes 393220
  7.2 32.5 %copy-start.12 = (bf16[5120]{0:T(1024)(128)(2,1)S(1)}, bf16[5120]{0:T(1024)(128)(2,1)}, u32[]{:S(2)}) copy-start(bf16[5120]{0:T(1024)(128)(2,1)} %param.14) | copy-start | bytes 30724
  7.2 32.5 %copy-start.9 = (bf16[256,5120]{1,0:T(8,128)(2,1)S(1)}, bf16[256,5120]{1,0:T(8,128)(2,1)}, u32[]{:S(2)}) copy-start(bf16[256,5120]{1,0:T(8,128)(2,1)} %param.13) | copy-start | bytes 7864324
  7.2 110.2 %all-gather.5.cloned.1.call-start = ((), (), s32[]{:S(2)}) async-start(), calls=%async_computation.2 | async-start | bytes 6963200 | tf_op jit(solution)/shard_map/gather_value/all_gather | solution.py:301
  22.1 32.5 %all-to-all-start = ((bf16[32,8,128]{2,1,0:T(8,128)(2,1)}), bf16[32,8,128]{2,1,0:T(8,128)(2,1)S(1)}, u32[]{:S(2)}, u32[]{:S(2)}) async-start(bf16[32,8,128]{2,1,0:T(8,128)(2,1)} %pad.19.clone), calls=%async_computation | async-start | bytes 131072 | tf_op jit(solution)/shard_map/first_exchange/all_to_all | solution.py:273
  39.7 1.7 %copy-start.10 = (bf16[256,5120]{1,0:T(8,128)(2,1)S(1)}, bf16[256,5120]{1,0:T(8,128)(2,1)}, u32[]{:S(2)}) copy-start(bf16[256,5120]{1,0:T(8,128)(2,1)} %param.13) | copy-start | bytes 7864324
  41.4 0.8 copy-start.13
  41.4 1.0 copy-start.11
  56.4 35.1 %all-to-all-start.1 = ((bf16[32,16,128]{2,1,0:T(8,128)(2,1)}), bf16[32,16,128]{2,1,0:T(8,128)(2,1)}, u32[]{:S(2)}, u32[]{:S(2)}) async-start(bf16[32,16,128]{2,1,0:T(8,128)(2,1)} %pad_maximum_fusion), calls=%async_computation.1 | async-start | bytes 262144 | tf_op jit(solution)/shard_map/second_exchange/all_to_all | solution.py:273
  92.8 0.7 copy-start.4
  117.4 12.8 %copy-start.1 = (bf16[64,5120]{1,0:T(8,128)(2,1)S(1)}, bf16[64,5120]{1,0:T(8,128)(2,1)}, u32[]{:S(2)}) copy-start(bf16[64,5120]{1,0:T(8,128)(2,1)} %reshape.123.matrix_ref) | copy-start | bytes 1966084
  117.4 12.8 %copy-start.2 = (bf16[640,64]{0,1:T(8,128)(2,1)S(1)}, bf16[640,64]{0,1:T(8,128)(2,1)}, u32[]{:S(2)}) copy-start(bf16[640,64]{0,1:T(8,128)(2,1)} %param.16) | copy-start | bytes 245764
  117.4 12.8 %copy-start.3 = (f32[2,64,64]{2,1,0:T(8,128)S(1)}, f32[2,64,64]{2,1,0:T(8,128)}, u32[]{:S(2)}) copy-start(f32[2,64,64]{2,1,0:T(8,128)} %fusion.26.gram_ref) | copy-start | bytes 98308
  117.4 12.8 %copy-start.5 = (f32[256,64]{1,0:T(8,128)S(1)}, f32[256,64]{1,0:T(8,128)}, u32[]{:S(2)}) copy-start(f32[256,64]{1,0:T(8,128)} %copy-done.4) | copy-start | bytes 196612
  117.4 12.8 %copy-start.6 = (f32[2,1000]{1,0:T(2,128)S(1)}, f32[2,1000]{1,0:T(2,128)}, u32[]{:S(2)}) copy-start(f32[2,1000]{1,0:T(2,128)} %mix_ref.1) | copy-start | bytes 24004
  117.4 12.8 %copy-start.7 = (f32[1000]{0:T(1024)S(1)}, f32[1000]{0:T(1024)}, u32[]{:S(2)}) copy-start(f32[1000]{0:T(1024)} %param.25) | copy-start | bytes 12004
  117.4 12.8 %copy-start.8 = (s32[16]{0:T(128)S(1)}, s32[16]{0:T(128)}, u32[]{:S(2)}) copy-start(s32[16]{0:T(128)} %tsteps_ref.1) | copy-start | bytes 196
  136.1 8.2 %copy-start.14 = (f32[256]{0:T(256)S(1)}, f32[256]{0:T(256)}, u32[]{:S(2)}) copy-start(f32[256]{0:T(256)} %copy-done.13) | copy-start | bytes 3076
  136.1 5.3 %collective-permute-start = (bf16[2,256,1280]{2,1,0:T(8,128)(2,1)}, bf16[2,256,1280]{2,1,0:T(8,128)(2,1)S(1)}, u32[]{:S(2)}, u32[]{:S(2)}) collective-permute-start(bf16[2,256,1280]{2,1,0:T(8,128)(2,1)} %get-tuple-element.21), channel_id=1, source_target_pairs={{0,1},{1,0},{2,3},{3,2},{4,5},{5,4},{6,7},{7,6},{8,9},{9,8},{10,11... | collective-permute-start | bytes 3932168 | tf_op jit(solution)/shard_map/backward/ppermute | solution.py:399
  141.6 18.1 %collective-permute-start.1 = (bf16[256,1280]{1,0:T(8,128)(2,1)S(1)}, bf16[256,1280]{1,0:T(8,128)(2,1)S(1)}, u32[]{:S(2)}, u32[]{:S(2)}) collective-permute-start(bf16[256,1280]{1,0:T(8,128)(2,1)S(1)} %fusion.13), channel_id=1, source_target_pairs={{0,2},{2,0},{1,3},{3,1},{4,6},{6,4},{5,7},{7,5},{8,10},{10,8},{9,1... | collective-permute-start | bytes 1966088 | tf_op jit(solution)/shard_map/backward/ppermute | solution.py:402
Sparse Core Ops, SparseCore 0:
  17.0 100.3 all-gather.4

commit v6 on v5

--- a/solution.py
+++ b/solution.py
@@ -9,7 +9,8 @@
 from jax.sharding import PartitionSpec as P
 
 FTOK = 2048
-SLOTS = 16
+SLOTS = 4
+ROWS = 8
 LANES = 128
 F32 = jnp.float32
 BF16 = jnp.bfloat16
@@ -45,12 +46,21 @@
 
 
 def forward_kernel(
-    normed_ref, weights_ref, head_ref, slope_ref, part_ref, held, head_held, total, sems, head_sem
+    normed_ref,
+    weights_ref,
+    head_ref,
+    slope_ref,
+    part_ref,
+    held,
+    head_held,
+    total,
+    sems,
+    head_sem,
 ):
     copies = fetch(weights_ref, held, sems)
     head_copy = pltpu.make_async_copy(head_ref, head_held, head_sem)
     head_copy.start()
-    steps = 4
+    steps = 10
     each = len(copies) // steps
     half, cols = held.shape[0], total.shape[1]
     deep = half // steps
@@ -91,7 +101,7 @@
     return pl.pallas_call(
         forward_kernel,
         in_specs=[vmem, hbm, hbm],
-        out_specs=[vmem, vmem, vmem],
+        out_specs=[vmem] * 3,
         out_shape=[
             jax.ShapeDtypeStruct((rows, cols), F32),
             jax.ShapeDtypeStruct((rows, 2 * latent_width), BF16),
@@ -100,7 +110,7 @@
         scratch_shapes=[
             pltpu.VMEM(gen_head.shape, BF16),
             pltpu.VMEM((rows, cols), F32),
-            pltpu.SemaphoreType.DMA((8,)),
+            pltpu.SemaphoreType.DMA((20,)),
             pltpu.SemaphoreType.DMA,
         ],
         compiler_params=pltpu.CompilerParams(vmem_limit_bytes=BUSY),
@@ -148,7 +158,9 @@
     latent_width = latent_ref.shape[1]
     latent = parts[:, :latent_width].astype(BF16)
     latent_ref[...] = latent
-    noisy = mix_ref[0, level] * latent.astype(F32) + mix_ref[1, level] * noise_ref[...]
+    noise = noise_ref[...].astype(F32)
+    noise = noise[0] + noise[1] + noise[2] + noise[3]
+    noisy = mix_ref[0, level] * latent.astype(F32) + mix_ref[1, level] * noise
     noisy = noisy.astype(BF16)
     exact = noisy.astype(F32)
     rows = noisy.shape[0]
@@ -226,6 +238,26 @@
     )(near, far, inverse, gain)
 
 
+def side_by_side_kernel(first_ref, second_ref, first_out, second_out):
+    count, _, wide = first_ref.shape
+    for i in range(count):
+        first_out[:, i * wide : (i + 1) * wide] = first_ref[i]
+        second_out[:, i * wide : (i + 1) * wide] = second_ref[i]
+
+
+def side_by_side(first, second):
+    count, rows, wide = first.shape
+    vmem = pl.BlockSpec(memory_space=pltpu.VMEM)
+    return pl.pallas_call(
+        side_by_side_kernel,
+        in_specs=[vmem, vmem],
+        out_specs=[vmem, vmem],
+        out_shape=[jax.ShapeDtypeStruct((rows, count * wide), BF16)] * 2,
+        compiler_params=pltpu.CompilerParams(vmem_limit_bytes=BUSY),
+        name="side_by_side",
+    )(first, second)
+
+
 def unpack_kernel(got_ref, slot_ref, noise_ref, matrix_ref):
     got = got_ref[...]
     total, lanes = got.shape
@@ -233,18 +265,21 @@
     rows = slot_ref.shape[0]
     at = lax.broadcasted_iota(jnp.int32, (rows, total), 1)
     holds = jnp.where(at == slot_ref[...], 1.0, 0.0).astype(BF16)
-    noise_ref[...] = jnp.dot(holds, got, preferred_element_type=F32)[:, :half]
-    senders = total // SLOTS
+    noise_ref[...] = jnp.dot(holds, got, preferred_element_type=F32)[:, :half].astype(BF16)
+    senders = total // ROWS
     count = 2 * (matrix_ref.shape[1] // half)
     row = lax.broadcasted_iota(jnp.int32, (count * senders, total), 0)
     at = lax.broadcasted_iota(jnp.int32, (count * senders, total), 1)
-    chosen = jnp.where(at == (row % senders) * SLOTS + row // senders, 1.0, 0.0).astype(BF16)
+    piece = row // senders
+    piece = jnp.where(piece < ROWS, piece, piece - ROWS + SLOTS)
+    chosen = jnp.where(at == (row % senders) * ROWS + piece, 1.0, 0.0).astype(BF16)
     parts = jnp.dot(chosen, got, preferred_element_type=F32).astype(BF16)
     for k in range(count):
         channel = k // (count // 2) * senders
         col = k % (count // 2) * half
+        side = half if k < ROWS else 0
         matrix_ref[channel : channel + senders, col : col + half] = parts[
-            k * senders : (k + 1) * senders, half:
+            k * senders : (k + 1) * senders, side : side + half
         ]
 
 
@@ -257,16 +292,12 @@
         in_specs=[vmem, vmem],
         out_specs=[vmem, vmem],
         out_shape=[
-            jax.ShapeDtypeStruct((rows, half), F32),
+            jax.ShapeDtypeStruct((rows, half), BF16),
             jax.ShapeDtypeStruct((half, cols), BF16),
         ],
         compiler_params=pltpu.CompilerParams(vmem_limit_bytes=16 * 2**20),
         name="unpack",
     )(got, slot)
-
-
-def side_by_side(x):
-    return x.transpose(1, 0, 2).reshape(x.shape[1], -1)
 
 
 def swap_all(x):
@@ -326,7 +357,9 @@
         before = (ids[None, :] < ids[:, None]).astype(BF16)
         prefix = jnp.dot(before, at, preferred_element_type=F32)
         rank = jnp.sum(prefix * at.astype(F32), axis=1, keepdims=True).astype(jnp.int32)
-        slot = target[:, None] * SLOTS + rank
+        mine_here = rank // SLOTS == yl * 2 + c
+        slot = jnp.where(mine_here, target[:, None] * SLOTS + rank % SLOTS, -1)
+        place_back = jnp.where(mine_here, target[:, None] * ROWS + rank % SLOTS, -1)
         total = seq_count * SLOTS
         holds = jnp.arange(total, dtype=jnp.int32)[:, None] == slot[:, 0][None, :]
         wanted = jnp.sum(jnp.where(holds, (owner % crit_rows + 1)[None, :], 0), axis=1)
@@ -337,7 +370,10 @@
     with jax.named_scope("first_exchange"):
         sent = jnp.concatenate([part, digits], axis=1)
         sent = jnp.pad(sent, ((0, 0), (0, 8 - sent.shape[1]), (0, 0)))
-        got = swap_all(sent)
+        gram = lax.dot_general(
+            critic_embed, critic_embed, (((2,), (2,)), ((0,), (0,))), preferred_element_type=F32
+        )
+        got, gram = lax.optimization_barrier((swap_all(sent), gram))
 
     with jax.named_scope("noise_replies"):
         digits = got[:, wide].astype(F32)
@@ -347,20 +383,21 @@
         found = found.reshape(seq_count, SLOTS, latent_width)
         mine = jnp.sum(got[:, :wide].astype(F32), axis=0).astype(BF16)
         mine = jnp.concatenate([mine[:, :quarter], mine[:, quarter:]], axis=0)
-        mine = jnp.pad(mine, ((0, SLOTS - mine.shape[0]), (0, 0)))
+        left = jnp.pad(mine[ROWS:], ((0, ROWS - SLOTS - (mine.shape[0] - ROWS)), (0, 0)))
 
     with jax.named_scope("second_exchange"):
-        mine = jnp.broadcast_to(mine[None], (seq_count, SLOTS, quarter))
-        got = swap_all(jnp.concatenate([found, mine], axis=2))
-        own_noise, matrix = unpack(got.reshape(total, LANES), slot, cols)
+        left = jnp.broadcast_to(left[None], (seq_count, ROWS - SLOTS, quarter))
+        right = jnp.broadcast_to(mine[None, :ROWS], (seq_count, ROWS, quarter))
+        sent = jnp.concatenate([jnp.concatenate([found, left], axis=1), right], axis=2)
+        got = swap_all(sent)
+        own_noise, matrix = unpack(got.reshape(seq_count * ROWS, LANES), place_back, cols)
 
     with jax.named_scope("critic_gather"):
-        matrix = side_by_side(lax.all_gather(matrix, ("group",) + TP, axis=0))
+        noise_parts = lax.all_gather(own_noise, TP, axis=0)
+        matrices = lax.all_gather(matrix, ("group",) + TP, axis=0)
         head = jnp.where(critic_id == 1, critic_head, -critic_head).T
-        head = side_by_side(lax.all_gather(head, ("group",) + TP, axis=0))
-        gram = lax.dot_general(
-            critic_embed, critic_embed, (((2,), (2,)), ((0,), (0,))), preferred_element_type=F32
-        )
+        heads = lax.all_gather(head, ("group",) + TP, axis=0)
+        matrix, head = side_by_side(matrices, heads)
 
     with jax.named_scope("forward"):
         inputs = hidden.astype(F32)
@@ -380,7 +417,7 @@
             place,
             tables,
             parts,
-            own_noise,
+            noise_parts,
             gram,
             matrix,
             head,

time: 168 us -> 166 us (0.988)
  blocking collectives: 60.1 us -> 66.1 us
  local copies, waits for them, and re-layouts: 12.7 us -> 7.2 us
  matrix products: 4.08 us -> 1.92 us
  waiting for transfers between devices: 29.1 us -> 27.2 us
    all_gather x2 -> x3, blocking collectives: 42.8 us -> 48.4 us  [the longest x1 24 us: local(): heads = lax.all_gather(head, ('group',) + TP, axis=0)]
    reshape x2 -> x0, local copies, waits for them, and re-layouts: 4.2 us -> none  [side_by_side(): return x.transpose(1, 0, 2).reshape(x.shape[1], -1)]
    all_gather x2 -> x0, local copies, waits for them, and re-layouts: 2.71 us -> none  [the longest x1 1.35 us: local(): head = side_by_side(lax.all_gather(head, ('group',) + TP, axis=0))]
    all_to_all x2, waiting for transfers between devices: 12.2 us -> 9.95 us  [swap_all(): return lax.all_to_all(x, SEQ, split_axis=0, concat_axis=0, tiled=True)]
    dot_general x1, matrix products: 3 us -> 1.1 us  [local(): lax.dot_general(critic_embed, critic_embed, (((2,), (2,)), ((0,), (0,))),...]
    unnamed x33 -> x41, local copies, waits for them, and re-layouts: 3.6 us -> 4.87 us
  transfers between devices with their start and end apart: 5 -> 5, of which waited for: 4 -> 4; matrix products, arithmetic and copies ran while one was open for 13% -> 7% of each run, Pallas kernels for 1% -> 1%
where the time goes in v6:
time: 166 us; the launch traced here: 165 us
  blocking collectives  66.1 us (40%)
  waiting for transfers between devices  27.2 us (16%)
  starting transfers between devices  26.8 us (16%)
  between operations  14.4 us (9%)
  Pallas kernels  14.2 us (9%)
  other arithmetic  7.31 us (4%)
  local copies, waits for them, and re-layouts  7.2 us (4%)
  matrix products  1.92 us (1%)
    all_gather x1, blocking collectives, local(): heads = lax.all_gather(head, ('group',) + TP, axis=0)  24 us
    all_to_all x2, starting transfers between devices, swap_all(): return lax.all_to_all(x, SEQ, split_axis=0, concat_axis=0, tiled=True)  22.1 us
    all_gather x1, blocking collectives, local(): matrices = lax.all_gather(matrix, ('group',) + TP, axis=0)  18.4 us
    ppermute x1, waiting for transfers between devices, local(): far = lax.ppermute(far, 'y_lo', SWAP)  13.9 us
    all_to_all x2, waiting for transfers between devices, swap_all(): return lax.all_to_all(x, SEQ, split_axis=0, concat_axis=0, tiled=True)  9.95 us
    all_gather x1, blocking collectives, local(): gen_pair = lax.all_gather(gen_value, 'y_hi', axis=1, tiled=True)  9.65 us
    all_gather x1, blocking collectives, local(): parts = lax.all_gather(part, TP, axis=0)  8.06 us
    all_gather x1, blocking collectives, local(): noise_parts = lax.all_gather(own_noise, TP, axis=0)  5.93 us
  transfers between devices with their start and end apart: 5, of which 4 were waited for; matrix products, arithmetic and copies ran while one was open for 7% of the time, Pallas kernels for 1%

profile of v6, /device:TPU:1, one launch (start us, length us, event | category | flops | bytes accessed | tf_op | source)
XLA Modules:
  0.0 165.1 jit_solution(10935932373571186442)
XLA Ops:
  7.2 0.0 copy-start
  7.2 0.0 copy-start.11
  7.2 0.0 all-gather.6.cloned.1.call-start
  7.3 9.7 %all_gather.30 = bf16[160,1280]{1,0:T(8,128)(2,1)} all-gather(bf16[160,640]{1,0:T(8,128)(2,1)} %param.15), channel_id=1, replica_groups=mesh['group'=4,'y_hi'=2,'z'=16,'y_lo'=2,'core'=2] {'y_hi'}, dimensions={1}, use_global_device_ids=true | all-gather | bytes 614400 | tf_op jit(solution)/shard_map/gather_value/all_gather | solution.py:331
  16.9 0.0 all-gather.6.cloned.1.call-update
  17.0 0.7 and_select_fusion.3
  17.7 0.2 fusion.5
  17.9 0.1 select_reduce_fusion
  18.0 0.1 reshape.144
  18.1 0.1 copy.35
  18.3 0.8 dynamic-slice_convert_fusion.1
  19.1 0.9 convert_multiply_fusion.2
  19.9 0.3 fusion.4
  20.3 0.1 copy.36
  20.3 0.1 convert_element_type.101
  20.5 0.1 maximum_maximum_fusion
  20.6 0.6 pad.19.clone
  21.2 17.6 %all-to-all-start = ((bf16[32,8,128]{2,1,0:T(8,128)(2,1)}), bf16[32,8,128]{2,1,0:T(8,128)(2,1)S(1)}, u32[]{:S(2)}, u32[]{:S(2)}) async-start(bf16[32,8,128]{2,1,0:T(8,128)(2,1)} %pad.19.clone), calls=%async_computation | async-start | bytes 131072 | tf_op jit(solution)/shard_map/first_exchange/all_to_all | solution.py:304
  38.9 0.0 copy-start.13
  38.9 0.6 fusion
  39.5 0.7 copy-done.13
  40.2 1.1 fusion.24.gram_ref
  41.3 0.7 copy-done.12
  42.0 0.8 fusion.2.normed_ref
  42.8 0.8 copy.39.slot_ref
  43.6 0.1 stack.27.place_ref
  43.6 0.6 fusion.10
  44.3 9.9 %all-to-all-done = bf16[32,8,128]{2,1,0:T(8,128)(2,1)S(1)} async-done(((bf16[32,8,128]{2,1,0:T(8,128)(2,1)}), bf16[32,8,128]{2,1,0:T(8,128)(2,1)S(1)}, u32[]{:S(2)}, u32[]{:S(2)}) %all-to-all-start) | async-done | bytes 65568 | tf_op jit(solution)/shard_map/first_exchange/all_to_all | solution.py:304
  54.2 0.1 slice_add_fusion
  54.3 0.1 eq.66
  54.4 0.3 convolution_convert_fusion.1
  54.7 0.1 copy.38
  54.9 0.1 slice.41
  55.0 0.1 fusion.23
  55.1 0.7 pad_maximum_fusion
  55.8 4.5 %all-to-all-start.1 = ((bf16[32,8,128]{2,1,0:T(8,128)(2,1)}), bf16[32,8,128]{2,1,0:T(8,128)(2,1)}, u32[]{:S(2)}, u32[]{:S(2)}) async-start(bf16[32,8,128]{2,1,0:T(8,128)(2,1)} %pad_maximum_fusion), calls=%async_computation.1 | async-start | bytes 131072 | tf_op jit(solution)/shard_map/second_exchange/all_to_all | solution.py:304
  60.4 24.0 %all-gather.3 = bf16[1024,320]{1,0:T(8,128)(2,1)S(1)} all-gather(bf16[64,320]{1,0:T(8,128)(2,1)} %fusion.10), channel_id=5, replica_groups=mesh['group'=4,'y_hi'=2,'z'=16,'y_lo'=2,'core'=2] {'group','y_lo','core'}, dimensions={0}, use_global_device_ids=true | all-gather | bytes 696320 | tf_op jit(solution)/shard_map/critic_gather/all_gather | solution.py:399
  84.4 0.0 all-to-all-done.1
  84.4 0.9 copy-done.5
  85.3 1.2 unpack.1
  86.5 18.4 %all-gather.2 = bf16[1024,320]{1,0:T(8,128)(2,1)S(1)} all-gather(bf16[64,320]{1,0:T(8,128)(2,1)S(1)} %get-tuple-element.22), channel_id=4, replica_groups=mesh['group'=4,'y_hi'=2,'z'=16,'y_lo'=2,'core'=2] {'group','y_lo','core'}, dimensions={0}, use_global_device_ids=true | all-gather | bytes 696320 | tf_op jit(solution)/shard_map/critic_gather/all_gather | solution.py:397
  104.9 0.4 side_by_side.1
  105.3 0.0 copy-start.1
  105.3 0.8 copy-done.1
  106.1 0.8 copy-done.3
  106.9 5.9 %all-gather.1 = bf16[1024,64]{1,0:T(8,128)(2,1)S(1)} all-gather(bf16[256,64]{1,0:T(8,128)(2,1)S(1)} %get-tuple-element.20), channel_id=3, replica_groups=mesh['group'=4,'y_hi'=2,'z'=16,'y_lo'=2,'core'=2] {'y_lo','core'}, dimensions={0}, use_global_device_ids=true | all-gather | bytes 163840 | tf_op jit(solution)/shard_map/critic_gather/all_gather | solution.py:396
  112.9 1.2 all-gather.6.cloned.1.call-done.weights_ref
  114.1 0.0 copy-start.9
  114.1 0.0 copy-start.10
  114.1 5.7 %forward.1 = (f32[256,640]{1,0:T(8,128)S(1)}, bf16[256,128]{1,0:T(8,128)(2,1)S(1)}, bf16[2560,1280]{1,0:T(8,128)(2,1)S(1)}) custom-call(bf16[256,5120]{1,0:T(8,128)(2,1)S(1)} %fusion.2.normed_ref, bf16[2560,1280]{1,0:T(8,128)(2,1)} %all-gather.6.cloned.1.call-done.weights_ref, bf16[64,640]{1,0:T(8,128)(2,1)} %bitcast.52), custom_call_target="tpu_custom_call" | custom-call | flops 1677721600 | bytes 6553600 | tf_op jit(solution)/shard_map/forward/forward/pallas_call | solution.py:101
  119.8 8.1 %all-gather = bf16[1024,128]{1,0:T(8,128)(2,1)S(1)} all-gather(bf16[256,128]{1,0:T(8,128)(2,1)S(1)} %get-tuple-element.18), channel_id=2, replica_groups=mesh['group'=4,'y_hi'=2,'z'=16,'y_lo'=2,'core'=2] {'y_lo','core'}, dimensions={0}, use_global_device_ids=true | all-gather | bytes 327680 | tf_op jit(solution)/shard_map/forward/all_gather | solution.py:409
  127.9 0.0 copy-start.18
  127.9 5.9 %critics.1 = (bf16[256,64]{1,0:T(8,128)(2,1)S(1)}, f32[256,1]{1,0:T(8,128)S(1)}, bf16[2,256,1280]{2,1,0:T(8,128)(2,1)}, bf16[2,256,1280]{2,1,0:T(8,128)(2,1)S(1)}) custom-call(s32[9]{0:T(128)S(1)} %stack.27.place_ref, s32[16]{0:T(128)S(1)} %copy-done.10, f32[2,1000]{1,0:T(2,128)S(1)} %copy-done.8, f32[1,1000]{1,0:T(1,128)S(1)} %bitcast.54, ...), custom_call_target="tpu_custom_call" | custom-call | tf_op jit(solution)/shard_map/critics/critics/pallas_call | solution.py:201
  133.8 2.1 %collective-permute-start = (bf16[2,256,1280]{2,1,0:T(8,128)(2,1)}, bf16[2,256,1280]{2,1,0:T(8,128)(2,1)S(1)}, u32[]{:S(2)}, u32[]{:S(2)}) collective-permute-start(bf16[2,256,1280]{2,1,0:T(8,128)(2,1)} %get-tuple-element.29), channel_id=1, source_target_pairs={{0,1},{1,0},{2,3},{3,2},{4,5},{5,4},{6,7},{7,6},{8,9},{9,8},{10,11... | collective-permute-start | bytes 3932168 | tf_op jit(solution)/shard_map/backward/ppermute | solution.py:436
  135.9 0.1 copy.40.inverse_ref
  136.0 0.1 dynamic-slice_convert_fusion
  136.1 0.7 copy.43
  136.8 2.1 %collective-permute-done = bf16[2,256,1280]{2,1,0:T(8,128)(2,1)S(1)} collective-permute-done((bf16[2,256,1280]{2,1,0:T(8,128)(2,1)}, bf16[2,256,1280]{2,1,0:T(8,128)(2,1)S(1)}, u32[]{:S(2)}, u32[]{:S(2)}) %collective-permute-start) | collective-permute-done | bytes 1310752 | tf_op jit(solution)/shard_map/backward/ppermute | solution.py:436
  138.9 0.2 fusion.6
  139.1 2.6 %collective-permute-start.1 = (bf16[256,1280]{1,0:T(8,128)(2,1)S(1)}, bf16[256,1280]{1,0:T(8,128)(2,1)S(1)}, u32[]{:S(2)}, u32[]{:S(2)}) collective-permute-start(bf16[256,1280]{1,0:T(8,128)(2,1)S(1)} %fusion.6), channel_id=1, source_target_pairs={{0,2},{2,0},{1,3},{3,1},{4,6},{6,4},{5,7},{7,5},{8,10},{10,8},{9,1... | collective-permute-start | bytes 1966088 | tf_op jit(solution)/shard_map/backward/ppermute | solution.py:439
  141.7 0.1 multiply_reduce_fusion
  141.8 1.5 fusion.3.near_ref
  143.3 13.9 %collective-permute-done.1.far_ref = bf16[256,1280]{1,0:T(8,128)(2,1)S(1)} collective-permute-done((bf16[256,1280]{1,0:T(8,128)(2,1)S(1)}, bf16[256,1280]{1,0:T(8,128)(2,1)S(1)}, u32[]{:S(2)}, u32[]{:S(2)}) %collective-permute-start.1) | collective-permute-done | bytes 655392 | tf_op jit(solution)/shard_map/backward/ppermute | solution.py:439
  157.2 1.1 finish.1
  (40 shorter events, 0.3 us)
Async XLA Ops:
  7.2 47.3 %copy-start = (bf16[1024,64]{0,1:T(8,128)(2,1)S(1)}, bf16[1024,64]{0,1:T(8,128)(2,1)}, u32[]{:S(2)}) copy-start(bf16[1024,64]{0,1:T(8,128)(2,1)} %param.21) | copy-start | bytes 393220
  7.2 11.0 %copy-start.14 = (bf16[160,320]{1,0:T(8,128)(2,1)S(1)}, bf16[160,320]{1,0:T(8,128)(2,1)}, u32[]{:S(2)}) copy-start(bf16[160,320]{1,0:T(8,128)(2,1)} %param.19) | copy-start | bytes 307204
  7.2 31.6 %copy-start.16 = (bf16[5120]{0:T(1024)(128)(2,1)S(1)}, bf16[5120]{0:T(1024)(128)(2,1)}, u32[]{:S(2)}) copy-start(bf16[5120]{0:T(1024)(128)(2,1)} %param.14) | copy-start | bytes 30724
  7.2 31.7 %copy-start.11 = (bf16[256,5120]{1,0:T(8,128)(2,1)S(1)}, bf16[256,5120]{1,0:T(8,128)(2,1)}, u32[]{:S(2)}) copy-start(bf16[256,5120]{1,0:T(8,128)(2,1)} %param.13) | copy-start | bytes 7864324
  7.2 106.9 %all-gather.6.cloned.1.call-start = ((), (), s32[]{:S(2)}) async-start(), calls=%async_computation.2 | async-start | bytes 6963200 | tf_op jit(solution)/shard_map/gather_value/all_gather | solution.py:332
  21.2 33.0 %all-to-all-start = ((bf16[32,8,128]{2,1,0:T(8,128)(2,1)}), bf16[32,8,128]{2,1,0:T(8,128)(2,1)S(1)}, u32[]{:S(2)}, u32[]{:S(2)}) async-start(bf16[32,8,128]{2,1,0:T(8,128)(2,1)} %pad.19.clone), calls=%async_computation | async-start | bytes 131072 | tf_op jit(solution)/shard_map/first_exchange/all_to_all | solution.py:304
  38.9 1.3 copy-start.13
  40.2 1.1 copy-start.17
  40.2 1.8 %copy-start.12 = (bf16[256,5120]{1,0:T(8,128)(2,1)S(1)}, bf16[256,5120]{1,0:T(8,128)(2,1)}, u32[]{:S(2)}) copy-start(bf16[256,5120]{1,0:T(8,128)(2,1)} %param.13) | copy-start | bytes 7864324
  42.0 1.7 %copy-start.15 = (bf16[320,64]{0,1:T(8,128)(2,1)S(1)}, bf16[320,64]{0,1:T(8,128)(2,1)}, u32[]{:S(2)}) copy-start(bf16[320,64]{0,1:T(8,128)(2,1)} %param.20) | copy-start | bytes 122884
  55.8 28.6 %all-to-all-start.1 = ((bf16[32,8,128]{2,1,0:T(8,128)(2,1)}), bf16[32,8,128]{2,1,0:T(8,128)(2,1)}, u32[]{:S(2)}, u32[]{:S(2)}) async-start(bf16[32,8,128]{2,1,0:T(8,128)(2,1)} %pad_maximum_fusion), calls=%async_computation.1 | async-start | bytes 131072 | tf_op jit(solution)/shard_map/second_exchange/all_to_all | solution.py:304
  84.4 0.9 copy-start.5
  105.3 0.8 copy-start.1
  106.1 0.8 copy-start.3
  114.1 13.8 %copy-start.2 = (bf16[64,5120]{1,0:T(8,128)(2,1)S(1)}, bf16[64,5120]{1,0:T(8,128)(2,1)}, u32[]{:S(2)}) copy-start(bf16[64,5120]{1,0:T(8,128)(2,1)} %copy-done.1) | copy-start | bytes 1966084
  114.1 13.8 %copy-start.4 = (bf16[64,5120]{1,0:T(8,128)(2,1)S(1)}, bf16[64,5120]{1,0:T(8,128)(2,1)}, u32[]{:S(2)}) copy-start(bf16[64,5120]{1,0:T(8,128)(2,1)} %copy-done.3) | copy-start | bytes 1966084
  114.1 13.8 %copy-start.6 = (bf16[640,64]{0,1:T(8,128)(2,1)S(1)}, bf16[640,64]{0,1:T(8,128)(2,1)}, u32[]{:S(2)}) copy-start(bf16[640,64]{0,1:T(8,128)(2,1)} %param.16) | copy-start | bytes 245764
  114.1 13.8 %copy-start.7 = (f32[2,64,64]{2,1,0:T(8,128)S(1)}, f32[2,64,64]{2,1,0:T(8,128)}, u32[]{:S(2)}) copy-start(f32[2,64,64]{2,1,0:T(8,128)} %fusion.24.gram_ref) | copy-start | bytes 98308
  114.1 13.8 %copy-start.8 = (f32[2,1000]{1,0:T(2,128)S(1)}, f32[2,1000]{1,0:T(2,128)}, u32[]{:S(2)}) copy-start(f32[2,1000]{1,0:T(2,128)} %mix_ref.1) | copy-start | bytes 24004
  114.1 13.8 %copy-start.9 = (f32[1000]{0:T(1024)S(1)}, f32[1000]{0:T(1024)}, u32[]{:S(2)}) copy-start(f32[1000]{0:T(1024)} %param.25) | copy-start | bytes 12004
  114.1 13.8 %copy-start.10 = (s32[16]{0:T(128)S(1)}, s32[16]{0:T(128)}, u32[]{:S(2)}) copy-start(s32[16]{0:T(128)} %tsteps_ref.1) | copy-start | bytes 196
  127.9 7.9 %copy-start.18 = (f32[256]{0:T(256)S(1)}, f32[256]{0:T(256)}, u32[]{:S(2)}) copy-start(f32[256]{0:T(256)} %copy-done.17) | copy-start | bytes 3076
  133.8 5.1 %collective-permute-start = (bf16[2,256,1280]{2,1,0:T(8,128)(2,1)}, bf16[2,256,1280]{2,1,0:T(8,128)(2,1)S(1)}, u32[]{:S(2)}, u32[]{:S(2)}) collective-permute-start(bf16[2,256,1280]{2,1,0:T(8,128)(2,1)} %get-tuple-element.29), channel_id=1, source_target_pairs={{0,1},{1,0},{2,3},{3,2},{4,5},{5,4},{6,7},{7,6},{8,9},{9,8},{10,11... | collective-permute-start | bytes 3932168 | tf_op jit(solution)/shard_map/backward/ppermute | solution.py:436
  139.1 18.1 %collective-permute-start.1 = (bf16[256,1280]{1,0:T(8,128)(2,1)S(1)}, bf16[256,1280]{1,0:T(8,128)(2,1)S(1)}, u32[]{:S(2)}, u32[]{:S(2)}) collective-permute-start(bf16[256,1280]{1,0:T(8,128)(2,1)S(1)} %fusion.6), channel_id=1, source_target_pairs={{0,2},{2,0},{1,3},{3,1},{4,6},{6,4},{5,7},{7,5},{8,10},{10,8},{9,1... | collective-permute-start | bytes 1966088 | tf_op jit(solution)/shard_map/backward/ppermute | solution.py:439
Sparse Core Ops, SparseCore 0:
  17.1 96.9 all-gather.5

commit v7 on v6

--- a/solution.py
+++ b/solution.py
@@ -60,7 +60,7 @@
     copies = fetch(weights_ref, held, sems)
     head_copy = pltpu.make_async_copy(head_ref, head_held, head_sem)
     head_copy.start()
-    steps = 10
+    steps = 4
     each = len(copies) // steps
     half, cols = held.shape[0], total.shape[1]
     deep = half // steps
@@ -110,7 +110,7 @@
         scratch_shapes=[
             pltpu.VMEM(gen_head.shape, BF16),
             pltpu.VMEM((rows, cols), F32),
-            pltpu.SemaphoreType.DMA((20,)),
+            pltpu.SemaphoreType.DMA((8,)),
             pltpu.SemaphoreType.DMA,
         ],
         compiler_params=pltpu.CompilerParams(vmem_limit_bytes=BUSY),
@@ -165,11 +165,12 @@
     exact = noisy.astype(F32)
     rows = noisy.shape[0]
     scales = []
+    turned = jnp.dot(
+        exact, gram_ref[...], precision=lax.Precision.HIGHEST, preferred_element_type=F32
+    )
     for which in range(2):
-        turned = jnp.dot(
-            exact, gram_ref[which], precision=lax.Precision.HIGHEST, preferred_element_type=F32
-        )
-        square = jnp.sum(turned * exact, axis=1, keepdims=True) / width
+        own = turned[:, which * latent_width : (which + 1) * latent_width]
+        square = jnp.sum(own * exact, axis=1, keepdims=True) / width
         scales.append(lax.rsqrt(jnp.maximum(square, 0.0) + 1e-06))
     wide = 256
     count = matrix_ref.shape[1] // wide
@@ -373,6 +374,7 @@
         gram = lax.dot_general(
             critic_embed, critic_embed, (((2,), (2,)), ((0,), (0,))), preferred_element_type=F32
         )
+        gram = jnp.concatenate([gram[0], gram[1]], axis=1)
         got, gram = lax.optimization_barrier((swap_all(sent), gram))
 
     with jax.named_scope("noise_replies"):

time: 166 us -> 164 us (0.988)
    unnamed x41 -> x39, local copies, waits for them, and re-layouts: 4.87 us -> 4.18 us
where the time goes in v7:
time: 164 us
  blocking collectives  65.4 us (40%)
  waiting for transfers between devices  27.7 us (17%)
  starting transfers between devices  27.4 us (17%)
  between operations  14.5 us (9%)
  Pallas kernels  13.7 us (8%)
  other arithmetic  7.21 us (4%)
  local copies, waits for them, and re-layouts  6.52 us (4%)
    all_gather x1, blocking collectives, local(): heads = lax.all_gather(head, ('group',) + TP, axis=0)  24.5 us
    all_to_all x2, starting transfers between devices, swap_all(): return lax.all_to_all(x, SEQ, split_axis=0, concat_axis=0, tiled=True)  22.2 us
    all_gather x1, blocking collectives, local(): matrices = lax.all_gather(matrix, ('group',) + TP, axis=0)  18.4 us
    ppermute x1, waiting for transfers between devices, local(): far = lax.ppermute(far, 'y_lo', SWAP)  13.3 us
    all_to_all x2, waiting for transfers between devices, swap_all(): return lax.all_to_all(x, SEQ, split_axis=0, concat_axis=0, tiled=True)  9.97 us
    all_gather x1, blocking collectives, local(): gen_pair = lax.all_gather(gen_value, 'y_hi', axis=1, tiled=True)  9.61 us
    all_gather x1, blocking collectives, local(): parts = lax.all_gather(part, TP, axis=0)  7 us
    pallas_call x1, Pallas kernels, critics(): pl.pallas_call(functools.partial(critic_kernel, width), in_specs=[smem] *...  5.95 us
  transfers between devices with their start and end apart: 5, of which 4 were waited for; matrix products, arithmetic and copies ran while one was open for 7% of the time, Pallas kernels for 1%

profile of v7, /device:TPU:1, one launch (start us, length us, event | category | flops | bytes accessed | tf_op | source)
XLA Modules:
  0.0 163.8 jit_solution(8356509413362713462)
XLA Ops:
  7.2 0.0 copy-start
  7.2 0.0 all-gather.6.cloned.1.call-start
  7.3 9.6 %all_gather.30 = bf16[160,1280]{1,0:T(8,128)(2,1)} all-gather(bf16[160,640]{1,0:T(8,128)(2,1)} %param.15), channel_id=1, replica_groups=mesh['group'=4,'y_hi'=2,'z'=16,'y_lo'=2,'core'=2] {'y_hi'}, dimensions={1}, use_global_device_ids=true | all-gather | bytes 614400 | tf_op jit(solution)/shard_map/gather_value/all_gather | solution.py:332
  16.9 0.0 all-gather.6.cloned.1.call-update
  16.9 0.7 and_select_fusion.3
  17.6 0.2 fusion.5
  17.9 0.1 select_reduce_fusion
  18.0 0.1 reshape.144
  18.1 0.1 copy.35
  18.2 0.8 dynamic-slice_convert_fusion.1
  19.0 0.0 copy-done.12
  19.0 0.1 convert_multiply_fusion.2
  19.1 0.3 fusion.4
  19.4 0.1 copy.36
  19.5 0.1 convert_element_type.101
  19.7 0.1 maximum_maximum_fusion
  19.8 0.6 pad.19.clone
  20.4 17.6 %all-to-all-start = ((bf16[32,8,128]{2,1,0:T(8,128)(2,1)}), bf16[32,8,128]{2,1,0:T(8,128)(2,1)S(1)}, u32[]{:S(2)}, u32[]{:S(2)}) async-start(bf16[32,8,128]{2,1,0:T(8,128)(2,1)} %pad.19.clone), calls=%async_computation | async-start | bytes 131072 | tf_op jit(solution)/shard_map/first_exchange/all_to_all | solution.py:305
  38.1 0.0 copy-start.11
  38.1 0.5 fusion.24
  38.6 0.7 pad_maximum_fusion.1.gram_ref
  39.3 0.7 copy-done.11
  39.9 0.6 fusion
  40.6 0.0 copy-start.14
  40.6 0.8 fusion.2.normed_ref
  41.4 0.8 copy.39.slot_ref
  42.2 0.1 stack.27.place_ref
  42.3 0.6 fusion.10
  42.9 10.0 %all-to-all-done = bf16[32,8,128]{2,1,0:T(8,128)(2,1)S(1)} async-done(((bf16[32,8,128]{2,1,0:T(8,128)(2,1)}), bf16[32,8,128]{2,1,0:T(8,128)(2,1)S(1)}, u32[]{:S(2)}, u32[]{:S(2)}) %all-to-all-start) | async-done | bytes 65568 | tf_op jit(solution)/shard_map/first_exchange/all_to_all | solution.py:305
  52.9 0.1 slice_add_fusion
  53.0 0.1 eq.66
  53.1 0.3 convolution_convert_fusion.1
  53.4 0.1 copy.38
  53.5 0.1 slice.49
  53.6 0.1 fusion.23
  53.7 0.7 pad_maximum_fusion
  54.5 4.5 %all-to-all-start.1 = ((bf16[32,8,128]{2,1,0:T(8,128)(2,1)}), bf16[32,8,128]{2,1,0:T(8,128)(2,1)}, u32[]{:S(2)}, u32[]{:S(2)}) async-start(bf16[32,8,128]{2,1,0:T(8,128)(2,1)} %pad_maximum_fusion), calls=%async_computation.1 | async-start | bytes 131072 | tf_op jit(solution)/shard_map/second_exchange/all_to_all | solution.py:305
  59.0 24.5 %all-gather.3 = bf16[1024,320]{1,0:T(8,128)(2,1)S(1)} all-gather(bf16[64,320]{1,0:T(8,128)(2,1)} %fusion.10), channel_id=5, replica_groups=mesh['group'=4,'y_hi'=2,'z'=16,'y_lo'=2,'core'=2] {'group','y_lo','core'}, dimensions={0}, use_global_device_ids=true | all-gather | bytes 696320 | tf_op jit(solution)/shard_map/critic_gather/all_gather | solution.py:401
  83.5 0.0 all-to-all-done.1
  83.5 0.9 copy-done.5
  84.4 1.2 unpack.1
  85.6 18.4 %all-gather.2 = bf16[1024,320]{1,0:T(8,128)(2,1)S(1)} all-gather(bf16[64,320]{1,0:T(8,128)(2,1)S(1)} %get-tuple-element.22), channel_id=4, replica_groups=mesh['group'=4,'y_hi'=2,'z'=16,'y_lo'=2,'core'=2] {'group','y_lo','core'}, dimensions={0}, use_global_device_ids=true | all-gather | bytes 696320 | tf_op jit(solution)/shard_map/critic_gather/all_gather | solution.py:399
  104.0 0.4 side_by_side.1
  104.3 0.0 copy-start.1
  104.3 0.8 copy-done.1
  105.2 0.8 copy-done.3
  106.0 5.9 %all-gather.1 = bf16[1024,64]{1,0:T(8,128)(2,1)S(1)} all-gather(bf16[256,64]{1,0:T(8,128)(2,1)S(1)} %get-tuple-element.20), channel_id=3, replica_groups=mesh['group'=4,'y_hi'=2,'z'=16,'y_lo'=2,'core'=2] {'y_lo','core'}, dimensions={0}, use_global_device_ids=true | all-gather | bytes 163840 | tf_op jit(solution)/shard_map/critic_gather/all_gather | solution.py:398
  111.9 2.3 %all-gather.6.cloned.1.call-done.weights_ref = bf16[2560,1280]{1,0:T(8,128)(2,1)} async-done(((bf16[160,1280]{1,0:T(8,128)(2,1)}), bf16[2560,1280]{1,0:T(8,128)(2,1)}) %all-gather.6.cloned.1.call-update) | async-done | bytes 6553616 | tf_op jit(solution)/shard_map/gather_value/all_gather | solution.py:333
  114.3 0.0 copy-start.9
  114.3 0.0 copy-start.10
  114.3 5.2 %forward.1 = (f32[256,640]{1,0:T(8,128)S(1)}, bf16[256,128]{1,0:T(8,128)(2,1)S(1)}, bf16[2560,1280]{1,0:T(8,128)(2,1)S(1)}) custom-call(bf16[256,5120]{1,0:T(8,128)(2,1)S(1)} %fusion.2.normed_ref, bf16[2560,1280]{1,0:T(8,128)(2,1)} %all-gather.6.cloned.1.call-done.weights_ref, bf16[64,640]{1,0:T(8,128)(2,1)} %bitcast.56), custom_call_target="tpu_custom_call" | custom-call | flops 1677721600 | bytes 6553600 | tf_op jit(solution)/shard_map/forward/forward/pallas_call | solution.py:101
  119.5 7.0 %all-gather = bf16[1024,128]{1,0:T(8,128)(2,1)S(1)} all-gather(bf16[256,128]{1,0:T(8,128)(2,1)S(1)} %get-tuple-element.18), channel_id=2, replica_groups=mesh['group'=4,'y_hi'=2,'z'=16,'y_lo'=2,'core'=2] {'y_lo','core'}, dimensions={0}, use_global_device_ids=true | all-gather | bytes 327680 | tf_op jit(solution)/shard_map/forward/all_gather | solution.py:411
  126.5 6.0 %critics.1 = (bf16[256,64]{1,0:T(8,128)(2,1)S(1)}, f32[256,1]{1,0:T(8,128)S(1)}, bf16[2,256,1280]{2,1,0:T(8,128)(2,1)}, bf16[2,256,1280]{2,1,0:T(8,128)(2,1)S(1)}) custom-call(s32[9]{0:T(128)S(1)} %stack.27.place_ref, s32[16]{0:T(128)S(1)} %copy-done.10, f32[2,1000]{1,0:T(2,128)S(1)} %copy-done.8, f32[1,1000]{1,0:T(1,128)S(1)} %bitcast.58, ...), custom_call_target="tpu_custom_call" | custom-call | tf_op jit(solution)/shard_map/critics/critics/pallas_call | solution.py:202
  132.5 2.1 %collective-permute-start = (bf16[2,256,1280]{2,1,0:T(8,128)(2,1)}, bf16[2,256,1280]{2,1,0:T(8,128)(2,1)S(1)}, u32[]{:S(2)}, u32[]{:S(2)}) collective-permute-start(bf16[2,256,1280]{2,1,0:T(8,128)(2,1)} %get-tuple-element.29), channel_id=1, source_target_pairs={{0,1},{1,0},{2,3},{3,2},{4,5},{5,4},{6,7},{7,6},{8,9},{9,8},{10,11... | collective-permute-start | bytes 3932168 | tf_op jit(solution)/shard_map/backward/ppermute | solution.py:438
  134.6 0.1 copy.40.inverse_ref
  134.7 0.1 dynamic-slice_convert_fusion
  134.8 0.7 copy.43
  135.5 2.1 %collective-permute-done = bf16[2,256,1280]{2,1,0:T(8,128)(2,1)S(1)} collective-permute-done((bf16[2,256,1280]{2,1,0:T(8,128)(2,1)}, bf16[2,256,1280]{2,1,0:T(8,128)(2,1)S(1)}, u32[]{:S(2)}, u32[]{:S(2)}) %collective-permute-start) | collective-permute-done | bytes 1310752 | tf_op jit(solution)/shard_map/backward/ppermute | solution.py:438
  137.6 0.2 fusion.6
  137.8 3.1 %collective-permute-start.1 = (bf16[256,1280]{1,0:T(8,128)(2,1)S(1)}, bf16[256,1280]{1,0:T(8,128)(2,1)S(1)}, u32[]{:S(2)}, u32[]{:S(2)}) collective-permute-start(bf16[256,1280]{1,0:T(8,128)(2,1)S(1)} %fusion.6), channel_id=1, source_target_pairs={{0,2},{2,0},{1,3},{3,1},{4,6},{6,4},{5,7},{7,5},{8,10},{10,8},{9,1... | collective-permute-start | bytes 1966088 | tf_op jit(solution)/shard_map/backward/ppermute | solution.py:441
  141.0 0.1 multiply_reduce_fusion
  141.1 1.5 fusion.3.near_ref
  142.5 13.3 %collective-permute-done.1.far_ref = bf16[256,1280]{1,0:T(8,128)(2,1)S(1)} collective-permute-done((bf16[256,1280]{1,0:T(8,128)(2,1)S(1)}, bf16[256,1280]{1,0:T(8,128)(2,1)S(1)}, u32[]{:S(2)}, u32[]{:S(2)}) %collective-permute-start.1) | collective-permute-done | bytes 655392 | tf_op jit(solution)/shard_map/backward/ppermute | solution.py:441
  155.9 1.1 finish.1
  (40 shorter events, 0.3 us)
Async XLA Ops:
  7.2 45.9 %copy-start = (bf16[1024,64]{0,1:T(8,128)(2,1)S(1)}, bf16[1024,64]{0,1:T(8,128)(2,1)}, u32[]{:S(2)}) copy-start(bf16[1024,64]{0,1:T(8,128)(2,1)} %param.21) | copy-start | bytes 393220
  7.2 10.9 %copy-start.13 = (bf16[160,320]{1,0:T(8,128)(2,1)S(1)}, bf16[160,320]{1,0:T(8,128)(2,1)}, u32[]{:S(2)}) copy-start(bf16[160,320]{1,0:T(8,128)(2,1)} %param.19) | copy-start | bytes 307204
  7.2 11.8 %copy-start.12 = (bf16[2,64,5120]{2,1,0:T(8,128)(2,1)S(1)}, bf16[2,64,5120]{2,1,0:T(8,128)(2,1)}, u32[]{:S(2)}) copy-start(bf16[2,64,5120]{2,1,0:T(8,128)(2,1)} %param.17) | copy-start | bytes 3932164
  7.2 30.8 %copy-start.15 = (bf16[5120]{0:T(1024)(128)(2,1)S(1)}, bf16[5120]{0:T(1024)(128)(2,1)}, u32[]{:S(2)}) copy-start(bf16[5120]{0:T(1024)(128)(2,1)} %param.14) | copy-start | bytes 30724
  7.2 107.0 %all-gather.6.cloned.1.call-start = ((), (), s32[]{:S(2)}) async-start(), calls=%async_computation.2 | async-start | bytes 6963200 | tf_op jit(solution)/shard_map/gather_value/all_gather | solution.py:333
  20.4 32.5 %all-to-all-start = ((bf16[32,8,128]{2,1,0:T(8,128)(2,1)}), bf16[32,8,128]{2,1,0:T(8,128)(2,1)S(1)}, u32[]{:S(2)}, u32[]{:S(2)}) async-start(bf16[32,8,128]{2,1,0:T(8,128)(2,1)} %pad.19.clone), calls=%async_computation | async-start | bytes 131072 | tf_op jit(solution)/shard_map/first_exchange/all_to_all | solution.py:305
  38.1 1.9 %copy-start.11 = (bf16[256,5120]{1,0:T(8,128)(2,1)S(1)}, bf16[256,5120]{1,0:T(8,128)(2,1)}, u32[]{:S(2)}) copy-start(bf16[256,5120]{1,0:T(8,128)(2,1)} %param.13) | copy-start | bytes 7864324
  40.6 0.8 copy-start.16
  40.6 1.7 %copy-start.14 = (bf16[320,64]{0,1:T(8,128)(2,1)S(1)}, bf16[320,64]{0,1:T(8,128)(2,1)}, u32[]{:S(2)}) copy-start(bf16[320,64]{0,1:T(8,128)(2,1)} %param.20) | copy-start | bytes 122884
  54.5 29.0 %all-to-all-start.1 = ((bf16[32,8,128]{2,1,0:T(8,128)(2,1)}), bf16[32,8,128]{2,1,0:T(8,128)(2,1)}, u32[]{:S(2)}, u32[]{:S(2)}) async-start(bf16[32,8,128]{2,1,0:T(8,128)(2,1)} %pad_maximum_fusion), calls=%async_computation.1 | async-start | bytes 131072 | tf_op jit(solution)/shard_map/second_exchange/all_to_all | solution.py:305
  83.5 0.9 copy-start.5
  104.3 0.8 copy-start.1
  105.2 0.8 copy-start.3
  114.3 12.2 %copy-start.2 = (bf16[64,5120]{1,0:T(8,128)(2,1)S(1)}, bf16[64,5120]{1,0:T(8,128)(2,1)}, u32[]{:S(2)}) copy-start(bf16[64,5120]{1,0:T(8,128)(2,1)} %copy-done.1) | copy-start | bytes 1966084
  114.3 12.2 %copy-start.4 = (bf16[64,5120]{1,0:T(8,128)(2,1)S(1)}, bf16[64,5120]{1,0:T(8,128)(2,1)}, u32[]{:S(2)}) copy-start(bf16[64,5120]{1,0:T(8,128)(2,1)} %copy-done.3) | copy-start | bytes 1966084
  114.3 12.2 %copy-start.6 = (bf16[640,64]{0,1:T(8,128)(2,1)S(1)}, bf16[640,64]{0,1:T(8,128)(2,1)}, u32[]{:S(2)}) copy-start(bf16[640,64]{0,1:T(8,128)(2,1)} %param.16) | copy-start | bytes 245764
  114.3 12.2 %copy-start.7 = (f32[64,128]{1,0:T(8,128)S(1)}, f32[64,128]{1,0:T(8,128)}, u32[]{:S(2)}) copy-start(f32[64,128]{1,0:T(8,128)} %pad_maximum_fusion.1.gram_ref) | copy-start | bytes 98308
  114.3 12.2 %copy-start.8 = (f32[2,1000]{1,0:T(2,128)S(1)}, f32[2,1000]{1,0:T(2,128)}, u32[]{:S(2)}) copy-start(f32[2,1000]{1,0:T(2,128)} %mix_ref.1) | copy-start | bytes 24004
  114.3 12.2 %copy-start.9 = (f32[1000]{0:T(1024)S(1)}, f32[1000]{0:T(1024)}, u32[]{:S(2)}) copy-start(f32[1000]{0:T(1024)} %param.25) | copy-start | bytes 12004
  114.3 12.2 %copy-start.10 = (s32[16]{0:T(128)S(1)}, s32[16]{0:T(128)}, u32[]{:S(2)}) copy-start(s32[16]{0:T(128)} %tsteps_ref.1) | copy-start | bytes 196
  126.5 8.0 %copy-start.17 = (f32[256]{0:T(256)S(1)}, f32[256]{0:T(256)}, u32[]{:S(2)}) copy-start(f32[256]{0:T(256)} %copy-done.16) | copy-start | bytes 3076
  132.5 5.1 %collective-permute-start = (bf16[2,256,1280]{2,1,0:T(8,128)(2,1)}, bf16[2,256,1280]{2,1,0:T(8,128)(2,1)S(1)}, u32[]{:S(2)}, u32[]{:S(2)}) collective-permute-start(bf16[2,256,1280]{2,1,0:T(8,128)(2,1)} %get-tuple-element.29), channel_id=1, source_target_pairs={{0,1},{1,0},{2,3},{3,2},{4,5},{5,4},{6,7},{7,6},{8,9},{9,8},{10,11... | collective-permute-start | bytes 3932168 | tf_op jit(solution)/shard_map/backward/ppermute | solution.py:438
  137.8 18.1 %collective-permute-start.1 = (bf16[256,1280]{1,0:T(8,128)(2,1)S(1)}, bf16[256,1280]{1,0:T(8,128)(2,1)S(1)}, u32[]{:S(2)}, u32[]{:S(2)}) collective-permute-start(bf16[256,1280]{1,0:T(8,128)(2,1)S(1)} %fusion.6), channel_id=1, source_target_pairs={{0,2},{2,0},{1,3},{3,1},{4,6},{6,4},{5,7},{7,5},{8,10},{10,8},{9,1... | collective-permute-start | bytes 1966088 | tf_op jit(solution)/shard_map/backward/ppermute | solution.py:441
Sparse Core Ops, SparseCore 0:
  17.0 97.1 all-gather.5

commit v8 on v7

--- a/solution.py
+++ b/solution.py
@@ -150,6 +150,7 @@
     latent_ref,
     mixed_ref,
     sent_ref,
+    other_ref,
     kept_ref,
 ):
     level = tsteps_ref[place_ref[0]]
@@ -185,9 +186,9 @@
     mixed_ref[...] = jnp.sum(cot * parts[:, latent_width:], axis=1, keepdims=True)
     grad_act = jnp.dot(cotangent, gen_head_ref[...], preferred_element_type=F32)
     grad_values = (slope_ref[...] * grad_act).astype(BF16)
-    for i in range(2):
+    for i, out_ref in enumerate((sent_ref, other_ref)):
         row, col = place_ref[1 + 2 * i], place_ref[2 + 2 * i]
-        store_slice(grad_values, weights_ref, row, col, sent_ref.at[i])
+        store_slice(grad_values, weights_ref, row, col, out_ref)
     for i in range(2):
         row, col = place_ref[5 + 2 * i], place_ref[6 + 2 * i]
         store_slice(grad_values, weights_ref, row, col, kept_ref.at[i])
@@ -202,11 +203,12 @@
     return pl.pallas_call(
         functools.partial(critic_kernel, width),
         in_specs=[smem] * 4 + [vmem] * 8,
-        out_specs=[vmem] * 4,
+        out_specs=[vmem] * 5,
         out_shape=[
             jax.ShapeDtypeStruct((rows, latent_width), BF16),
             jax.ShapeDtypeStruct((rows, 1), F32),
-            jax.ShapeDtypeStruct((2, rows, columns), BF16),
+            jax.ShapeDtypeStruct((rows, columns), BF16),
+            jax.ShapeDtypeStruct((rows, columns), BF16),
             jax.ShapeDtypeStruct((2, rows, columns), BF16),
         ],
         compiler_params=pltpu.CompilerParams(vmem_limit_bytes=BUSY),
@@ -414,7 +416,7 @@
         frame = shard_id * rows // FTOK
         place = jnp.stack([frame, 1 - c, 1 - yl, 1 - c, yl, c, 1 - yl, c, yl]).astype(jnp.int32)
         tables = (tsteps, noise_mix, gap_weight[None, :])
-        gen_latent, mixed, sent, kept = critics(
+        gen_latent, mixed, sent, other, kept = critics(
             width,
             place,
             tables,
@@ -436,10 +438,11 @@
         slope_out = inverse * gain[None, :]
         pulled = inverse * inverse * (mixed / width)
         got = lax.ppermute(sent, "core", SWAP)
-        far = (kept[0].astype(F32) + got[0].astype(F32)).astype(BF16)
-        far, kept, got = lax.optimization_barrier((far, kept, got))
+        other = lax.ppermute(other, "core", SWAP)
+        far = (kept[0].astype(F32) + got.astype(F32)).astype(BF16)
+        far, kept = lax.optimization_barrier((far, kept))
         far = lax.ppermute(far, "y_lo", SWAP)
-        near = kept[1].astype(F32) + got[1].astype(F32)
+        near = kept[1].astype(F32) + other.astype(F32)
         near = slope_out * near - own * pulled
         grad_hidden = finish(near, far, inverse, gain[None, :])
     return (gen_latent, grad_hidden)

time: 164 us -> 166 us (1.012)
  waiting for transfers between devices: 27.7 us -> 25.3 us
  starting transfers between devices: 27.4 us -> 29.4 us
    ppermute x0 -> x1, starting transfers between devices: none -> 2.26 us  [local(): other = lax.ppermute(other, 'core', SWAP)]
    ppermute x1, waiting for transfers between devices: 2.11 us -> 0.01 us  [local(): got = lax.ppermute(sent, 'core', SWAP)]
  transfers between devices with their start and end apart: 5 -> 6, of which waited for: 4 -> 3; matrix products, arithmetic and copies ran while one was open for 7% -> 8% of each run, Pallas kernels for 1% -> 1%
where the time goes in v8:
time: 166 us; the launch traced here: 165 us
  blocking collectives  66.4 us (40%)
  starting transfers between devices  29.4 us (18%)
  waiting for transfers between devices  25.3 us (15%)
  between operations  14.5 us (9%)
  Pallas kernels  13.5 us (8%)
  other arithmetic  8.26 us (5%)
  local copies, waits for them, and re-layouts  6.53 us (4%)
    all_gather x1, blocking collectives, local(): heads = lax.all_gather(head, ('group',) + TP, axis=0)  24.7 us
    all_to_all x2, starting transfers between devices, swap_all(): return lax.all_to_all(x, SEQ, split_axis=0, concat_axis=0, tiled=True)  22.2 us
    all_gather x1, blocking collectives, local(): matrices = lax.all_gather(matrix, ('group',) + TP, axis=0)  18.4 us
    ppermute x1, waiting for transfers between devices, local(): far = lax.ppermute(far, 'y_lo', SWAP)  13.6 us
    all_to_all x2, waiting for transfers between devices, swap_all(): return lax.all_to_all(x, SEQ, split_axis=0, concat_axis=0, tiled=True)  9.77 us
    all_gather x1, blocking collectives, local(): gen_pair = lax.all_gather(gen_value, 'y_hi', axis=1, tiled=True)  9.62 us
    all_gather x1, blocking collectives, local(): parts = lax.all_gather(part, TP, axis=0)  7.75 us
    all_gather x1, blocking collectives, local(): noise_parts = lax.all_gather(own_noise, TP, axis=0)  5.95 us
  transfers between devices with their start and end apart: 6, of which 3 were waited for; matrix products, arithmetic and copies ran while one was open for 8% of the time, Pallas kernels for 1%

profile of v8, /device:TPU:1, one launch (start us, length us, event | category | flops | bytes accessed | tf_op | source)
XLA Modules:
  0.0 165.2 jit_solution(6074522915699853228)
XLA Ops:
  7.2 0.0 copy-start
  7.2 0.0 all-gather.6.cloned.1.call-start
  7.3 9.6 %all_gather.30 = bf16[160,1280]{1,0:T(8,128)(2,1)} all-gather(bf16[160,640]{1,0:T(8,128)(2,1)} %param.15), channel_id=1, replica_groups=mesh['group'=4,'y_hi'=2,'z'=16,'y_lo'=2,'core'=2] {'y_hi'}, dimensions={1}, use_global_device_ids=true | all-gather | bytes 614400 | tf_op jit(solution)/shard_map/gather_value/all_gather | solution.py:334
  16.9 0.0 all-gather.6.cloned.1.call-update
  16.9 0.7 and_select_fusion.3
  17.6 0.2 fusion.7
  17.9 0.1 select_reduce_fusion
  18.0 0.1 reshape.141
  18.1 0.1 copy.35
  18.2 0.8 dynamic-slice_convert_fusion.1
  19.0 0.1 convert_multiply_fusion.2
  19.1 0.3 fusion.6
  19.4 0.1 copy.36
  19.5 0.1 convert_element_type.100
  19.7 0.1 maximum_maximum_fusion
  19.8 0.6 pad.19.clone
  20.4 17.6 %all-to-all-start = ((bf16[32,8,128]{2,1,0:T(8,128)(2,1)}), bf16[32,8,128]{2,1,0:T(8,128)(2,1)S(1)}, u32[]{:S(2)}, u32[]{:S(2)}) async-start(bf16[32,8,128]{2,1,0:T(8,128)(2,1)} %pad.19.clone), calls=%async_computation | async-start | bytes 131072 | tf_op jit(solution)/shard_map/first_exchange/all_to_all | solution.py:307
  38.1 0.0 copy-start.11
  38.1 0.5 fusion.25
  38.6 0.7 pad_maximum_fusion.1.gram_ref
  39.3 0.7 copy-done.11
  39.9 0.6 fusion
  40.6 0.0 copy-start.14
  40.6 0.8 fusion.2.normed_ref
  41.4 0.8 copy.39.slot_ref
  42.2 0.1 stack.27.place_ref
  42.3 0.6 fusion.11
  42.9 9.8 %all-to-all-done = bf16[32,8,128]{2,1,0:T(8,128)(2,1)S(1)} async-done(((bf16[32,8,128]{2,1,0:T(8,128)(2,1)}), bf16[32,8,128]{2,1,0:T(8,128)(2,1)S(1)}, u32[]{:S(2)}, u32[]{:S(2)}) %all-to-all-start) | async-done | bytes 65568 | tf_op jit(solution)/shard_map/first_exchange/all_to_all | solution.py:307
  52.7 0.1 slice_add_fusion
  52.8 0.1 eq.66
  52.9 0.3 convolution_convert_fusion.1
  53.2 0.1 copy.38
  53.3 0.1 slice.43
  53.4 0.1 fusion.24
  53.5 0.7 pad_maximum_fusion
  54.2 4.6 %all-to-all-start.1 = ((bf16[32,8,128]{2,1,0:T(8,128)(2,1)}), bf16[32,8,128]{2,1,0:T(8,128)(2,1)}, u32[]{:S(2)}, u32[]{:S(2)}) async-start(bf16[32,8,128]{2,1,0:T(8,128)(2,1)} %pad_maximum_fusion), calls=%async_computation.1 | async-start | bytes 131072 | tf_op jit(solution)/shard_map/second_exchange/all_to_all | solution.py:307
  58.8 24.7 %all-gather.3 = bf16[1024,320]{1,0:T(8,128)(2,1)S(1)} all-gather(bf16[64,320]{1,0:T(8,128)(2,1)} %fusion.11), channel_id=5, replica_groups=mesh['group'=4,'y_hi'=2,'z'=16,'y_lo'=2,'core'=2] {'group','y_lo','core'}, dimensions={0}, use_global_device_ids=true | all-gather | bytes 696320 | tf_op jit(solution)/shard_map/critic_gather/all_gather | solution.py:403
  83.5 0.9 copy-done.5
  84.4 1.2 unpack.1
  85.6 18.4 %all-gather.2 = bf16[1024,320]{1,0:T(8,128)(2,1)S(1)} all-gather(bf16[64,320]{1,0:T(8,128)(2,1)S(1)} %get-tuple-element.22), channel_id=4, replica_groups=mesh['group'=4,'y_hi'=2,'z'=16,'y_lo'=2,'core'=2] {'group','y_lo','core'}, dimensions={0}, use_global_device_ids=true | all-gather | bytes 696320 | tf_op jit(solution)/shard_map/critic_gather/all_gather | solution.py:401
  104.0 0.4 side_by_side.1
  104.3 0.0 copy-start.1
  104.3 0.8 copy-done.1
  105.2 0.8 copy-done.3
  106.0 5.9 %all-gather.1 = bf16[1024,64]{1,0:T(8,128)(2,1)S(1)} all-gather(bf16[256,64]{1,0:T(8,128)(2,1)S(1)} %get-tuple-element.20), channel_id=3, replica_groups=mesh['group'=4,'y_hi'=2,'z'=16,'y_lo'=2,'core'=2] {'y_lo','core'}, dimensions={0}, use_global_device_ids=true | all-gather | bytes 163840 | tf_op jit(solution)/shard_map/critic_gather/all_gather | solution.py:400
  112.0 1.9 %all-gather.6.cloned.1.call-done.weights_ref = bf16[2560,1280]{1,0:T(8,128)(2,1)} async-done(((bf16[160,1280]{1,0:T(8,128)(2,1)}), bf16[2560,1280]{1,0:T(8,128)(2,1)}) %all-gather.6.cloned.1.call-update) | async-done | bytes 6553616 | tf_op jit(solution)/shard_map/gather_value/all_gather | solution.py:335
  113.9 0.0 copy-start.9
  113.9 0.0 copy-start.10
  113.9 5.2 %forward.1 = (f32[256,640]{1,0:T(8,128)S(1)}, bf16[256,128]{1,0:T(8,128)(2,1)S(1)}, bf16[2560,1280]{1,0:T(8,128)(2,1)S(1)}) custom-call(bf16[256,5120]{1,0:T(8,128)(2,1)S(1)} %fusion.2.normed_ref, bf16[2560,1280]{1,0:T(8,128)(2,1)} %all-gather.6.cloned.1.call-done.weights_ref, bf16[64,640]{1,0:T(8,128)(2,1)} %bitcast.56), custom_call_target="tpu_custom_call" | custom-call | flops 1677721600 | bytes 6553600 | tf_op jit(solution)/shard_map/forward/forward/pallas_call | solution.py:101
  119.1 7.7 %all-gather = bf16[1024,128]{1,0:T(8,128)(2,1)S(1)} all-gather(bf16[256,128]{1,0:T(8,128)(2,1)S(1)} %get-tuple-element.18), channel_id=2, replica_groups=mesh['group'=4,'y_hi'=2,'z'=16,'y_lo'=2,'core'=2] {'y_lo','core'}, dimensions={0}, use_global_device_ids=true | all-gather | bytes 327680 | tf_op jit(solution)/shard_map/forward/all_gather | solution.py:413
  126.9 5.7 %critics.1 = (bf16[256,64]{1,0:T(8,128)(2,1)S(1)}, f32[256,1]{1,0:T(8,128)S(1)}, bf16[256,1280]{1,0:T(8,128)(2,1)}, bf16[256,1280]{1,0:T(8,128)(2,1)S(1)}, bf16[2,256,1280]{2,1,0:T(8,128)(2,1)S(1)}) custom-call(s32[9]{0:T(128)S(1)} %stack.27.place_ref, s32[16]{0:T(128)S(1)} %copy-done.10, f32[2,1000]{1,0:T(2,128)S(1)} %copy-done.8, f32[1,1000]{1,0:T(1,128)S(1)} %bitcast.58, ...), custom_call_target="tpu_custom_call" | custom-call | tf_op jit(solution)/shard_map/critics/critics/pallas_call | solution.py:203
  132.6 2.1 %collective-permute-start = (bf16[256,1280]{1,0:T(8,128)(2,1)}, bf16[256,1280]{1,0:T(8,128)(2,1)}, u32[]{:S(2)}, u32[]{:S(2)}) collective-permute-start(bf16[256,1280]{1,0:T(8,128)(2,1)} %get-tuple-element.29), channel_id=1, source_target_pairs={{0,1},{1,0},{2,3},{3,2},{4,5},{5,4},{6,7},{7,6},{8,9},{9,8},{10,11... | collective-permute-start | bytes 1966088 | tf_op jit(solution)/shard_map/backward/ppermute | solution.py:440
  134.7 2.3 %collective-permute-start.1 = (bf16[256,1280]{1,0:T(8,128)(2,1)S(1)}, bf16[256,1280]{1,0:T(8,128)(2,1)S(1)}, u32[]{:S(2)}, u32[]{:S(2)}) collective-permute-start(bf16[256,1280]{1,0:T(8,128)(2,1)S(1)} %get-tuple-element.31), channel_id=1, source_target_pairs={{0,1},{1,0},{2,3},{3,2},{4,5},{5,4},{6,7},{7,6},{8,9},{9,8},{10,11... | collective-permute-start | bytes 1966088 | tf_op jit(solution)/shard_map/backward/ppermute | solution.py:441
  137.0 0.1 dynamic-slice_convert_fusion
  137.1 0.1 copy.40.inverse_ref
  137.2 0.7 copy.43
  137.9 0.0 collective-permute-done
  137.9 1.2 fusion.5
  139.2 2.8 %collective-permute-start.2 = (bf16[256,1280]{1,0:T(8,128)(2,1)S(1)}, bf16[256,1280]{1,0:T(8,128)(2,1)S(1)}, u32[]{:S(2)}, u32[]{:S(2)}) collective-permute-start(bf16[256,1280]{1,0:T(8,128)(2,1)S(1)} %fusion.5), channel_id=1, source_target_pairs={{0,2},{2,0},{1,3},{3,1},{4,6},{6,4},{5,7},{7,5},{8,10},{10,8},{9,1... | collective-permute-start | bytes 1966088 | tf_op jit(solution)/shard_map/backward/ppermute | solution.py:444
  142.0 0.1 multiply_reduce_fusion
  142.1 0.0 collective-permute-done.1
  142.1 1.5 fusion.4.near_ref
  143.6 13.6 %collective-permute-done.2.far_ref = bf16[256,1280]{1,0:T(8,128)(2,1)S(1)} collective-permute-done((bf16[256,1280]{1,0:T(8,128)(2,1)S(1)}, bf16[256,1280]{1,0:T(8,128)(2,1)S(1)}, u32[]{:S(2)}, u32[]{:S(2)}) %collective-permute-start.2) | collective-permute-done | bytes 655392 | tf_op jit(solution)/shard_map/backward/ppermute | solution.py:444
  157.3 1.1 finish.1
  (42 shorter events, 0.3 us)
Async XLA Ops:
  7.2 45.7 %copy-start = (bf16[1024,64]{0,1:T(8,128)(2,1)S(1)}, bf16[1024,64]{0,1:T(8,128)(2,1)}, u32[]{:S(2)}) copy-start(bf16[1024,64]{0,1:T(8,128)(2,1)} %param.21) | copy-start | bytes 393220
  7.2 10.9 %copy-start.13 = (bf16[160,320]{1,0:T(8,128)(2,1)S(1)}, bf16[160,320]{1,0:T(8,128)(2,1)}, u32[]{:S(2)}) copy-start(bf16[160,320]{1,0:T(8,128)(2,1)} %param.19) | copy-start | bytes 307204
  7.2 11.8 %copy-start.12 = (bf16[2,64,5120]{2,1,0:T(8,128)(2,1)S(1)}, bf16[2,64,5120]{2,1,0:T(8,128)(2,1)}, u32[]{:S(2)}) copy-start(bf16[2,64,5120]{2,1,0:T(8,128)(2,1)} %param.17) | copy-start | bytes 3932164
  7.2 30.8 %copy-start.15 = (bf16[5120]{0:T(1024)(128)(2,1)S(1)}, bf16[5120]{0:T(1024)(128)(2,1)}, u32[]{:S(2)}) copy-start(bf16[5120]{0:T(1024)(128)(2,1)} %param.14) | copy-start | bytes 30724
  7.2 106.7 %all-gather.6.cloned.1.call-start = ((), (), s32[]{:S(2)}) async-start(), calls=%async_computation.2 | async-start | bytes 6963200 | tf_op jit(solution)/shard_map/gather_value/all_gather | solution.py:335
  20.4 32.2 %all-to-all-start = ((bf16[32,8,128]{2,1,0:T(8,128)(2,1)}), bf16[32,8,128]{2,1,0:T(8,128)(2,1)S(1)}, u32[]{:S(2)}, u32[]{:S(2)}) async-start(bf16[32,8,128]{2,1,0:T(8,128)(2,1)} %pad.19.clone), calls=%async_computation | async-start | bytes 131072 | tf_op jit(solution)/shard_map/first_exchange/all_to_all | solution.py:307
  38.1 1.9 %copy-start.11 = (bf16[256,5120]{1,0:T(8,128)(2,1)S(1)}, bf16[256,5120]{1,0:T(8,128)(2,1)}, u32[]{:S(2)}) copy-start(bf16[256,5120]{1,0:T(8,128)(2,1)} %param.13) | copy-start | bytes 7864324
  40.5 0.8 copy-start.16
  40.6 1.7 %copy-start.14 = (bf16[320,64]{0,1:T(8,128)(2,1)S(1)}, bf16[320,64]{0,1:T(8,128)(2,1)}, u32[]{:S(2)}) copy-start(bf16[320,64]{0,1:T(8,128)(2,1)} %param.20) | copy-start | bytes 122884
  54.2 29.2 %all-to-all-start.1 = ((bf16[32,8,128]{2,1,0:T(8,128)(2,1)}), bf16[32,8,128]{2,1,0:T(8,128)(2,1)}, u32[]{:S(2)}, u32[]{:S(2)}) async-start(bf16[32,8,128]{2,1,0:T(8,128)(2,1)} %pad_maximum_fusion), calls=%async_computation.1 | async-start | bytes 131072 | tf_op jit(solution)/shard_map/second_exchange/all_to_all | solution.py:307
  83.5 0.9 copy-start.5
  104.3 0.8 copy-start.1
  105.2 0.9 copy-start.3
  113.9 13.0 %copy-start.2 = (bf16[64,5120]{1,0:T(8,128)(2,1)S(1)}, bf16[64,5120]{1,0:T(8,128)(2,1)}, u32[]{:S(2)}) copy-start(bf16[64,5120]{1,0:T(8,128)(2,1)} %copy-done.1) | copy-start | bytes 1966084
  113.9 13.0 %copy-start.4 = (bf16[64,5120]{1,0:T(8,128)(2,1)S(1)}, bf16[64,5120]{1,0:T(8,128)(2,1)}, u32[]{:S(2)}) copy-start(bf16[64,5120]{1,0:T(8,128)(2,1)} %copy-done.3) | copy-start | bytes 1966084
  113.9 13.0 %copy-start.6 = (bf16[640,64]{0,1:T(8,128)(2,1)S(1)}, bf16[640,64]{0,1:T(8,128)(2,1)}, u32[]{:S(2)}) copy-start(bf16[640,64]{0,1:T(8,128)(2,1)} %param.16) | copy-start | bytes 245764
  113.9 13.0 %copy-start.7 = (f32[64,128]{1,0:T(8,128)S(1)}, f32[64,128]{1,0:T(8,128)}, u32[]{:S(2)}) copy-start(f32[64,128]{1,0:T(8,128)} %pad_maximum_fusion.1.gram_ref) | copy-start | bytes 98308
  113.9 13.0 %copy-start.8 = (f32[2,1000]{1,0:T(2,128)S(1)}, f32[2,1000]{1,0:T(2,128)}, u32[]{:S(2)}) copy-start(f32[2,1000]{1,0:T(2,128)} %mix_ref.1) | copy-start | bytes 24004
  113.9 13.0 %copy-start.9 = (f32[1000]{0:T(1024)S(1)}, f32[1000]{0:T(1024)}, u32[]{:S(2)}) copy-start(f32[1000]{0:T(1024)} %param.25) | copy-start | bytes 12004
  113.9 13.0 %copy-start.10 = (s32[16]{0:T(128)S(1)}, s32[16]{0:T(128)}, u32[]{:S(2)}) copy-start(s32[16]{0:T(128)} %tsteps_ref.1) | copy-start | bytes 196
  126.9 10.2 %copy-start.17 = (f32[256]{0:T(256)S(1)}, f32[256]{0:T(256)}, u32[]{:S(2)}) copy-start(f32[256]{0:T(256)} %copy-done.16) | copy-start | bytes 3076
  132.6 5.3 %collective-permute-start = (bf16[256,1280]{1,0:T(8,128)(2,1)}, bf16[256,1280]{1,0:T(8,128)(2,1)}, u32[]{:S(2)}, u32[]{:S(2)}) collective-permute-start(bf16[256,1280]{1,0:T(8,128)(2,1)} %get-tuple-element.29), channel_id=1, source_target_pairs={{0,1},{1,0},{2,3},{3,2},{4,5},{5,4},{6,7},{7,6},{8,9},{9,8},{10,11... | collective-permute-start | bytes 1966088 | tf_op jit(solution)/shard_map/backward/ppermute | solution.py:440
  134.7 7.4 %collective-permute-start.1 = (bf16[256,1280]{1,0:T(8,128)(2,1)S(1)}, bf16[256,1280]{1,0:T(8,128)(2,1)S(1)}, u32[]{:S(2)}, u32[]{:S(2)}) collective-permute-start(bf16[256,1280]{1,0:T(8,128)(2,1)S(1)} %get-tuple-element.31), channel_id=1, source_target_pairs={{0,1},{1,0},{2,3},{3,2},{4,5},{5,4},{6,7},{7,6},{8,9},{9,8},{10,11... | collective-permute-start | bytes 1966088 | tf_op jit(solution)/shard_map/backward/ppermute | solution.py:441
  139.2 18.1 %collective-permute-start.2 = (bf16[256,1280]{1,0:T(8,128)(2,1)S(1)}, bf16[256,1280]{1,0:T(8,128)(2,1)S(1)}, u32[]{:S(2)}, u32[]{:S(2)}) collective-permute-start(bf16[256,1280]{1,0:T(8,128)(2,1)S(1)} %fusion.5), channel_id=1, source_target_pairs={{0,2},{2,0},{1,3},{3,1},{4,6},{6,4},{5,7},{7,5},{8,10},{10,8},{9,1... | collective-permute-start | bytes 1966088 | tf_op jit(solution)/shard_map/backward/ppermute | solution.py:444
Sparse Core Ops, SparseCore 0:
  17.0 96.8 all-gather.5
